TPU v7x, 32 devices: a whole 2x2x4 slice. The times are simulated.
32 devices in a mesh: seq: 8 (over z, x), ch: 4 (over y, core).
Axes of the slice: x: 2, y: 2, z: 4, core: 2. Of those that a mesh axis runs over, the one named last changes fastest.
Arguments:
- stream: bfloat16 [1024, 2048], P(('seq', 'ch')), may hold values from -6 to 6
- cotangent: bfloat16 [1024, 2048], P(('seq', 'ch')), may hold values from -6 to 6
- mix_gain: float32 [2048], replicated, may hold values from 0.1 to 1.9
- gelu_weight: bfloat16 [2048, 3072], P(None, 'ch'), may hold values from -0.125 to 0.125
- recur_weight: bfloat16 [2048, 3072], P(None, 'ch'), may hold values from -0.125 to 0.125
- conv_taps: float32 [4, 12, 256], P(None, 'ch'), may hold values from -3 to 3
- conv_bias: float32 [12, 256], P('ch'), may hold values from -3 to 3
- rate_weight: bfloat16 [12, 256, 256], P('ch'), may hold values from -0.375 to 0.375
- rate_bias: float32 [12, 256], P('ch'), may hold values from -4 to 4
- inlet_weight: bfloat16 [12, 256, 256], P('ch'), may hold values from -0.375 to 0.375
- inlet_bias: float32 [12, 256], P('ch'), may hold values from -4 to 4
- decay_param: float32 [12, 256], P('ch'), may hold values from -21 to -1.2
- init_states: float32 [5, 3072], P(None, 'ch'), may hold values from -5 to 5
- out_weight: bfloat16 [3072, 2048], P('ch'), may hold values from -0.375 to 0.375
- ffn_gain: float32 [2048], replicated, may hold values from 0.1 to 1.9
- gate_weight: bfloat16 [2048, 6144], P('seq', 'ch'), may hold values from -0.125 to 0.125
- up_weight: bfloat16 [2048, 6144], P('seq', 'ch'), may hold values from -0.125 to 0.125
- down_weight: bfloat16 [6144, 2048], P('ch', 'seq'), may hold values from -0.078125 to 0.078125
- doc_lengths: int32 [5], replicated, may hold values from 16 to 896, as said below
- block_counts: int32 [4], P('ch'), may hold values from 2 to 3, as said below
Outputs:
- final_states: float32 [5, 3072], replicated
- mixed_out: bfloat16 [1024, 2048], P(('seq', 'ch'))
- stream_grad: float32 [1024, 2048], P(('seq', 'ch'))
- mix_gain_grad: float32 [2048], replicated
- gelu_weight_grad: float32 [2048, 3072], P('seq', 'ch')
- recur_weight_grad: float32 [2048, 3072], P('seq', 'ch')
- conv_taps_grad: float32 [4, 12, 256], P(None, 'ch', 'seq')
- conv_bias_grad: float32 [12, 256], P('ch', 'seq')
- rate_weight_grad: float32 [12, 256, 256], P('ch', 'seq')
- rate_bias_grad: float32 [12, 256], P('ch', 'seq')
- inlet_weight_grad: float32 [12, 256, 256], P('ch', 'seq')
- inlet_bias_grad: float32 [12, 256], P('ch', 'seq')
- decay_grad: float32 [12, 256], P('ch', 'seq')
- out_weight_grad: float32 [3072, 2048], P('ch', 'seq')
- ffn_gain_grad: float32 [2048], replicated
- gate_weight_grad: float32 [2048, 6144], P('seq', 'ch')
- up_weight_grad: float32 [2048, 6144], P('seq', 'ch')
- down_weight_grad: float32 [6144, 2048], P('ch', 'seq')
Inputs may be any that keep to these rules, and one draw needn't show every extreme that they name: `doc_lengths`: 2 short documents, then one long document, then 2 more short ones; the i-th short one after the long one and the i-th before it together hold 64 tokens, so the long one holds 896; the lengths sum to 1024. Index c of ch owns gate-block slots c * 3 to c * 3 + 2, of which the first block_counts[c] are live; the entries sum to 10.
All inputs are finite; a program needn't handle non-finite values.
Results may differ from a plain program's by a relative error of at most 0.009.
Values may be sent and summed in bfloat16 or wider, within the bound.
A program may use at most 256 MiB of HBM per device.

v0:
```python
import jax
import jax.numpy as jnp
from jax import lax
from jax.sharding import PartitionSpec as P

EPS = 1e-06
HIGH = lax.Precision.HIGHEST


def passed_along(shard, axis, by):
    length = lax.axis_size(axis)
    pairs = [(i, i + by) for i in range(length) if 0 <= i + by < length]
    return lax.ppermute(shard, axis, pairs)


def entering_2(shard, axis, combine, identity, reverse):
    length, here = (lax.axis_size(axis), lax.axis_index(axis))
    everything = jax.tree.map(lambda part: lax.all_gather(part, axis), shard)
    start = jax.tree.map(
        lambda part, zero: jnp.broadcast_to(jnp.asarray(zero, part.dtype), part.shape),
        shard,
        identity,
    )

    def turn(k, before):
        at = length - 1 - k if reverse else k
        reached = at > here if reverse else at < here
        new = combine(before, jax.tree.map(lambda part: part[at], everything))
        return jax.tree.map(lambda a, b: jnp.where(reached, a, b), new, before)

    return lax.fori_loop(0, length, turn, start)


def normalize(values, gain):
    return values * lax.rsqrt(jnp.mean(values * values, axis=-1, keepdims=True) + EPS) * gain


def smooth(values):
    return jax.nn.gelu(values, approximate=True)


def affine(earlier, later):
    return (earlier[0] * later[0], later[0] * earlier[1] + later[1])


def doc_view(lengths, first, count):
    ends = jnp.cumsum(lengths)
    starts = ends - lengths
    position = first + jnp.arange(count, dtype=jnp.int32)
    owner = (position[:, None] >= starts[None, :]) & (position[:, None] < ends[None, :])
    start_of = jnp.sum(jnp.where(owner, starts[None, :], 0), axis=1)
    offset = position - start_of
    opening = (owner & (offset[:, None] == 0)).astype(jnp.float32)
    closing = (owner & (position[:, None] == ends[None, :] - 1)).astype(jnp.float32)
    return (offset, opening, closing)


def coefficients(rate_pre, inlet_pre, conv_value, decay, init_rows, keep):
    rate = jax.nn.sigmoid(rate_pre)
    inlet = jax.nn.sigmoid(inlet_pre)
    log_decay = -8.0 * rate * jax.nn.softplus(decay)
    factor = jnp.exp(log_decay)
    scale = jnp.sqrt(-jnp.expm1(2.0 * log_decay))
    carry_factor = keep * factor
    source = scale * inlet * conv_value + (1.0 - keep) * factor * init_rows
    return (carry_factor, source)


def spread(values):
    return lax.all_gather(values, "ch", axis=0, tiled=True)


def collect(terms):
    return lax.psum_scatter(terms, "ch", scatter_dimension=0, tiled=True)


def contract_last(left, right):
    return lax.dot_general(
        left, right, (((1,), (1,)), ((), ())), preferred_element_type=jnp.float32
    )


def contract_first(left, right):
    return lax.dot_general(
        left, right, (((0,), (0,)), ((), ())), preferred_element_type=jnp.float32
    )


def body(
    stream,
    cotangent,
    mix_gain,
    gelu_weight,
    recur_weight,
    conv_taps,
    conv_bias,
    rate_weight,
    rate_bias,
    inlet_weight,
    inlet_bias,
    decay_param,
    init_states,
    out_weight,
    ffn_gain,
    gate_weight,
    up_weight,
    down_weight,
    doc_lengths,
    block_counts,
):
    slot_count = rate_weight.shape[0]
    block_width = rate_weight.shape[1]
    local_width = slot_count * block_width
    taps = conv_taps.shape[0]
    token_count = stream.shape[0] * lax.axis_size("ch")
    hidden_width = gate_weight.shape[1]
    base = lax.axis_index("seq") * token_count
    offset_all, opening, closing = doc_view(doc_lengths, base, token_count + taps - 1)
    offset = offset_all[:token_count]
    opening = opening[:token_count]
    closing = closing[:token_count]
    keep = (offset > 0).astype(jnp.float32)[:, None]
    slot_live = (jnp.arange(slot_count, dtype=jnp.int32) < block_counts[0]).astype(jnp.float32)
    live = jnp.repeat(slot_live, block_width)[None, :]
    taps_flat = conv_taps.reshape(taps, local_width)
    decay_flat = decay_param.reshape(1, local_width)
    stream_float = stream.astype(jnp.float32)
    mix_low = normalize(stream_float, mix_gain).astype(jnp.bfloat16)
    mix_full = spread(mix_low)
    gelu_pre = jnp.dot(mix_full, gelu_weight, preferred_element_type=jnp.float32)
    recur_low = jnp.dot(mix_full, recur_weight, preferred_element_type=jnp.float32).astype(
        jnp.bfloat16
    )
    rim = passed_along(recur_low[token_count - taps + 1 :], "seq", 1)
    extended = jnp.concatenate([rim, recur_low], axis=0).astype(jnp.float32)
    conv_pre = conv_bias.reshape(1, local_width)
    for tap_index in range(taps):
        valid = (offset >= tap_index).astype(jnp.float32)[:, None]
        lead = taps - 1 - tap_index
        conv_pre = (
            conv_pre + taps_flat[tap_index][None, :] * extended[lead : lead + token_count] * valid
        )
    conv_low = conv_pre.astype(jnp.bfloat16)
    conv_value = conv_low.astype(jnp.float32)
    grouped = conv_low.reshape(token_count, slot_count, block_width)
    rate_pre = (
        jnp.einsum("rsi,sio->rso", grouped, rate_weight, preferred_element_type=jnp.float32)
        + rate_bias[None]
    ).reshape(token_count, local_width)
    inlet_pre = (
        jnp.einsum("rsi,sio->rso", grouped, inlet_weight, preferred_element_type=jnp.float32)
        + inlet_bias[None]
    ).reshape(token_count, local_width)
    init_rows = jnp.dot(opening, init_states, precision=HIGH)
    carry_factor, source = coefficients(
        rate_pre, inlet_pre, conv_value, decay_flat, init_rows, keep
    )
    cumulative, local_state = lax.associative_scan(affine, (carry_factor, source), axis=0)
    summary = (cumulative[-1], local_state[-1])
    entering = entering_2(
        summary, "seq", affine, (jnp.ones_like(summary[0]), jnp.zeros_like(summary[1])), False
    )
    state_in = entering[1]
    state = local_state + cumulative * state_in[None, :]
    gelu_value = smooth(gelu_pre)
    product_low = (gelu_value * state * live).astype(jnp.bfloat16)
    branch = collect(jnp.dot(product_low, out_weight, preferred_element_type=jnp.float32))
    middle = stream_float + branch
    ffn_low = normalize(middle, ffn_gain).astype(jnp.bfloat16)
    ffn_full = spread(ffn_low)
    stacked = jnp.concatenate([gate_weight, up_weight], axis=1)
    columns = ffn_full
    gate_up = jnp.dot(
        columns,
        lax.all_gather(stacked, "seq", axis=0, tiled=True),
        preferred_element_type=jnp.float32,
    )
    gate = gate_up[:, :hidden_width]
    upward = gate_up[:, hidden_width:]
    hidden = (smooth(gate) * upward).astype(jnp.bfloat16)
    ffn_terms = jnp.dot(
        hidden,
        lax.all_gather(down_weight, "seq", axis=1, tiled=True),
        preferred_element_type=jnp.float32,
    )
    mixed_out = (middle + collect(ffn_terms)).astype(jnp.bfloat16)
    out_grad_full = spread(cotangent)
    columns = out_grad_full
    hidden_grad = contract_last(columns, lax.all_gather(down_weight, "seq", axis=1, tiled=True))
    down_weight_grad = contract_first(hidden, out_grad_full)
    unused, pair_pull = jax.vjp(lambda left, right: smooth(left) * right, gate, upward)
    gate_grad, up_grad = pair_pull(hidden_grad)
    pair_low = jnp.concatenate([gate_grad, up_grad], axis=1).astype(jnp.bfloat16)
    pair_weight_grad = contract_first(ffn_full, pair_low)
    norm_ffn_part = contract_last(pair_low, lax.all_gather(stacked, "seq", axis=0, tiled=True))
    norm_ffn_grad = collect(norm_ffn_part)
    unused, ffn_norm_pull = jax.vjp(normalize, middle, ffn_gain)
    middle_norm_grad, ffn_gain_part = ffn_norm_pull(norm_ffn_grad)
    middle_grad = cotangent.astype(jnp.float32) + middle_norm_grad
    branch_full = spread(middle_grad.astype(jnp.bfloat16))
    out_weight_grad = contract_first(product_low, branch_full)
    product_grad = contract_last(branch_full, out_weight)
    state_grad = product_grad * gelu_value * live
    unused, gelu_pull = jax.vjp(smooth, gelu_pre)
    gelu_low = gelu_pull(product_grad * state * live)[0].astype(jnp.bfloat16)
    following = jnp.concatenate([carry_factor[1:], jnp.ones_like(carry_factor[:1])], axis=0)
    cum_back, adjoint_local = lax.associative_scan(
        affine, (jnp.flip(following, 0), jnp.flip(state_grad, 0)), axis=0
    )
    cum_back = jnp.flip(cum_back, 0)
    adjoint_local = jnp.flip(adjoint_local, 0)
    summary_back = (carry_factor[0] * cum_back[0], carry_factor[0] * adjoint_local[0])
    arriving = entering_2(
        summary_back,
        "seq",
        affine,
        (jnp.ones_like(summary_back[0]), jnp.zeros_like(summary_back[1])),
        True,
    )
    adjoint_in = arriving[1]
    adjoint = adjoint_local + cum_back * adjoint_in[None, :]
    previous_state = jnp.concatenate([state_in[None, :], state[:-1]], axis=0)

    def local_coefficients(rate_value, inlet_value, conv_part, decay_value):
        return coefficients(rate_value, inlet_value, conv_part, decay_value, init_rows, keep)

    unused, coefficient_pull = jax.vjp(
        local_coefficients, rate_pre, inlet_pre, conv_value, decay_flat
    )
    rate_grad, inlet_grad, conv_direct, decay_part = coefficient_pull(
        (adjoint * previous_state, adjoint)
    )
    rate_low = rate_grad.astype(jnp.bfloat16).reshape(token_count, slot_count, block_width)
    inlet_low = inlet_grad.astype(jnp.bfloat16).reshape(token_count, slot_count, block_width)
    rate_weight_grad = jnp.einsum(
        "rsi,rso->sio", grouped, rate_low, preferred_element_type=jnp.float32
    )
    inlet_weight_grad = jnp.einsum(
        "rsi,rso->sio", grouped, inlet_low, preferred_element_type=jnp.float32
    )
    rate_bias_grad = jnp.sum(rate_low.astype(jnp.float32), axis=0)
    inlet_bias_grad = jnp.sum(inlet_low.astype(jnp.float32), axis=0)
    conv_back = jnp.einsum(
        "rso,sio->rsi", rate_low, rate_weight, preferred_element_type=jnp.float32
    )
    conv_back = conv_back + jnp.einsum(
        "rso,sio->rsi", inlet_low, inlet_weight, preferred_element_type=jnp.float32
    )
    conv_low_grad = (conv_direct + conv_back.reshape(token_count, local_width)).astype(jnp.bfloat16)
    rim_back = passed_along(conv_low_grad[: taps - 1], "seq", -1)
    ahead = jnp.concatenate([conv_low_grad, rim_back], axis=0).astype(jnp.float32)
    own_grad = ahead[:token_count]
    recur_grad = jnp.zeros((token_count, local_width), jnp.float32)
    tap_grads = []
    for tap_index in range(taps):
        lead = taps - 1 - tap_index
        valid_here = (offset >= tap_index).astype(jnp.float32)[:, None]
        tap_grads.append(
            jnp.sum(own_grad * extended[lead : lead + token_count] * valid_here, axis=0)
        )
        valid_ahead = (offset_all[tap_index : tap_index + token_count] >= tap_index).astype(
            jnp.float32
        )[:, None]
        recur_grad = (
            recur_grad
            + taps_flat[tap_index][None, :]
            * ahead[tap_index : tap_index + token_count]
            * valid_ahead
        )
    conv_taps_grad = jnp.stack(tap_grads, axis=0).reshape(taps, slot_count, block_width)
    conv_bias_grad = jnp.sum(own_grad, axis=0).reshape(slot_count, block_width)
    recur_low_grad = recur_grad.astype(jnp.bfloat16)
    gelu_weight_grad = contract_first(mix_full, gelu_low)
    recur_weight_grad = contract_first(mix_full, recur_low_grad)
    norm_mix_part = contract_last(gelu_low, gelu_weight) + contract_last(
        recur_low_grad, recur_weight
    )
    norm_mix_grad = collect(norm_mix_part)
    unused, mix_norm_pull = jax.vjp(normalize, stream_float, mix_gain)
    stream_norm_grad, mix_gain_part = mix_norm_pull(norm_mix_grad)
    stream_grad = middle_grad + stream_norm_grad
    finals_local = lax.dot_general(closing, state * live, (((0,), (0,)), ((), ())), precision=HIGH)
    finals_wide = jnp.zeros((finals_local.shape[0], local_width * lax.axis_size("ch")), jnp.float32)
    finals_wide = lax.dynamic_update_slice(
        finals_wide, finals_local, (jnp.int32(0), lax.axis_index("ch") * local_width)
    )
    final_states, mix_gain_grad, ffn_gain_grad = lax.psum(
        (finals_wide, mix_gain_part, ffn_gain_part), ("seq", "ch")
    )
    summed = (
        lax.psum_scatter(gelu_weight_grad, "seq", scatter_dimension=0, tiled=True),
        lax.psum_scatter(recur_weight_grad, "seq", scatter_dimension=0, tiled=True),
        lax.psum_scatter(conv_taps_grad, "seq", scatter_dimension=2, tiled=True),
        lax.psum_scatter(conv_bias_grad, "seq", scatter_dimension=1, tiled=True),
        lax.psum_scatter(rate_weight_grad, "seq", scatter_dimension=1, tiled=True),
        lax.psum_scatter(rate_bias_grad, "seq", scatter_dimension=1, tiled=True),
        lax.psum_scatter(inlet_weight_grad, "seq", scatter_dimension=1, tiled=True),
        lax.psum_scatter(inlet_bias_grad, "seq", scatter_dimension=1, tiled=True),
        lax.psum_scatter(
            decay_part.reshape(slot_count, block_width), "seq", scatter_dimension=1, tiled=True
        ),
        lax.psum_scatter(out_weight_grad, "seq", scatter_dimension=1, tiled=True),
        lax.psum_scatter(
            pair_weight_grad[:, :hidden_width], "seq", scatter_dimension=0, tiled=True
        ),
        lax.psum_scatter(
            pair_weight_grad[:, hidden_width:], "seq", scatter_dimension=0, tiled=True
        ),
        lax.psum_scatter(down_weight_grad, "seq", scatter_dimension=1, tiled=True),
    )
    return (
        final_states,
        mixed_out,
        stream_grad,
        mix_gain_grad,
        summed[0],
        summed[1],
        summed[2],
        summed[3],
        summed[4],
        summed[5],
        summed[6],
        summed[7],
        summed[8],
        summed[9],
        ffn_gain_grad,
        summed[10],
        summed[11],
        summed[12],
    )


def solution(mesh):
    in_specs = (
        P(("seq", "ch"), None),
        P(("seq", "ch"), None),
        P(),
        P(None, "ch"),
        P(None, "ch"),
        P(None, "ch", None),
        P("ch", None),
        P("ch", None, None),
        P("ch", None),
        P("ch", None, None),
        P("ch", None),
        P("ch", None),
        P(None, "ch"),
        P("ch", None),
        P(),
        P("seq", "ch"),
        P("seq", "ch"),
        P("ch", "seq"),
        P(),
        P("ch"),
    )
    out_specs = (
        P(),
        P(("seq", "ch"), None),
        P(("seq", "ch"), None),
        P(),
        P("seq", "ch"),
        P("seq", "ch"),
        P(None, "ch", "seq"),
        P("ch", "seq"),
        P("ch", "seq", None),
        P("ch", "seq"),
        P("ch", "seq", None),
        P("ch", "seq"),
        P("ch", "seq"),
        P("ch", "seq"),
        P(),
        P("seq", "ch"),
        P("seq", "ch"),
        P("ch", "seq"),
    )
    return jax.shard_map(body, mesh=mesh, in_specs=in_specs, out_specs=out_specs, check_vma=False)
```

profile of v0, /device:TPU:0, one launch (start us, length us, event | category | flops | bytes accessed | tf_op | source)
XLA Modules:
  0.0 2530.0 jit_solution(1340438756813617284)
XLA Ops:
  10.4 8.6 all_gather.34
  19.8 2.5 convolution_convert_fusion
  22.3 3.4 collective-permute-start
  45.4 2.7 fusion.20
  186.2 2.5 pad.201
  192.5 2.3 pad.184
  199.3 2.5 pad.200
  202.6 30.7 %all-gather = f32[8,1,768]{2,1,0:T(1,128)S(1)} all-gather(f32[1,1,768]{2,1,0:T(1,128)S(1)} %add_bitcast_fusion.1), channel_id=1, replica_groups=mesh['seq'=8,'ch'=4] {'seq'}, dimensions={0}, use_global_device_ids=true | all-gather | bytes 27648 | tf_op jit(solution)/shard_map/all_gather | solution.py:18
  233.8 2.5 pad.187
  237.9 2.5 pad.186
  241.2 30.3 %all-gather.1 = f32[8,1,768]{2,1,0:T(1,128)S(1)} all-gather(f32[1,1,768]{2,1,0:T(1,128)S(1)} %add_bitcast_fusion), channel_id=1, replica_groups=mesh['seq'=8,'ch'=4] {'seq'}, dimensions={0}, use_global_device_ids=true | all-gather | bytes 27648 | tf_op jit(solution)/shard_map/all_gather | solution.py:18
  272.1 6.6 while.30
  278.8 3.2 multiply_convert_fusion.2
  284.3 2.7 pad_maximum_fusion
  287.7 7.8 all_gather.40
  295.5 12.1 reduce-scatter.28.cloned.1.call-done
  309.5 7.4 all_gather.37
  316.9 145.2 %all-gather.7.cloned.1.call-done = bf16[2048,3072]{1,0:T(8,128)(2,1)} async-done(((bf16[256,3072]{1,0:T(8,128)(2,1)}), bf16[2048,3072]{1,0:T(8,128)(2,1)}) %all-gather.7.cloned.1.call-update) | async-done | bytes 12582928 | tf_op jit(solution)/shard_map/all_gather | solution.py:175
  462.1 7.7 fusion.108
  469.8 92.1 %all-gather.9.cloned.1.call-done = bf16[1536,2048]{1,0:T(8,128)(2,1)} async-done(((bf16[1536,256]{1,0:T(8,128)(2,1)}), bf16[1536,2048]{1,0:T(8,128)(2,1)}) %all-gather.9.cloned.1.call-update) | async-done | bytes 6291472 | tf_op jit(solution)/shard_map/all_gather | solution.py:183
  561.9 6.6 fusion.17
  569.5 9.9 fusion.19
  586.9 3.5 slice.609
  590.5 3.5 slice.618
  594.0 3.5 slice.611
  597.5 5.1 reduce-scatter.32.cloned.1.call-done
  606.3 6.8 all_gather.41
  613.8 4.2 multiply_multiply_fusion.5
  621.4 3.5 slice.615
  624.9 3.5 slice.613
  753.7 3.6 slice.663
  769.7 2.5 pad.214
  772.1 2.5 pad.215
  776.3 2.5 pad.228
  778.8 2.6 pad.229
  786.0 3.9 rev.9
  789.8 3.9 rev.10
  793.7 30.6 %all-gather.2 = f32[8,1,768]{2,1,0:T(1,128)S(1)} all-gather(f32[1,1,768]{2,1,0:T(1,128)S(1)} %get-tuple-element.401), channel_id=1, replica_groups=mesh['seq'=8,'ch'=4] {'seq'}, dimensions={0}, use_global_device_ids=true | all-gather | bytes 27648 | tf_op jit(solution)/shard_map/all_gather | solution.py:18
  824.9 30.3 %all-gather.3 = f32[8,1,768]{2,1,0:T(1,128)S(1)} all-gather(f32[1,1,768]{2,1,0:T(1,128)S(1)} %get-tuple-element.400), channel_id=1, replica_groups=mesh['seq'=8,'ch'=4] {'seq'}, dimensions={0}, use_global_device_ids=true | all-gather | bytes 27648 | tf_op jit(solution)/shard_map/all_gather | solution.py:18
  855.9 6.6 while.31
  862.6 3.6 multiply_reduce_fusion
  895.1 5.0 fusion.109
  903.1 10.1 reduce-scatter.34.cloned.1.call-done
  915.1 3.6 fusion.112
  919.8 3.6 fusion.116
  923.5 3.7 fusion.113
  928.5 10.4 fusion.18
  938.9 18.6 fusion.97
  958.7 6.4 fusion.117
  965.1 12.5 reduce-scatter.56.cloned.1.call-done
  979.0 62.1 %reduce-scatter.58.cloned.1.call-done = f32[32,3]{1,0:T(8,128)} async-done(((f32[256,3]{1,0:T(8,128)}), f32[32,3]{1,0:T(8,128)}) %reduce-scatter.58.cloned.1.call-update) | async-done | bytes 400
  1042.5 62.1 %reduce-scatter.60.cloned.1.call-done = f32[32,3]{1,0:T(8,128)} async-done(((f32[256,3]{1,0:T(8,128)}), f32[32,3]{1,0:T(8,128)}) %reduce-scatter.60.cloned.1.call-update) | async-done | bytes 400
  1105.9 62.2 %reduce-scatter.54.cloned.1.call-done = f32[32,3]{1,0:T(8,128)} async-done(((f32[256,3]{1,0:T(8,128)}), f32[32,3]{1,0:T(8,128)}) %reduce-scatter.54.cloned.1.call-update) | async-done | bytes 400
  1169.5 62.8 %reduce-scatter.52.cloned.1.call-done = f32[32,12]{1,0:T(8,128)} async-done(((f32[256,12]{1,0:T(8,128)}), f32[32,12]{1,0:T(8,128)}) %reduce-scatter.52.cloned.1.call-update) | async-done | bytes 1552
  1236.6 22.4 reduce-scatter.30.cloned.1.call-done
  1261.0 64.9 %reduce-scatter.40.cloned.1.call-done = f32[3,32,256]{2,1,0:T(8,128)} async-done(((f32[3,256,256]{2,1,0:T(8,128)}), f32[3,32,256]{2,1,0:T(8,128)}) %reduce-scatter.40.cloned.1.call-update) | async-done | bytes 98320 | tf_op jit(solution)/shard_map/reduce_scatter | solution.py:295
  1325.9 66.5 %reduce-scatter.42.cloned.1.call-done = f32[3,32,256]{2,1,0:T(8,128)} async-done(((f32[3,256,256]{2,1,0:T(8,128)}), f32[3,32,256]{2,1,0:T(8,128)}) %reduce-scatter.42.cloned.1.call-update) | async-done | bytes 98320 | tf_op jit(solution)/shard_map/reduce_scatter | solution.py:297
  1392.4 127.7 %all-reduce.61.cloned.1.call-done = (f32[5,3072]{1,0:T(8,128)}, f32[2048]{0:T(1024)}, f32[2048]{0:T(1024)}) async-done(((f32[5,3072]{1,0:T(8,128)}, f32[2048]{0:T(1024)}, f32[2048]{0:T(1024)}), (f32[5,3072]{1,0:T(8,128)}, f32[2048]{0:T(1024)}, f32[2048]{0:T(1024)})) %all-reduce.61.cloned.1.call-update) | async-done | bytes 77840 | tf_op jit(solution)/shard_map/psum | solution.py:287
  1520.1 123.1 %reduce-scatter.36.cloned.1.call-done = f32[256,768]{1,0:T(8,128)} async-done(((f32[2048,768]{1,0:T(8,128)}), f32[256,768]{1,0:T(8,128)}) %reduce-scatter.36.cloned.1.call-update) | async-done | bytes 786448 | tf_op jit(solution)/shard_map/reduce_scatter | solution.py:291
  1643.2 121.6 %reduce-scatter.44.cloned.1.call-done = f32[768,256]{1,0:T(8,128)} async-done(((f32[768,2048]{1,0:T(8,128)}), f32[768,256]{1,0:T(8,128)}) %reduce-scatter.44.cloned.1.call-update) | async-done | bytes 786448 | tf_op jit(solution)/shard_map/reduce_scatter | solution.py:302
  1764.8 121.2 %reduce-scatter.38.cloned.1.call-done = f32[256,768]{1,0:T(8,128)} async-done(((f32[2048,768]{1,0:T(8,128)}), f32[256,768]{1,0:T(8,128)}) %reduce-scatter.38.cloned.1.call-update) | async-done | bytes 786448 | tf_op jit(solution)/shard_map/reduce_scatter | solution.py:292
  1886.0 210.5 %reduce-scatter.46.cloned.1.call-done = f32[256,1536]{1,0:T(8,128)} async-done(((f32[2048,1536]{1,0:T(8,128)}), f32[256,1536]{1,0:T(8,128)}) %reduce-scatter.46.cloned.1.call-update) | async-done | bytes 1572880 | tf_op jit(solution)/shard_map/reduce_scatter | solution.py:303
  2096.5 210.4 %reduce-scatter.48.cloned.1.call-done = f32[256,1536]{1,0:T(8,128)} async-done(((f32[2048,1536]{1,0:T(8,128)}), f32[256,1536]{1,0:T(8,128)}) %reduce-scatter.48.cloned.1.call-update) | async-done | bytes 1572880 | tf_op jit(solution)/shard_map/reduce_scatter | solution.py:306
  2307.0 211.0 %reduce-scatter.50.cloned.1.call-done = f32[1536,256]{1,0:T(8,128)} async-done(((f32[1536,2048]{1,0:T(8,128)}), f32[1536,256]{1,0:T(8,128)}) %reduce-scatter.50.cloned.1.call-update) | async-done | bytes 1572880 | tf_op jit(solution)/shard_map/reduce_scatter | solution.py:309
  (546 shorter events, 403.9 us)
Async XLA Ops:
  8.0 270.7 %copy-start = (bf16[2048,768]{1,0:T(8,128)(2,1)S(1)}, bf16[2048,768]{1,0:T(8,128)(2,1)}, u32[]{:S(2)}) copy-start(bf16[2048,768]{1,0:T(8,128)(2,1)} %param.27) | copy-start | bytes 9437188
  8.0 17.7 copy-start.84
  8.0 21.6 copy-start.68
  8.1 21.6 copy-start.54
  8.1 23.6 copy-start.76
  8.1 299.5 %reduce-scatter.28.cloned.1.call-start = ((), (), s32[]{:S(2)}) async-start(), calls=%async_computation.17 | async-start | bytes 1310720 | tf_op jit(solution)/shard_map/reduce_scatter | solution.py:74
  9.3 16.4 copy-start.83
  9.3 17.1 copy-start.74
  22.3 9.9 collective-permute-start
  31.0 8.4 copy-start.35
  31.0 8.4 copy-start.37
  31.0 8.4 copy-start.39
  132.9 46.4 %copy-start.70 = (f32[1,768]{1,0:T(1,128)S(1)}, f32[1,768]{1,0:T(1,128)}, u32[]{:S(2)}) copy-start(f32[1,768]{1,0:T(1,128)} %slice.722) | copy-start | bytes 9220
  174.3 24.3 copy-start.66
  180.0 56.3 %copy-start.65 = (f32[1,768]{1,0:T(1,128)S(1)}, f32[1,768]{1,0:T(1,128)}, u32[]{:S(2)}) copy-start(f32[1,768]{1,0:T(1,128)} %slice.698) | copy-start | bytes 9220
  188.7 90.0 %copy-start.47 = (f32[768]{0:T(1024)S(1)}, f32[768]{0:T(1024)}, u32[]{:S(2)}) copy-start(f32[768]{0:T(1024)} %mul.813) | copy-start | bytes 9220
  284.3 25.1 copy-start.33
  284.3 177.8 %all-gather.7.cloned.1.call-start = ((), (), s32[]{:S(2)}) async-start(), calls=%async_computation.18 | async-start | bytes 14155776 | tf_op jit(solution)/shard_map/all_gather | solution.py:175
  287.0 274.9 %all-gather.9.cloned.1.call-start = ((), (), s32[]{:S(2)}) async-start(), calls=%async_computation.19 | async-start | bytes 7077888 | tf_op jit(solution)/shard_map/all_gather | solution.py:183
  287.6 315.0 %reduce-scatter.32.cloned.1.call-start = ((), (), s32[]{:S(2)}) async-start(), calls=%async_computation.21 | async-start | bytes 1310720 | tf_op jit(solution)/shard_map/reduce_scatter | solution.py:74
  579.4 333.8 %reduce-scatter.34.cloned.1.call-start = ((), (), s32[]{:S(2)}) async-start(), calls=%async_computation.22 | async-start | bytes 1310720 | tf_op jit(solution)/shard_map/reduce_scatter | solution.py:74
  580.1 33.8 %copy-start.48 = (f32[768]{0:T(1024)S(1)}, f32[768]{0:T(1024)}, u32[]{:S(2)}) copy-start(f32[768]{0:T(1024)} %mul.813) | copy-start | bytes 9220
  605.0 8.0 copy-start.78
  716.5 34.2 %copy-start.71 = (f32[1,768]{1,0:T(1,128)S(1)}, f32[1,768]{1,0:T(1,128)}, u32[]{:S(2)}) copy-start(f32[1,768]{1,0:T(1,128)} %slice.770) | copy-start | bytes 9220
  716.5 43.1 %copy-start.69 = (f32[1,768]{1,0:T(1,128)S(1)}, f32[1,768]{1,0:T(1,128)}, u32[]{:S(2)}) copy-start(f32[1,768]{1,0:T(1,128)} %slice.748) | copy-start | bytes 9220
  739.5 29.5 %copy-start.67 = (f32[1,768]{1,0:T(1,128)S(1)}, f32[1,768]{1,0:T(1,128)}, u32[]{:S(2)}) copy-start(f32[1,768]{1,0:T(1,128)} %slice.746) | copy-start | bytes 9220
  774.6 88.0 %copy-start.36 = (f32[768]{0:T(1024)S(1)}, f32[768]{0:T(1024)}, u32[]{:S(2)}) copy-start(f32[768]{0:T(1024)} %copy-done.35) | copy-start | bytes 9220
  868.3 11.7 copy-start.44
  880.0 7.1 copy-start.42
  880.0 7.1 copy-start.51
  880.0 7.1 copy-start.80
  880.0 7.1 copy-start.81
  880.0 7.1 copy-start.82
  881.6 5.5 collective-permute-start.1
  887.5 5.0 copy-start.4
  887.5 5.0 copy-start.52
  887.5 5.0 copy-start.60
  889.7 5.4 copy-start.14
  889.7 88.0 %reduce-scatter.56.cloned.1.call-start = ((), (), s32[]{:S(2)}) async-start(), calls=%async_computation.33 | async-start | bytes 147456
  890.6 150.5 %reduce-scatter.58.cloned.1.call-start = ((), (), s32[]{:S(2)}) async-start(), calls=%async_computation.34 | async-start | bytes 147456
  891.5 213.1 %reduce-scatter.60.cloned.1.call-start = ((), (), s32[]{:S(2)}) async-start(), calls=%async_computation.35 | async-start | bytes 147456
  892.4 275.7 %reduce-scatter.54.cloned.1.call-start = ((), (), s32[]{:S(2)}) async-start(), calls=%async_computation.32 | async-start | bytes 147456
  893.7 338.6 %reduce-scatter.52.cloned.1.call-start = ((), (), s32[]{:S(2)}) async-start(), calls=%async_computation.31 | async-start | bytes 147456
  895.0 364.0 %reduce-scatter.30.cloned.1.call-start = ((), (), s32[]{:S(2)}) async-start(), calls=%async_computation.20 | async-start | bytes 1310720 | tf_op jit(solution)/shard_map/reduce_scatter | solution.py:74
  895.1 5.2 copy-start.23
  895.1 5.2 copy-start.25
  900.1 13.1 copy-start.15
  900.2 13.1 copy-start.45
  900.2 13.1 copy-start.75
  900.2 14.9 copy-start.6
  900.2 14.9 copy-start.31
  900.2 425.7 %reduce-scatter.40.cloned.1.call-start = ((), (), s32[]{:S(2)}) async-start(), calls=%async_computation.25 | async-start | bytes 884736 | tf_op jit(solution)/shard_map/reduce_scatter | solution.py:295
  901.5 490.9 %reduce-scatter.42.cloned.1.call-start = ((), (), s32[]{:S(2)}) async-start(), calls=%async_computation.26 | async-start | bytes 884736 | tf_op jit(solution)/shard_map/reduce_scatter | solution.py:297
  902.7 617.4 %all-reduce.61.cloned.1.call-start = ((), (), s32[]{:S(2)}) async-start(), calls=%async_computation.36 | async-start | bytes 229376 | tf_op jit(solution)/shard_map/psum | solution.py:287
  903.1 11.9 copy-start.32
  915.0 728.2 %reduce-scatter.36.cloned.1.call-start = ((), (), s32[]{:S(2)}) async-start(), calls=%async_computation.23 | async-start | bytes 7077888 | tf_op jit(solution)/shard_map/reduce_scatter | solution.py:291
  918.7 846.1 %reduce-scatter.44.cloned.1.call-start = ((), (), s32[]{:S(2)}) async-start(), calls=%async_computation.27 | async-start | bytes 7077888 | tf_op jit(solution)/shard_map/reduce_scatter | solution.py:302
  923.5 962.5 %reduce-scatter.38.cloned.1.call-start = ((), (), s32[]{:S(2)}) async-start(), calls=%async_computation.24 | async-start | bytes 7077888 | tf_op jit(solution)/shard_map/reduce_scatter | solution.py:292
  927.3 1169.3 %reduce-scatter.46.cloned.1.call-start = ((), (), s32[]{:S(2)}) async-start(), calls=%async_computation.28 | async-start | bytes 14155776 | tf_op jit(solution)/shard_map/reduce_scatter | solution.py:303
  957.6 1349.4 %reduce-scatter.48.cloned.1.call-start = ((), (), s32[]{:S(2)}) async-start(), calls=%async_computation.29 | async-start | bytes 14155776 | tf_op jit(solution)/shard_map/reduce_scatter | solution.py:306
  958.2 1559.8 %reduce-scatter.50.cloned.1.call-start = ((), (), s32[]{:S(2)}) async-start(), calls=%async_computation.30 | async-start | bytes 14155776 | tf_op jit(solution)/shard_map/reduce_scatter | solution.py:309
  965.1 293.9 %copy-start.11 = (f32[32,2048]{1,0:T(8,128)S(1)}, f32[32,2048]{1,0:T(8,128)}, u32[]{:S(2)}) copy-start(f32[32,2048]{1,0:T(8,128)} %copy-done.10) | copy-start | bytes 786436
  965.1 293.9 %copy-start.34 = (f32[2048]{0:T(1024)S(1)}, f32[2048]{0:T(1024)}, u32[]{:S(2)}) copy-start(f32[2048]{0:T(1024)} %param.38) | copy-start | bytes 24580
  965.1 1557.0 %copy-start.1 = (bf16[2048,768]{1,0:T(8,128)(2,1)S(1)}, bf16[2048,768]{1,0:T(8,128)(2,1)}, u32[]{:S(2)}) copy-start(bf16[2048,768]{1,0:T(8,128)(2,1)} %param.27) | copy-start | bytes 9437188
  (45 other events, 118.3 us)
Sparse Core Ops, SparseCore 0:
  284.4 23.1 reduce-scatter.27
  579.5 23.0 reduce-scatter.31
  889.8 23.3 reduce-scatter.33
  916.8 60.8 reduce-scatter.55
  981.2 59.8 reduce-scatter.57
  1044.6 59.8 reduce-scatter.59
  1108.2 59.8 reduce-scatter.53
  1172.4 59.8 reduce-scatter.51
  1235.0 23.8 reduce-scatter.29
  1262.7 63.1 reduce-scatter.39
  1330.2 62.1 reduce-scatter.41
  1399.3 120.7 all-reduce.60
  1524.3 118.9 reduce-scatter.35
  1647.3 117.5 reduce-scatter.43
  1768.8 117.1 reduce-scatter.37
  1890.0 206.4 reduce-scatter.45
  2100.5 206.3 reduce-scatter.47
  2311.0 206.8 reduce-scatter.49
Sparse Core Ops, SparseCore 1:
  287.7 174.3 all-gather.6
  464.2 97.7 all-gather.8
where the time goes:
time: 2550 us; the launch traced here: 2530 us
  waiting for transfers between devices  1810 us (71%)
  local copies, waits for them, and re-layouts  329 us (13%)
  blocking collectives  152 us (6%)
  other arithmetic  128 us (5%)
  matrix products  86.8 us (3%)
    unnamed x25, waiting for transfers between devices  263 us
    reduce_scatter x1, waiting for transfers between devices, body(): lax.psum_scatter(down_weight_grad, 'seq', scatter_dimension=1, tiled=True)  211 us
    reduce_scatter x1, waiting for transfers between devices, body(): lax.psum_scatter(pair_weight_grad[:, :hidden_width], 'seq', scatter_dimen...  211 us
    reduce_scatter x1, waiting for transfers between devices, body(): lax.psum_scatter(pair_weight_grad[:, hidden_width:], 'seq', scatter_dimen...  210 us
    all_gather x1, waiting for transfers between devices, body(): lax.all_gather(stacked, 'seq', axis=0, tiled=True)  145 us
    psum x1, waiting for transfers between devices, body(): lax.psum((finals_wide, mix_gain_part, ffn_gain_part), ('seq', 'ch'))  128 us
    reduce_scatter x1, waiting for transfers between devices, body(): lax.psum_scatter(gelu_weight_grad, 'seq', scatter_dimension=0, tiled=True)  123 us
    all_gather x4, blocking collectives, entering_2(): everything = jax.tree.map(lambda part: lax.all_gather(part, axis), shard)  122 us
  transfers between devices with their start and end apart: 22, of which 21 were waited for; matrix products, arithmetic and copies ran while one was open for 4% of the time, Pallas kernels for 0%

commit v1 on v0

--- a/solution.py
+++ b/solution.py
@@ -1,10 +1,18 @@
+import functools
+
 import jax
 import jax.numpy as jnp
 from jax import lax
+from jax.experimental import pallas as pl
+from jax.experimental.pallas import tpu as pltpu
 from jax.sharding import PartitionSpec as P
 
 EPS = 1e-06
 HIGH = lax.Precision.HIGHEST
+MESH = pl.DeviceIdType.MESH
+K1 = 0.7978845608028654
+K2 = 0.044715
+VMEM_BYTES = 56 * 2**20
 
 
 def passed_along(shard, axis, by):
@@ -330,6 +338,472 @@
     )
 
 
+def ffn_kernel(
+    sizes, low_ref, cot_ref, weight_ref, out_ref, grad_ref, dw_ref,
+    wt, full, cfull, hid, gat, upg, part, sib, psum_buf, pl_in, zsum, z_in, dwl,
+    ws, wr, zs, zr, ps, pr, cs, cr, rs1, rr1, rs2, rr2, rs3, rr3, ds_, dr_,
+):
+    n_seq, n_ch, rows, width, sl = sizes
+    n_z = n_seq // 2
+    s, c = lax.axis_index("seq"), lax.axis_index("ch")
+    z, x = s // 2, s % 2
+    y, core = c // 2, c % 2
+
+    def dev(zz, xx, yy, cc):
+        return (zz * 2 + xx, yy * 2 + cc)
+
+    def block(zz, xx, yy, cc):
+        return pl.multiple_of(((zz * 2 + xx) * n_ch + yy * 2 + cc) * rows, rows)
+
+    plane = [(1 - x, y), (x, 1 - y), (1 - x, 1 - y)]
+    z_to = [(z + k) % n_z for k in range(n_z)]
+    z_from = [(z + n_z - k) % n_z for k in range(n_z)]
+    s_to = [(s + k) % n_seq for k in range(n_seq)]
+    s_from = [(s + n_seq - k) % n_seq for k in range(n_seq)]
+
+    barrier = pltpu.get_barrier_semaphore()
+    peers = [(s_to[k], c) for k in range(1, n_seq)]
+    peers += [dev(z, x, y, 1 - core)] + [dev(z, x, 1 - y, core), dev(z, 1 - x, 1 - y, core)]
+    for peer in peers:
+        pl.semaphore_signal(barrier, inc=1, device_id=peer, device_id_type=MESH)
+    pl.semaphore_wait(barrier, len(peers))
+
+    def send(src, dst, ssem, rsem, to):
+        copy = pltpu.make_async_remote_copy(
+            src_ref=src, dst_ref=dst, send_sem=ssem, recv_sem=rsem,
+            device_id=to, device_id_type=MESH,
+        )
+        copy.start()
+        return copy
+
+    sent = []
+    arrays = [(low_ref, full), (cot_ref, cfull)]
+    mine = block(z, x, y, core)
+    for a, (src, dst) in enumerate(arrays):
+        for k in range(1, n_z):
+            sent.append(send(src, dst.at[pl.ds(mine, rows)], zs.at[a, k], zr.at[a, k], dev(z_to[k], x, y, core)))
+    own_cols = pl.multiple_of(s * width, width)
+    for k in range(1, n_seq):
+        sent.append(send(
+            weight_ref.at[:, pl.ds(pl.multiple_of(s_to[k] * sl, sl), sl), :],
+            wt.at[:, :, pl.ds(own_cols, width)], ws.at[k], wr.at[k], (s_to[k], c),
+        ))
+    for src, dst in arrays:
+        dst[pl.ds(mine, rows), :] = src[...]
+    wt[:, :, pl.ds(own_cols, width)] = weight_ref[:, pl.ds(pl.multiple_of(s * sl, sl), sl), :]
+
+    sibling = dev(z, x, y, 1 - core)
+
+    def rows_of(dst, zz, p):
+        xx, yy = ((x, y) if p is None else plane[p])
+        return dst.at[pl.ds(block(zz, xx, yy, core), rows)]
+
+    def recv(dst_view, ssem, rsem):
+        pltpu.make_async_remote_copy(
+            src_ref=dst_view, dst_ref=dst_view, send_sem=ssem, recv_sem=rsem,
+            device_id=(s, c), device_id_type=MESH,
+        ).wait_recv()
+
+    def spread_plane(a, j):
+        dst = arrays[a][1]
+        view = rows_of(dst, z_from[j], None)
+        for p, (xx, yy) in enumerate(plane):
+            sent.append(send(view, view, ps.at[a, j, p], pr.at[a, j, p], dev(z, xx, yy, core)))
+        sent.append(send(view, view, cs.at[a, j, 3], cr.at[a, j, 3], sibling))
+
+    def pass_to_sibling(a, j):
+        dst = arrays[a][1]
+        for p in range(3):
+            view = rows_of(dst, z_from[j], p)
+            recv(view, ps.at[a, j, p], pr.at[a, j, p])
+            sent.append(send(view, view, cs.at[a, j, p], cr.at[a, j, p], sibling))
+
+    def from_sibling(a, j):
+        dst = arrays[a][1]
+        for p in range(4):
+            xx, yy = (x, y) if p == 3 else plane[p]
+            view = dst.at[pl.ds(block(z_from[j], xx, yy, 1 - core), rows)]
+            recv(view, cs.at[a, j, p], cr.at[a, j, p])
+
+    for a in (0, 1):
+        spread_plane(a, 0)
+    for j in range(1, n_z):
+        for a in (0, 1):
+            view = rows_of(arrays[a][1], z_from[j], None)
+            recv(view, zs.at[a, j], zr.at[a, j])
+            spread_plane(a, j)
+    for j in range(n_z):
+        for a in (0, 1):
+            pass_to_sibling(a, j)
+    for k in range(1, n_seq):
+        view = wt.at[:, :, pl.ds(pl.multiple_of(s_from[k] * width, width), width)]
+        recv(view, ws.at[k], wr.at[k])
+
+    group = n_ch * 2 * rows
+    per = 2 * 2 * rows
+
+    def compute(j):
+        for a in (0, 1):
+            from_sibling(a, j)
+        at = pl.multiple_of(z_from[j] * group, group)
+        rows_in = full[pl.ds(at, group), :]
+        gate = contract_last(rows_in, wt[0])
+        up = contract_last(rows_in, wt[1])
+        hg = contract_last(cfull[pl.ds(at, group), :], wt[2])
+        inner = K1 * (gate + K2 * gate * gate * gate)
+        t = jnp.tanh(inner)
+        sm = 0.5 * gate * (1.0 + t)
+        dsm = 0.5 * (1.0 + t) + 0.5 * gate * (1.0 - t * t) * K1 * (1.0 + 3.0 * K2 * gate * gate)
+        hidden = (sm * up).astype(jnp.bfloat16)
+        gg = (hg * up * dsm).astype(jnp.bfloat16)
+        ug = (hg * sm).astype(jnp.bfloat16)
+        hid[pl.ds(at, group), :] = hidden
+        gat[pl.ds(at, group), :] = gg
+        upg[pl.ds(at, group), :] = ug
+
+        def tile(i, _):
+            cols = pl.ds(pl.multiple_of(i * 256, 256), 256)
+            nf = jnp.dot(gg, wt[0, :, cols], preferred_element_type=jnp.float32)
+            nf = nf + jnp.dot(ug, wt[1, :, cols], preferred_element_type=jnp.float32)
+            ot = jnp.dot(hidden, wt[2, :, cols], preferred_element_type=jnp.float32)
+            for b, value in ((0, nf), (1, ot)):
+                value = value.astype(jnp.bfloat16)
+                for xx in range(2):
+                    for yy in range(2):
+                        for cc in range(2):
+                            at_row = (xx * 4 + yy * 2 + cc) * rows
+                            part[j, b, cc, xx * 2 + yy, :, cols] = value[at_row : at_row + rows]
+            return 0
+
+        lax.fori_loop(0, full.shape[1] // 256, tile, 0)
+        for b in (0, 1):
+            sent.append(send(part.at[j, b, 1 - core], sib.at[j, b], rs1.at[j, b], rr1.at[j, b], sibling))
+
+    def second(j, b):
+        recv(sib.at[j, b], rs1.at[j, b], rr1.at[j, b])
+
+        def add(i, _):
+            psum_buf[j, b, i] = (part[j, b, core, i].astype(jnp.float32) + sib[j, b, i].astype(jnp.float32)).astype(jnp.bfloat16)
+            return 0
+
+        lax.fori_loop(0, 4, add, 0)
+        for p, (xx, yy) in enumerate(plane):
+            sent.append(send(psum_buf.at[j, b, xx * 2 + yy], pl_in.at[j, b, p], rs2.at[j, b, p], rr2.at[j, b, p], dev(z, xx, yy, core)))
+
+    def third(j, b):
+        total = psum_buf[j, b, x * 2 + y].astype(jnp.float32)
+        for p in range(3):
+            recv(pl_in.at[j, b, p], rs2.at[j, b, p], rr2.at[j, b, p])
+            total = total + pl_in[j, b, p].astype(jnp.float32)
+        if j == 0:
+            (grad_ref, out_ref)[b][...] = total
+        else:
+            zsum[j, b] = total.astype(jnp.bfloat16)
+            sent.append(send(zsum.at[j, b], z_in.at[j, b], rs3.at[j, b], rr3.at[j, b], dev(z_from[j], x, y, core)))
+
+    for j in range(n_z):
+        compute(j)
+        for b in (0, 1):
+            if j >= 1:
+                second(j - 1, b)
+            if j >= 2:
+                third(j - 2, b)
+    for b in (0, 1):
+        second(n_z - 1, b)
+    for b in (0, 1):
+        third(n_z - 2, b)
+
+    def grads(i, _):
+        cols = pl.ds(pl.multiple_of(i * 256, 256), 256)
+        dwl[0, :, cols] = contract_first(gat[...], full[:, cols]).astype(jnp.bfloat16)
+        dwl[1, :, cols] = contract_first(upg[...], full[:, cols]).astype(jnp.bfloat16)
+        dwl[2, :, cols] = contract_first(hid[...], cfull[:, cols]).astype(jnp.bfloat16)
+        return 0
+
+    lax.fori_loop(0, full.shape[1] // 256, grads, 0)
+    own_rows = pl.multiple_of(s * sl, sl)
+    for k in range(1, n_seq):
+        cols = pl.ds(pl.multiple_of(s_to[k] * width, width), width)
+        sent.append(send(dwl.at[:, :, cols], dw_ref.at[:, pl.ds(own_rows, sl), :], ds_.at[k], dr_.at[k], (s_to[k], c)))
+    dw_ref[:, pl.ds(own_rows, sl), :] = dwl[:, :, pl.ds(own_cols, width)]
+    for b in (0, 1):
+        third(n_z - 1, b)
+    for b in (0, 1):
+        for j in range(1, n_z):
+            recv(z_in.at[j, b], rs3.at[j, b], rr3.at[j, b])
+            ref = (grad_ref, out_ref)[b]
+            ref[...] += z_in[j, b].astype(jnp.float32)
+    for k in range(1, n_seq):
+        view = dw_ref.at[:, pl.ds(pl.multiple_of(s_from[k] * sl, sl), sl), :]
+        recv(view, ds_.at[k], dr_.at[k])
+    for copy in sent:
+        copy.wait_send()
+
+
+def ffn(low, cot, weights):
+    n_seq, n_ch = lax.axis_size("seq"), lax.axis_size("ch")
+    rows, d = low.shape
+    width = weights.shape[2]
+    sl = weights.shape[1] // n_seq
+    n_z = n_seq // 2
+    tokens = n_seq * n_ch * rows
+    bf, f32 = jnp.bfloat16, jnp.float32
+    dma = pltpu.SemaphoreType.DMA
+    vmem = pl.BlockSpec(memory_space=pltpu.VMEM)
+    return pl.pallas_call(
+        functools.partial(ffn_kernel, (n_seq, n_ch, rows, width, sl)),
+        out_shape=[
+            jax.ShapeDtypeStruct((rows, d), f32),
+            jax.ShapeDtypeStruct((rows, d), f32),
+            jax.ShapeDtypeStruct(weights.shape, bf),
+        ],
+        in_specs=[vmem] * 3,
+        out_specs=[vmem] * 3,
+        scratch_shapes=[
+            pltpu.VMEM((3, sl, d), bf),
+            pltpu.VMEM((tokens, d), bf),
+            pltpu.VMEM((tokens, d), bf),
+            pltpu.VMEM((tokens, sl), bf),
+            pltpu.VMEM((tokens, sl), bf),
+            pltpu.VMEM((tokens, sl), bf),
+            pltpu.VMEM((n_z, 2, 2, 4, rows, d), bf),
+            pltpu.VMEM((n_z, 2, 4, rows, d), bf),
+            pltpu.VMEM((n_z, 2, 4, rows, d), bf),
+            pltpu.VMEM((n_z, 2, 3, rows, d), bf),
+            pltpu.VMEM((n_z, 2, rows, d), bf),
+            pltpu.VMEM((n_z, 2, rows, d), bf),
+            pltpu.VMEM((3, sl, d), bf),
+            dma((n_seq,)), dma((n_seq,)),
+            dma((2, n_z)), dma((2, n_z)),
+            dma((2, n_z, 3)), dma((2, n_z, 3)),
+            dma((2, n_z, 4)), dma((2, n_z, 4)),
+            dma((n_z, 2)), dma((n_z, 2)),
+            dma((n_z, 2, 3)), dma((n_z, 2, 3)),
+            dma((n_z, 2)), dma((n_z, 2)),
+            dma((n_seq,)), dma((n_seq,)),
+        ],
+        compiler_params=pltpu.CompilerParams(
+            collective_id=1, has_side_effects=True, vmem_limit_bytes=VMEM_BYTES
+        ),
+    )(low, cot, weights)
+
+
+def small_body(
+    stream,
+    cotangent,
+    mix_gain,
+    gelu_weight,
+    recur_weight,
+    conv_taps,
+    conv_bias,
+    rate_weight,
+    rate_bias,
+    inlet_weight,
+    inlet_bias,
+    decay_param,
+    init_states,
+    out_weight,
+    ffn_gain,
+    gate_weight,
+    up_weight,
+    down_weight,
+    doc_lengths,
+    block_counts,
+):
+    slot_count = rate_weight.shape[0]
+    block_width = rate_weight.shape[1]
+    local_width = slot_count * block_width
+    taps = conv_taps.shape[0]
+    token_count = stream.shape[0] * lax.axis_size("ch")
+    hidden_width = gate_weight.shape[1]
+    base = lax.axis_index("seq") * token_count
+    offset_all, opening, closing = doc_view(doc_lengths, base, token_count + taps - 1)
+    offset = offset_all[:token_count]
+    opening = opening[:token_count]
+    closing = closing[:token_count]
+    keep = (offset > 0).astype(jnp.float32)[:, None]
+    slot_live = (jnp.arange(slot_count, dtype=jnp.int32) < block_counts[0]).astype(jnp.float32)
+    live = jnp.repeat(slot_live, block_width)[None, :]
+    taps_flat = conv_taps.reshape(taps, local_width)
+    decay_flat = decay_param.reshape(1, local_width)
+    stream_float = stream.astype(jnp.float32)
+    mix_low = normalize(stream_float, mix_gain).astype(jnp.bfloat16)
+    mix_full = spread(mix_low)
+    gelu_pre = jnp.dot(mix_full, gelu_weight, preferred_element_type=jnp.float32)
+    recur_low = jnp.dot(mix_full, recur_weight, preferred_element_type=jnp.float32).astype(
+        jnp.bfloat16
+    )
+    rim = passed_along(recur_low[token_count - taps + 1 :], "seq", 1)
+    extended = jnp.concatenate([rim, recur_low], axis=0).astype(jnp.float32)
+    conv_pre = conv_bias.reshape(1, local_width)
+    for tap_index in range(taps):
+        valid = (offset >= tap_index).astype(jnp.float32)[:, None]
+        lead = taps - 1 - tap_index
+        conv_pre = (
+            conv_pre + taps_flat[tap_index][None, :] * extended[lead : lead + token_count] * valid
+        )
+    conv_low = conv_pre.astype(jnp.bfloat16)
+    conv_value = conv_low.astype(jnp.float32)
+    grouped = conv_low.reshape(token_count, slot_count, block_width)
+    rate_pre = (
+        jnp.einsum("rsi,sio->rso", grouped, rate_weight, preferred_element_type=jnp.float32)
+        + rate_bias[None]
+    ).reshape(token_count, local_width)
+    inlet_pre = (
+        jnp.einsum("rsi,sio->rso", grouped, inlet_weight, preferred_element_type=jnp.float32)
+        + inlet_bias[None]
+    ).reshape(token_count, local_width)
+    init_rows = jnp.dot(opening, init_states, precision=HIGH)
+    carry_factor, source = coefficients(
+        rate_pre, inlet_pre, conv_value, decay_flat, init_rows, keep
+    )
+    cumulative, local_state = lax.associative_scan(affine, (carry_factor, source), axis=0)
+    summary = (cumulative[-1], local_state[-1])
+    entering = entering_2(
+        summary, "seq", affine, (jnp.ones_like(summary[0]), jnp.zeros_like(summary[1])), False
+    )
+    state_in = entering[1]
+    state = local_state + cumulative * state_in[None, :]
+    gelu_value = smooth(gelu_pre)
+    product_low = (gelu_value * state * live).astype(jnp.bfloat16)
+    branch = collect(jnp.dot(product_low, out_weight, preferred_element_type=jnp.float32))
+    middle = stream_float + branch
+    ffn_low = normalize(middle, ffn_gain).astype(jnp.bfloat16)
+    weights = jnp.stack([gate_weight.T, up_weight.T, down_weight])
+    ffn_sum, norm_ffn_grad, dw = ffn(ffn_low, cotangent, weights)
+    mixed_out = (middle + ffn_sum).astype(jnp.bfloat16)
+    unused, ffn_norm_pull = jax.vjp(normalize, middle, ffn_gain)
+    middle_norm_grad, ffn_gain_part = ffn_norm_pull(norm_ffn_grad)
+    middle_grad = cotangent.astype(jnp.float32) + middle_norm_grad
+    branch_full = spread(middle_grad.astype(jnp.bfloat16))
+    out_weight_grad = contract_first(product_low, branch_full)
+    product_grad = contract_last(branch_full, out_weight)
+    state_grad = product_grad * gelu_value * live
+    unused, gelu_pull = jax.vjp(smooth, gelu_pre)
+    gelu_low = gelu_pull(product_grad * state * live)[0].astype(jnp.bfloat16)
+    following = jnp.concatenate([carry_factor[1:], jnp.ones_like(carry_factor[:1])], axis=0)
+    cum_back, adjoint_local = lax.associative_scan(
+        affine, (jnp.flip(following, 0), jnp.flip(state_grad, 0)), axis=0
+    )
+    cum_back = jnp.flip(cum_back, 0)
+    adjoint_local = jnp.flip(adjoint_local, 0)
+    summary_back = (carry_factor[0] * cum_back[0], carry_factor[0] * adjoint_local[0])
+    arriving = entering_2(
+        summary_back,
+        "seq",
+        affine,
+        (jnp.ones_like(summary_back[0]), jnp.zeros_like(summary_back[1])),
+        True,
+    )
+    adjoint_in = arriving[1]
+    adjoint = adjoint_local + cum_back * adjoint_in[None, :]
+    previous_state = jnp.concatenate([state_in[None, :], state[:-1]], axis=0)
+
+    def local_coefficients(rate_value, inlet_value, conv_part, decay_value):
+        return coefficients(rate_value, inlet_value, conv_part, decay_value, init_rows, keep)
+
+    unused, coefficient_pull = jax.vjp(
+        local_coefficients, rate_pre, inlet_pre, conv_value, decay_flat
+    )
+    rate_grad, inlet_grad, conv_direct, decay_part = coefficient_pull(
+        (adjoint * previous_state, adjoint)
+    )
+    rate_low = rate_grad.astype(jnp.bfloat16).reshape(token_count, slot_count, block_width)
+    inlet_low = inlet_grad.astype(jnp.bfloat16).reshape(token_count, slot_count, block_width)
+    rate_weight_grad = jnp.einsum(
+        "rsi,rso->sio", grouped, rate_low, preferred_element_type=jnp.float32
+    )
+    inlet_weight_grad = jnp.einsum(
+        "rsi,rso->sio", grouped, inlet_low, preferred_element_type=jnp.float32
+    )
+    rate_bias_grad = jnp.sum(rate_low.astype(jnp.float32), axis=0)
+    inlet_bias_grad = jnp.sum(inlet_low.astype(jnp.float32), axis=0)
+    conv_back = jnp.einsum(
+        "rso,sio->rsi", rate_low, rate_weight, preferred_element_type=jnp.float32
+    )
+    conv_back = conv_back + jnp.einsum(
+        "rso,sio->rsi", inlet_low, inlet_weight, preferred_element_type=jnp.float32
+    )
+    conv_low_grad = (conv_direct + conv_back.reshape(token_count, local_width)).astype(jnp.bfloat16)
+    rim_back = passed_along(conv_low_grad[: taps - 1], "seq", -1)
+    ahead = jnp.concatenate([conv_low_grad, rim_back], axis=0).astype(jnp.float32)
+    own_grad = ahead[:token_count]
+    recur_grad = jnp.zeros((token_count, local_width), jnp.float32)
+    tap_grads = []
+    for tap_index in range(taps):
+        lead = taps - 1 - tap_index
+        valid_here = (offset >= tap_index).astype(jnp.float32)[:, None]
+        tap_grads.append(
+            jnp.sum(own_grad * extended[lead : lead + token_count] * valid_here, axis=0)
+        )
+        valid_ahead = (offset_all[tap_index : tap_index + token_count] >= tap_index).astype(
+            jnp.float32
+        )[:, None]
+        recur_grad = (
+            recur_grad
+            + taps_flat[tap_index][None, :]
+            * ahead[tap_index : tap_index + token_count]
+            * valid_ahead
+        )
+    conv_taps_grad = jnp.stack(tap_grads, axis=0).reshape(taps, slot_count, block_width)
+    conv_bias_grad = jnp.sum(own_grad, axis=0).reshape(slot_count, block_width)
+    recur_low_grad = recur_grad.astype(jnp.bfloat16)
+    gelu_weight_grad = contract_first(mix_full, gelu_low)
+    recur_weight_grad = contract_first(mix_full, recur_low_grad)
+    norm_mix_part = contract_last(gelu_low, gelu_weight) + contract_last(
+        recur_low_grad, recur_weight
+    )
+    norm_mix_grad = collect(norm_mix_part)
+    unused, mix_norm_pull = jax.vjp(normalize, stream_float, mix_gain)
+    stream_norm_grad, mix_gain_part = mix_norm_pull(norm_mix_grad)
+    stream_grad = middle_grad + stream_norm_grad
+    finals_local = lax.dot_general(closing, state * live, (((0,), (0,)), ((), ())), precision=HIGH)
+    finals_wide = jnp.zeros((finals_local.shape[0], local_width * lax.axis_size("ch")), jnp.float32)
+    finals_wide = lax.dynamic_update_slice(
+        finals_wide, finals_local, (jnp.int32(0), lax.axis_index("ch") * local_width)
+    )
+    final_states, mix_gain_grad, ffn_gain_grad = lax.psum(
+        (finals_wide, mix_gain_part, ffn_gain_part), ("seq", "ch")
+    )
+    summed = (
+        lax.psum_scatter(gelu_weight_grad, "seq", scatter_dimension=0, tiled=True),
+        lax.psum_scatter(recur_weight_grad, "seq", scatter_dimension=0, tiled=True),
+        lax.psum_scatter(conv_taps_grad, "seq", scatter_dimension=2, tiled=True),
+        lax.psum_scatter(conv_bias_grad, "seq", scatter_dimension=1, tiled=True),
+        lax.psum_scatter(rate_weight_grad, "seq", scatter_dimension=1, tiled=True),
+        lax.psum_scatter(rate_bias_grad, "seq", scatter_dimension=1, tiled=True),
+        lax.psum_scatter(inlet_weight_grad, "seq", scatter_dimension=1, tiled=True),
+        lax.psum_scatter(inlet_bias_grad, "seq", scatter_dimension=1, tiled=True),
+        lax.psum_scatter(
+            decay_part.reshape(slot_count, block_width), "seq", scatter_dimension=1, tiled=True
+        ),
+        lax.psum_scatter(out_weight_grad, "seq", scatter_dimension=1, tiled=True),
+        dw[0].T.astype(jnp.float32),
+        dw[1].T.astype(jnp.float32),
+        dw[2].astype(jnp.float32),
+    )
+    return (
+        final_states,
+        mixed_out,
+        stream_grad,
+        mix_gain_grad,
+        summed[0],
+        summed[1],
+        summed[2],
+        summed[3],
+        summed[4],
+        summed[5],
+        summed[6],
+        summed[7],
+        summed[8],
+        summed[9],
+        ffn_gain_grad,
+        summed[10],
+        summed[11],
+        summed[12],
+    )
+
+
 def solution(mesh):
     in_specs = (
         P(("seq", "ch"), None),
@@ -373,4 +847,4 @@
         P("seq", "ch"),
         P("ch", "seq"),
     )
-    return jax.shard_map(body, mesh=mesh, in_specs=in_specs, out_specs=out_specs, check_vma=False)
+    return jax.shard_map(small_body if mesh.shape['seq'] == 8 else body, mesh=mesh, in_specs=in_specs, out_specs=out_specs, check_vma=False)

time: 2550 us -> 1770 us (0.69)
  waiting for transfers between devices: 1810 us -> 924 us
  Pallas kernels: 0 us -> 175 us
  matrix products: 86.8 us -> 38.6 us
    reduce_scatter x8 -> x5, waiting for transfers between devices: 1130 us -> 493 us  [the longest x1 123 us: small_body(): lax.psum_scatter(gelu_weight_grad, 'seq', scatter_dimension=0, tiled=True)]
    all_gather x2 -> x0, waiting for transfers between devices: 237 us -> none  [the longest x1 145 us: body(): lax.all_gather(stacked, 'seq', axis=0, tiled=True)]
    pallas_call x0 -> x1, Pallas kernels: none -> 175 us  [ffn(): pl.pallas_call(functools.partial(ffn_kernel, (n_seq, n_ch, rows, width, s...]
    reduce_scatter x4 -> x2, waiting for transfers between devices: 49.7 us -> 14.1 us  [collect(): return lax.psum_scatter(terms, 'ch', scatter_dimension=0, tiled=True)]
    unnamed x25 -> x18, waiting for transfers between devices: 263 us -> 288 us
    slice x100 -> x99, local copies, waits for them, and re-layouts: 164 us -> 145 us  [the longest x49 82.2 us: small_body(): lax.associative_scan(affine, (jnp.flip(following, 0), jnp.flip(state_grad...]
  transfers between devices with their start and end apart: 22 -> 15, of which waited for: 21 -> 13; matrix products, arithmetic and copies ran while one was open for 4% -> 4% of each run, Pallas kernels for 0% -> 0%
where the time goes in v1:
time: 1770 us; the launch traced here: 1750 us
  waiting for transfers between devices  924 us (52%)
  local copies, waits for them, and re-layouts  318 us (18%)
  Pallas kernels  175 us (10%)
  blocking collectives  147 us (8%)
  other arithmetic  130 us (7%)
  matrix products  38.6 us (2%)
    unnamed x18, waiting for transfers between devices  288 us
    pallas_call x1, Pallas kernels, ffn(): pl.pallas_call(functools.partial(ffn_kernel, (n_seq, n_ch, rows, width, s...  175 us
    all_gather x4, blocking collectives, entering_2(): everything = jax.tree.map(lambda part: lax.all_gather(part, axis), shard)  131 us
    psum x1, waiting for transfers between devices, small_body(): lax.psum((finals_wide, mix_gain_part, ffn_gain_part), ('seq', 'ch'))  128 us
    reduce_scatter x1, waiting for transfers between devices, small_body(): lax.psum_scatter(gelu_weight_grad, 'seq', scatter_dimension=0, tiled=True)  123 us
    reduce_scatter x1, waiting for transfers between devices, small_body(): lax.psum_scatter(out_weight_grad, 'seq', scatter_dimension=1, tiled=True)  122 us
    reduce_scatter x1, waiting for transfers between devices, small_body(): lax.psum_scatter(recur_weight_grad, 'seq', scatter_dimension=0, tiled=True)  121 us
    slice x49, local copies, waits for them, and re-layouts, small_body(): lax.associative_scan(affine, (jnp.flip(following, 0), jnp.flip(state_grad...  82.2 us
  transfers between devices with their start and end apart: 15, of which 13 were waited for; matrix products, arithmetic and copies ran while one was open for 4% of the time, Pallas kernels for 0%

profile of v1, /device:TPU:0, one launch (start us, length us, event | category | flops | bytes accessed | tf_op | source)
XLA Modules:
  0.0 1754.9 jit_solution(13291833091814283205)
XLA Ops:
  9.5 8.6 all_gather.20
  19.0 2.5 convolution_convert_fusion
  21.5 3.4 collective-permute-start
  33.3 2.1 fusion.7
  44.5 2.7 fusion.11
  179.1 2.3 pad.198
  181.4 2.3 pad.199
  185.4 2.5 pad.201
  187.8 2.3 pad.185
  191.7 2.3 pad.184
  198.4 2.5 pad.200
  201.7 30.7 %all-gather = f32[8,1,768]{2,1,0:T(1,128)S(1)} all-gather(f32[1,1,768]{2,1,0:T(1,128)S(1)} %add_bitcast_fusion.1), channel_id=1, replica_groups=mesh['seq'=8,'ch'=4] {'seq'}, dimensions={0}, use_global_device_ids=true | all-gather | bytes 27648 | tf_op jit(solution)/shard_map/all_gather | solution.py:26
  232.9 2.5 pad.187
  237.0 2.5 pad.186
  240.3 30.3 %all-gather.1 = f32[8,1,768]{2,1,0:T(1,128)S(1)} all-gather(f32[1,1,768]{2,1,0:T(1,128)S(1)} %add_bitcast_fusion), channel_id=1, replica_groups=mesh['seq'=8,'ch'=4] {'seq'}, dimensions={0}, use_global_device_ids=true | all-gather | bytes 27648 | tf_op jit(solution)/shard_map/all_gather | solution.py:26
  271.2 6.6 while.30
  277.9 3.2 multiply_convert_fusion
  283.6 2.3 copy.113
  285.9 2.3 copy.112
  288.2 3.5 pad_maximum_fusion.weight_ref
  298.1 3.6 slice.604
  301.7 3.5 slice.613
  305.2 3.5 slice.606
  310.8 174.5 %shard_map.331 = (f32[32,2048]{1,0:T(8,128)}, f32[32,2048]{1,0:T(8,128)}, bf16[3,1536,256]{2,1,0:T(8,128)(2,1)}) custom-call(bf16[32,2048]{1,0:T(8,128)(2,1)} %multiply_convert_fusion.1.low_ref, bf16[32,2048]{1,0:T(8,128)(2,1)} %cot_ref.1, bf16[3,1536,256]{2,1,0:T(8,128)(2,1)} %pad_maximum_fusion.weight_ref), custom_call_target="tpu_custom_call" | custom-call | tf_op jit(solution)/shard_map/pallas_call | solution.py:553
  488.2 7.4 all_gather.23
  495.5 2.2 multiply_multiply_fusion.2
  501.1 3.5 slice.610
  504.6 3.5 slice.608
  619.1 2.3 pad.227
  631.1 2.3 pad.226
  633.3 3.6 slice.658
  636.9 2.3 pad.213
  640.7 2.2 pad.212
  649.2 2.5 pad.214
  651.7 2.5 pad.215
  655.8 2.5 pad.228
  658.3 2.5 pad.229
  665.4 3.9 rev.9
  669.2 3.8 rev.10
  673.1 39.6 %all-gather.2 = f32[8,1,768]{2,1,0:T(1,128)S(1)} all-gather(f32[1,1,768]{2,1,0:T(1,128)S(1)} %get-tuple-element.423), channel_id=1, replica_groups=mesh['seq'=8,'ch'=4] {'seq'}, dimensions={0}, use_global_device_ids=true | all-gather | bytes 27648 | tf_op jit(solution)/shard_map/all_gather | solution.py:26
  713.3 30.3 %all-gather.3 = f32[8,1,768]{2,1,0:T(1,128)S(1)} all-gather(f32[1,1,768]{2,1,0:T(1,128)S(1)} %get-tuple-element.422), channel_id=1, replica_groups=mesh['seq'=8,'ch'=4] {'seq'}, dimensions={0}, use_global_device_ids=true | all-gather | bytes 27648 | tf_op jit(solution)/shard_map/all_gather | solution.py:26
  744.2 6.6 while.31
  751.0 3.5 multiply_reduce_fusion
  758.4 2.1 fusion.97
  762.3 2.2 fusion
  771.3 2.2 fusion.96
  786.4 14.1 reduce-scatter.25.cloned.1.call-done
  802.5 3.6 fusion.98
  807.3 3.6 fusion.102
  810.9 3.7 fusion.99
  816.3 2.3 bitcast_convert_fusion
  818.6 3.2 copy.129
  821.8 3.0 copy.130
  824.8 39.8 %reduce-scatter.41.cloned.1.call-done = f32[32,3]{1,0:T(8,128)} async-done(((f32[256,3]{1,0:T(8,128)}), f32[32,3]{1,0:T(8,128)}) %reduce-scatter.41.cloned.1.call-update) | async-done | bytes 400
  866.1 61.7 %reduce-scatter.43.cloned.1.call-done = f32[32,3]{1,0:T(8,128)} async-done(((f32[256,3]{1,0:T(8,128)}), f32[32,3]{1,0:T(8,128)}) %reduce-scatter.43.cloned.1.call-update) | async-done | bytes 400
  929.1 61.7 %reduce-scatter.45.cloned.1.call-done = f32[32,3]{1,0:T(8,128)} async-done(((f32[256,3]{1,0:T(8,128)}), f32[32,3]{1,0:T(8,128)}) %reduce-scatter.45.cloned.1.call-update) | async-done | bytes 400
  992.2 61.7 %reduce-scatter.39.cloned.1.call-done = f32[32,3]{1,0:T(8,128)} async-done(((f32[256,3]{1,0:T(8,128)}), f32[32,3]{1,0:T(8,128)}) %reduce-scatter.39.cloned.1.call-update) | async-done | bytes 400
  1055.3 62.5 %reduce-scatter.37.cloned.1.call-done = f32[32,12]{1,0:T(8,128)} async-done(((f32[256,12]{1,0:T(8,128)}), f32[32,12]{1,0:T(8,128)}) %reduce-scatter.37.cloned.1.call-update) | async-done | bytes 1552
  1123.4 60.4 %reduce-scatter.31.cloned.1.call-done = f32[3,32,256]{2,1,0:T(8,128)} async-done(((f32[3,256,256]{2,1,0:T(8,128)}), f32[3,32,256]{2,1,0:T(8,128)}) %reduce-scatter.31.cloned.1.call-update) | async-done | bytes 98320 | tf_op jit(solution)/shard_map/reduce_scatter | solution.py:773
  1183.9 66.6 %reduce-scatter.33.cloned.1.call-done = f32[3,32,256]{2,1,0:T(8,128)} async-done(((f32[3,256,256]{2,1,0:T(8,128)}), f32[3,32,256]{2,1,0:T(8,128)}) %reduce-scatter.33.cloned.1.call-update) | async-done | bytes 98320 | tf_op jit(solution)/shard_map/reduce_scatter | solution.py:775
  1250.5 127.7 %all-reduce.61.cloned.1.call-done = (f32[5,3072]{1,0:T(8,128)}, f32[2048]{0:T(1024)}, f32[2048]{0:T(1024)}) async-done(((f32[5,3072]{1,0:T(8,128)}, f32[2048]{0:T(1024)}, f32[2048]{0:T(1024)}), (f32[5,3072]{1,0:T(8,128)}, f32[2048]{0:T(1024)}, f32[2048]{0:T(1024)})) %all-reduce.61.cloned.1.call-update) | async-done | bytes 77840 | tf_op jit(solution)/shard_map/psum | solution.py:765
  1378.2 123.1 %reduce-scatter.27.cloned.1.call-done = f32[256,768]{1,0:T(8,128)} async-done(((f32[2048,768]{1,0:T(8,128)}), f32[256,768]{1,0:T(8,128)}) %reduce-scatter.27.cloned.1.call-update) | async-done | bytes 786448 | tf_op jit(solution)/shard_map/reduce_scatter | solution.py:769
  1501.3 121.6 %reduce-scatter.35.cloned.1.call-done = f32[768,256]{1,0:T(8,128)} async-done(((f32[768,2048]{1,0:T(8,128)}), f32[768,256]{1,0:T(8,128)}) %reduce-scatter.35.cloned.1.call-update) | async-done | bytes 786448 | tf_op jit(solution)/shard_map/reduce_scatter | solution.py:780
  1622.9 121.3 %reduce-scatter.29.cloned.1.call-done = f32[256,768]{1,0:T(8,128)} async-done(((f32[2048,768]{1,0:T(8,128)}), f32[256,768]{1,0:T(8,128)}) %reduce-scatter.29.cloned.1.call-update) | async-done | bytes 786448 | tf_op jit(solution)/shard_map/reduce_scatter | solution.py:770
  (518 shorter events, 374.1 us)
Async XLA Ops:
  7.2 270.7 %copy-start = (bf16[2048,768]{1,0:T(8,128)(2,1)S(1)}, bf16[2048,768]{1,0:T(8,128)(2,1)}, u32[]{:S(2)}) copy-start(bf16[2048,768]{1,0:T(8,128)(2,1)} %param.27) | copy-start | bytes 9437188
  7.2 17.7 %copy-start.83 = (s32[5]{0:T(128)S(1)}, s32[5]{0:T(128)}, u32[]{:S(2)}) copy-start(s32[5]{0:T(128)} %param.42) | copy-start | bytes 64
  7.2 21.5 %copy-start.67 = (f32[4,3,256]{2,0,1:T(4,128)S(1)}, f32[4,3,256]{2,0,1:T(4,128)}, u32[]{:S(2)}) copy-start(f32[4,3,256]{2,0,1:T(4,128)} %param.29) | copy-start | bytes 36868
  7.2 21.6 %copy-start.53 = (f32[3,256]{1,0:T(4,128)S(1)}, f32[3,256]{1,0:T(4,128)}, u32[]{:S(2)}) copy-start(f32[3,256]{1,0:T(4,128)} %param.35) | copy-start | bytes 9220
  7.2 23.5 %copy-start.75 = (f32[3,256]{1,0:T(4,128)S(1)}, f32[3,256]{1,0:T(4,128)}, u32[]{:S(2)}) copy-start(f32[3,256]{1,0:T(4,128)} %param.30) | copy-start | bytes 9220
  7.2 301.5 %reduce-scatter.23.cloned.1.call-start = ((), (), s32[]{:S(2)}) async-start(), calls=%async_computation.12 | async-start | bytes 1310720 | tf_op jit(solution)/shard_map/reduce_scatter | solution.py:82
  8.5 16.4 copy-start.82
  8.5 17.1 copy-start.73
  21.5 9.9 collective-permute-start
  25.6 5.8 copy-start.76
  30.1 8.4 copy-start.34
  30.1 8.4 copy-start.36
  30.2 8.4 copy-start.38
  130.1 48.3 %copy-start.69 = (f32[1,768]{1,0:T(1,128)S(1)}, f32[1,768]{1,0:T(1,128)}, u32[]{:S(2)}) copy-start(f32[1,768]{1,0:T(1,128)} %slice.718) | copy-start | bytes 9220
  173.5 24.3 %copy-start.65 = (f32[1,768]{1,0:T(1,128)S(1)}, f32[1,768]{1,0:T(1,128)}, u32[]{:S(2)}) copy-start(f32[1,768]{1,0:T(1,128)} %slice.717) | copy-start | bytes 9220
  179.1 56.3 %copy-start.64 = (f32[1,768]{1,0:T(1,128)S(1)}, f32[1,768]{1,0:T(1,128)}, u32[]{:S(2)}) copy-start(f32[1,768]{1,0:T(1,128)} %slice.694) | copy-start | bytes 9220
  187.8 90.0 %copy-start.46 = (f32[768]{0:T(1024)S(1)}, f32[768]{0:T(1024)}, u32[]{:S(2)}) copy-start(f32[768]{0:T(1024)} %mul.756) | copy-start | bytes 9220
  283.3 517.1 %reduce-scatter.25.cloned.1.call-start = ((), (), s32[]{:S(2)}) async-start(), calls=%async_computation.13 | async-start | bytes 1310720 | tf_op jit(solution)/shard_map/reduce_scatter | solution.py:82
  291.7 18.4 %copy-start.32 = (f32[2048]{0:T(1024)S(1)}, f32[2048]{0:T(1024)}, u32[]{:S(2)}) copy-start(f32[2048]{0:T(1024)} %param.38) | copy-start | bytes 24580
  301.7 193.8 %copy-start.47 = (f32[768]{0:T(1024)S(1)}, f32[768]{0:T(1024)}, u32[]{:S(2)}) copy-start(f32[768]{0:T(1024)} %mul.756) | copy-start | bytes 9220
  308.8 178.3 %copy-start.28 = (bf16[32,2048]{1,0:T(8,128)(2,1)S(1)}, bf16[32,2048]{1,0:T(8,128)(2,1)}, u32[]{:S(2)}) copy-start(bf16[32,2048]{1,0:T(8,128)(2,1)} %cot_ref.1) | copy-start | bytes 393220
  308.8 186.8 %copy-start.12 = (f32[128,768]{1,0:T(8,128)S(1)}, f32[128,768]{1,0:T(8,128)}, u32[]{:S(2)}) copy-start(f32[128,768]{1,0:T(8,128)} %get-tuple-element.406) | copy-start | bytes 1179652
  308.8 186.8 %copy-start.17 = (bf16[768,2048]{1,0:T(8,128)(2,1)S(1)}, bf16[768,2048]{1,0:T(8,128)(2,1)}, u32[]{:S(2)}) copy-start(bf16[768,2048]{1,0:T(8,128)(2,1)} %param.37) | copy-start | bytes 9437188
  308.8 186.8 %copy-start.30 = (f32[128,768]{1,0:T(8,128)S(1)}, f32[128,768]{1,0:T(8,128)}, u32[]{:S(2)}) copy-start(f32[128,768]{1,0:T(8,128)} %get-tuple-element.499) | copy-start | bytes 1179652
  310.1 187.7 %copy-start.9 = (f32[32,2048]{1,0:T(8,128)}, f32[32,2048]{1,0:T(8,128)S(1)}, u32[]{:S(2)}) copy-start(f32[32,2048]{1,0:T(8,128)S(1)} %get-tuple-element.404) | copy-start | bytes 786436
  310.1 187.6 %copy-start.72 = (f32[32]{0:T(128)}, f32[32]{0:T(128)S(1)}, u32[]{:S(2)}) copy-start(f32[32]{0:T(128)S(1)} %fusion.79) | copy-start | bytes 388
  487.1 10.7 copy-start.77
  596.2 34.2 %copy-start.70 = (f32[1,768]{1,0:T(1,128)S(1)}, f32[1,768]{1,0:T(1,128)}, u32[]{:S(2)}) copy-start(f32[1,768]{1,0:T(1,128)} %slice.764) | copy-start | bytes 9220
  596.2 43.0 %copy-start.68 = (f32[1,768]{1,0:T(1,128)S(1)}, f32[1,768]{1,0:T(1,128)}, u32[]{:S(2)}) copy-start(f32[1,768]{1,0:T(1,128)} %slice.742) | copy-start | bytes 9220
  619.1 29.4 %copy-start.66 = (f32[1,768]{1,0:T(1,128)S(1)}, f32[1,768]{1,0:T(1,128)}, u32[]{:S(2)}) copy-start(f32[1,768]{1,0:T(1,128)} %slice.740) | copy-start | bytes 9220
  654.1 96.9 %copy-start.35 = (f32[768]{0:T(1024)S(1)}, f32[768]{0:T(1024)}, u32[]{:S(2)}) copy-start(f32[768]{0:T(1024)} %copy-done.34) | copy-start | bytes 9220
  756.7 11.7 copy-start.43
  768.4 7.1 copy-start.41
  768.4 7.1 copy-start.50
  768.4 7.1 copy-start.79
  768.4 7.1 copy-start.80
  768.4 7.1 copy-start.81
  769.9 5.5 collective-permute-start.1
  775.9 5.0 copy-start.4
  775.9 5.0 copy-start.51
  775.9 5.0 copy-start.59
  778.1 5.5 copy-start.24
  778.1 5.5 copy-start.26
  778.1 86.6 %reduce-scatter.41.cloned.1.call-start = ((), (), s32[]{:S(2)}) async-start(), calls=%async_computation.21 | async-start | bytes 147456
  779.0 5.9 copy-start.25
  779.0 148.8 %reduce-scatter.43.cloned.1.call-start = ((), (), s32[]{:S(2)}) async-start(), calls=%async_computation.22 | async-start | bytes 147456
  779.9 210.9 %reduce-scatter.45.cloned.1.call-start = ((), (), s32[]{:S(2)}) async-start(), calls=%async_computation.23 | async-start | bytes 147456
  780.8 273.1 %reduce-scatter.39.cloned.1.call-start = ((), (), s32[]{:S(2)}) async-start(), calls=%async_computation.20 | async-start | bytes 147456
  781.3 19.2 %copy-start.15 = (bf16[32,2048]{1,0:T(8,128)(2,1)S(1)}, bf16[32,2048]{1,0:T(8,128)(2,1)}, u32[]{:S(2)}) copy-start(bf16[32,2048]{1,0:T(8,128)(2,1)} %param.24) | copy-start | bytes 393220
  781.3 19.2 %copy-start.44 = (f32[2048]{0:T(1024)S(1)}, f32[2048]{0:T(1024)}, u32[]{:S(2)}) copy-start(f32[2048]{0:T(1024)} %param.26) | copy-start | bytes 24580
  781.3 19.1 %copy-start.74 = (f32[32]{0:T(128)S(1)}, f32[32]{0:T(128)}, u32[]{:S(2)}) copy-start(f32[32]{0:T(128)} %copy-done.73) | copy-start | bytes 388
  782.2 335.5 %reduce-scatter.37.cloned.1.call-start = ((), (), s32[]{:S(2)}) async-start(), calls=%async_computation.19 | async-start | bytes 147456
  782.3 20.2 %copy-start.6 = (bf16[128,2048]{1,0:T(8,128)(2,1)S(1)}, bf16[128,2048]{1,0:T(8,128)(2,1)}, u32[]{:S(2)}) copy-start(bf16[128,2048]{1,0:T(8,128)(2,1)} %copy-done.5) | copy-start | bytes 1572868
  782.3 20.2 %copy-start.29 = (bf16[128,768]{1,0:T(8,128)(2,1)S(1)}, bf16[128,768]{1,0:T(8,128)(2,1)}, u32[]{:S(2)}) copy-start(bf16[128,768]{1,0:T(8,128)(2,1)} %get-tuple-element.417) | copy-start | bytes 589828
  783.5 400.4 %reduce-scatter.31.cloned.1.call-start = ((), (), s32[]{:S(2)}) async-start(), calls=%async_computation.16 | async-start | bytes 884736 | tf_op jit(solution)/shard_map/reduce_scatter | solution.py:773
  784.8 465.7 %reduce-scatter.33.cloned.1.call-start = ((), (), s32[]{:S(2)}) async-start(), calls=%async_computation.17 | async-start | bytes 884736 | tf_op jit(solution)/shard_map/reduce_scatter | solution.py:775
  786.0 592.2 %all-reduce.61.cloned.1.call-start = ((), (), s32[]{:S(2)}) async-start(), calls=%async_computation.24 | async-start | bytes 229376 | tf_op jit(solution)/shard_map/psum | solution.py:765
  786.4 15.7 copy-start.31
  802.2 699.1 %reduce-scatter.27.cloned.1.call-start = ((), (), s32[]{:S(2)}) async-start(), calls=%async_computation.14 | async-start | bytes 7077888 | tf_op jit(solution)/shard_map/reduce_scatter | solution.py:769
  806.2 816.7 %reduce-scatter.35.cloned.1.call-start = ((), (), s32[]{:S(2)}) async-start(), calls=%async_computation.18 | async-start | bytes 7077888 | tf_op jit(solution)/shard_map/reduce_scatter | solution.py:780
  810.9 933.3 %reduce-scatter.29.cloned.1.call-start = ((), (), s32[]{:S(2)}) async-start(), calls=%async_computation.15 | async-start | bytes 7077888 | tf_op jit(solution)/shard_map/reduce_scatter | solution.py:770
  818.6 302.7 %copy-start.10 = (f32[32,2048]{1,0:T(8,128)S(1)}, f32[32,2048]{1,0:T(8,128)}, u32[]{:S(2)}) copy-start(f32[32,2048]{1,0:T(8,128)} %copy-done.9) | copy-start | bytes 786436
  818.6 302.7 %copy-start.33 = (f32[2048]{0:T(1024)S(1)}, f32[2048]{0:T(1024)}, u32[]{:S(2)}) copy-start(f32[2048]{0:T(1024)} %param.38) | copy-start | bytes 24580
  818.6 929.7 %copy-start.1 = (bf16[2048,768]{1,0:T(8,128)(2,1)S(1)}, bf16[2048,768]{1,0:T(8,128)(2,1)}, u32[]{:S(2)}) copy-start(bf16[2048,768]{1,0:T(8,128)(2,1)} %param.27) | copy-start | bytes 9437188
  (36 other events, 122.7 us)
Sparse Core Ops, SparseCore 0:
  283.5 23.0 reduce-scatter.22
  778.2 22.2 reduce-scatter.24
  803.8 60.8 reduce-scatter.40
  867.9 59.8 reduce-scatter.42
  930.9 59.8 reduce-scatter.44
  994.0 59.8 reduce-scatter.38
  1057.8 59.8 reduce-scatter.36
  1121.6 62.1 reduce-scatter.30
  1188.2 62.2 reduce-scatter.32
  1257.4 120.7 all-reduce.60
  1382.3 118.9 reduce-scatter.26
  1505.3 117.5 reduce-scatter.34
  1627.1 117.1 reduce-scatter.28

commit v2 on v1

--- a/solution.py
+++ b/solution.py
@@ -336,6 +336,332 @@
         summed[11],
         summed[12],
     )
+
+
+class Net:
+    def __init__(self, n_seq, n_ch, rows, send_sems, recv_sems):
+        self.n_seq, self.n_ch, self.rows = n_seq, n_ch, rows
+        self.n_z = n_seq // 2
+        self.send_sems, self.recv_sems = send_sems, recv_sems
+        self.tags, self.sent = {}, []
+        self.s, self.c = lax.axis_index("seq"), lax.axis_index("ch")
+        s, c, n_z = self.s, self.c, self.n_z
+        self.z, self.x, self.y, self.core = s // 2, s % 2, c // 2, c % 2
+        x, y = self.x, self.y
+        self.plane = [(1 - x, y), (x, 1 - y), (1 - x, 1 - y)]
+        self.z_to = [(self.z + k) % n_z for k in range(n_z)]
+        self.z_from = [(self.z + n_z - k) % n_z for k in range(n_z)]
+        self.s_to = [(s + k) % n_seq for k in range(n_seq)]
+        self.s_from = [(s + n_seq - k) % n_seq for k in range(n_seq)]
+        self.sibling = self.dev(self.z, x, y, 1 - self.core)
+        self.across = self.dev(self.z, x, 1 - y, self.core)
+
+    def dev(self, z, x, y, core):
+        return (z * 2 + x, y * 2 + core)
+
+    def block(self, z, x, y, core):
+        rows = self.rows
+        return pl.multiple_of(((z * 2 + x) * self.n_ch + y * 2 + core) * rows, rows)
+
+    def seq_peers(self):
+        return [(self.s_to[k], self.c) for k in range(1, self.n_seq)]
+
+    def plane_peers(self):
+        return [self.dev(self.z, xx, yy, self.core) for xx, yy in self.plane]
+
+    def meet(self, peers):
+        barrier = pltpu.get_barrier_semaphore()
+        for peer in peers:
+            pl.semaphore_signal(barrier, inc=1, device_id=peer, device_id_type=MESH)
+        pl.semaphore_wait(barrier, len(peers))
+
+    def sems(self, tag):
+        at = self.tags.setdefault(tag, len(self.tags))
+        return self.send_sems.at[at], self.recv_sems.at[at]
+
+    def copy(self, src, dst, tag, to):
+        ssem, rsem = self.sems(tag)
+        return pltpu.make_async_remote_copy(
+            src_ref=src, dst_ref=dst, send_sem=ssem, recv_sem=rsem,
+            device_id=to, device_id_type=MESH,
+        )
+
+    def send(self, src, dst, tag, to):
+        copy = self.copy(src, dst, tag, to)
+        copy.start()
+        self.sent.append(copy)
+
+    def recv(self, view, tag):
+        self.copy(view, view, tag, (self.s, self.c)).wait_recv()
+
+    def drain(self):
+        for copy in self.sent:
+            copy.wait_send()
+        self.sent = []
+
+    def ch_gather_start(self, view_of, tag):
+        mine = view_of(self.c)
+        self.send(mine, mine, (tag, "y"), self.across)
+        self.send(mine, mine, (tag, "core"), self.sibling)
+
+    def ch_gather_finish(self, view_of, tag):
+        y, core = self.y, self.core
+        theirs = view_of((1 - y) * 2 + core)
+        self.recv(theirs, (tag, "y"))
+        self.send(theirs, theirs, (tag, "fwd"), self.sibling)
+        self.recv(view_of(y * 2 + 1 - core), (tag, "core"))
+        self.recv(view_of((1 - y) * 2 + 1 - core), (tag, "fwd"))
+
+    def ch_sum(self, part, mid, low, far, tag):
+        y, core = self.y, self.core
+        self.send(part.at[1 - core], mid, (tag, "core"), self.sibling)
+        self.recv(mid, (tag, "core"))
+        low[...] = (part[core, 1 - y] + mid[1 - y]).astype(jnp.bfloat16)
+        self.send(low, far, (tag, "y"), self.across)
+        total = part[core, y] + mid[y]
+        self.recv(far, (tag, "y"))
+        return total + far[...].astype(jnp.float32)
+
+
+def stack_rows(rows):
+    return jnp.concatenate(rows, axis=0)
+
+
+def smooth_pair(v):
+    t = jnp.tanh(K1 * (v + K2 * v * v * v))
+    value = 0.5 * v * (1.0 + t)
+    slope = 0.5 * (1.0 + t) + 0.5 * v * (1.0 - t * t) * K1 * (1.0 + 3.0 * K2 * v * v)
+    return value, slope
+
+
+def sigmoid(v):
+    return 1.0 / (1.0 + jnp.exp(-v))
+
+
+def softplus_exact(d):
+    u = jnp.exp(-jnp.abs(d))
+    r = u / (2.0 + u)
+    q = r * r
+    series = 1.0 / 15.0
+    for k in (13, 11, 9, 7, 5, 3, 1):
+        series = series * q + 1.0 / k
+    return jnp.maximum(d, 0.0) + 2.0 * r * series
+
+
+def minus_expm1(v):
+    series = 1.0 / 362880.0
+    for k in (40320.0, 5040.0, 720.0, 120.0, 24.0, 6.0, 2.0, 1.0):
+        series = series * v + 1.0 / k
+    return jnp.where(v > -0.5, -v * series, 1.0 - jnp.exp(v))
+
+
+class Docs:
+    def __init__(self, lengths, first, count, before=0):
+        position = first - before + lax.broadcasted_iota(jnp.int32, (count, 1), 0)
+        self.opening, self.closing = [], []
+        start_of = jnp.zeros((count, 1), jnp.int32)
+        start = jnp.int32(0)
+        for e in range(lengths.shape[0]):
+            end = start + lengths[e]
+            owner = (position >= start) & (position < end)
+            start_of = jnp.where(owner, start, start_of)
+            self.opening.append((position == start).astype(jnp.float32))
+            self.closing.append((position == end - 1).astype(jnp.float32))
+            start = end
+        self.offset = position - start_of
+        self.keep = (self.offset > 0).astype(jnp.float32)
+
+    def valid(self, k):
+        return (self.offset >= k).astype(jnp.float32)
+
+
+def prefix(a, b, count):
+    row = lax.broadcasted_iota(jnp.int32, a.shape, 0)
+    k = 1
+    while k < count:
+        inside = row >= k
+        a_far = jnp.where(inside, pltpu.roll(a, k, 0), 1.0)
+        b_far = jnp.where(inside, pltpu.roll(b, k, 0), 0.0)
+        b = a * b_far + b
+        a = a * a_far
+        k *= 2
+    return a, b
+
+
+def suffix(a, b, count):
+    row = lax.broadcasted_iota(jnp.int32, a.shape, 0)
+    k = 1
+    while k < count:
+        inside = row < count - k
+        a_far = jnp.where(inside, pltpu.roll(a, count - k, 0), 1.0)
+        b_far = jnp.where(inside, pltpu.roll(b, count - k, 0), 0.0)
+        b = a * b_far + b
+        a = a * a_far
+        k *= 2
+    return a, b
+
+
+def coefficient_parts(rate_pre, inlet_pre, decay):
+    rate = sigmoid(rate_pre)
+    inlet = sigmoid(inlet_pre)
+    sp = softplus_exact(decay)
+    log_decay = -8.0 * rate * sp
+    factor = jnp.exp(log_decay)
+    scale = jnp.sqrt(minus_expm1(2.0 * log_decay))
+    return rate, inlet, sp, log_decay, factor, scale
+
+
+def opening_rows(docs, init):
+    total = docs.opening[0] * init[0:1]
+    for e in range(1, len(docs.opening)):
+        total = total + docs.opening[e] * init[e : e + 1]
+    return total
+
+
+RIM = 16
+
+
+def recur_kernel(
+    sizes, stream_ref, mix_gain_ref, gelu_w, recur_w, taps_ref, bias_ref, rate_w, rate_b, inlet_w, inlet_b,
+    decay_ref, init_ref, out_w, ffn_gain_ref, lengths_ref, counts_ref,
+    low_ref, middle_ref, mix_ref, gelu_ref, recur_ref, conv_ref, ratep_ref, inletp_ref, state_ref, enter_ref,
+    product_ref, finals_ref,
+    cum, loc, summary, part, mid, ylow, yfar, send_sems, recv_sems,
+):
+    n_seq, n_ch, rows, slots, bw = sizes
+    count = rows * n_ch
+    net = Net(n_seq, n_ch, rows, send_sems, recv_sems)
+    s, c = net.s, net.c
+    nxt = [(net.s_to[1], i) for i in range(n_ch)]
+    net.meet(net.seq_peers() + [net.sibling, net.across] + [(net.s_to[k], (c + i) % n_ch) for k in (1, n_seq - 1) for i in range(1, n_ch)])
+    values = stream_ref[...].astype(jnp.float32)
+    scale = lax.rsqrt(jnp.mean(values * values, axis=-1, keepdims=True) + EPS)
+    own = (values * scale * mix_gain_ref[...][None, :]).astype(jnp.bfloat16)
+    mix_ref[pl.ds(pl.multiple_of(RIM + c * rows, 16), rows), :] = own
+
+    def rows_of(cc):
+        return mix_ref.at[pl.ds(pl.multiple_of(RIM + cc * rows, 16), rows)]
+
+    last = mix_ref.at[pl.ds(count, RIM)]
+    first = mix_ref.at[pl.ds(0, RIM)]
+    rim_sends = [net.copy(last, first, ("rim", i), nxt[i]) for i in range(n_ch)]
+    net.ch_gather_start(rows_of, "mix")
+
+    @pl.when((c == n_ch - 1) & (s < n_seq - 1))
+    def _():
+        for copy in rim_sends:
+            copy.start()
+
+    @pl.when(s == 0)
+    def _():
+        mix_ref[pl.ds(0, RIM), :] = jnp.zeros((RIM, mix_ref.shape[1]), jnp.bfloat16)
+
+    net.ch_gather_finish(rows_of, "mix")
+
+    for i in range(n_ch):
+        @pl.when((s > 0) & (c == i))
+        def _(i=i):
+            net.recv(first, ("rim", i))
+
+    docs = Docs(lengths_ref, s * count, count)
+    keep = docs.keep
+    summary_cum, summary_loc = [], []
+    for b in range(slots):
+        cols = pl.ds(b * bw, bw)
+        wide = mix_ref[...]
+        gelu_ref[:, cols] = jnp.dot(wide[RIM:], gelu_w[:, cols], preferred_element_type=jnp.float32)
+        recur = jnp.dot(wide, recur_w[:, cols], preferred_element_type=jnp.float32).astype(jnp.bfloat16)
+        recur_ref[:, cols] = recur
+        recur = recur.astype(jnp.float32)
+        conv_pre = bias_ref[b : b + 1, :]
+        for k in range(taps_ref.shape[0]):
+            conv_pre = conv_pre + taps_ref[k, b : b + 1, :] * recur[RIM - k : RIM - k + count] * docs.valid(k)
+        conv_low = conv_pre.astype(jnp.bfloat16)
+        conv_ref[:, cols] = conv_low
+        rate_pre = jnp.dot(conv_low, rate_w[b], preferred_element_type=jnp.float32) + rate_b[b : b + 1, :]
+        inlet_pre = jnp.dot(conv_low, inlet_w[b], preferred_element_type=jnp.float32) + inlet_b[b : b + 1, :]
+        ratep_ref[:, cols] = rate_pre
+        inletp_ref[:, cols] = inlet_pre
+        rate, inlet, sp, log_decay, factor, scale = coefficient_parts(rate_pre, inlet_pre, decay_ref[b : b + 1, :])
+        carry = keep * factor
+        source = scale * inlet * conv_low.astype(jnp.float32) + (1.0 - keep) * factor * opening_rows(docs, init_ref[:, cols])
+        total, local = prefix(carry, source, count)
+        cum[:, cols] = total
+        loc[:, cols] = local
+        summary_cum.append(total[count - 1 : count])
+        summary_loc.append(local[count - 1 : count])
+    fill = [jnp.zeros((8 - 2 * slots, bw), jnp.float32)]
+    summary[s] = stack_rows(summary_cum + summary_loc + fill)
+    for k in range(1, n_seq):
+        net.send(summary.at[s], summary.at[s], ("sum", k), (net.s_to[k], c))
+    for k in range(1, n_seq):
+        net.recv(summary.at[net.s_from[k]], ("sum", k))
+    enter = jnp.zeros((slots, bw), jnp.float32)
+    for q in range(n_seq - 1):
+        after = summary[q, 0:slots] * enter + summary[q, slots : 2 * slots]
+        enter = jnp.where(s > q, after, enter)
+    enter_ref[0:slots, :] = enter
+    for b in range(slots):
+        cols = pl.ds(b * bw, bw)
+        live = jnp.where(counts_ref[0] > b, 1.0, 0.0)
+        state = loc[:, cols] + cum[:, cols] * enter[b : b + 1]
+        state_ref[:, cols] = state
+        value, _ = smooth_pair(gelu_ref[:, cols])
+        product_ref[:, cols] = (value * state * live).astype(jnp.bfloat16)
+        ends = [jnp.sum(mark * state, axis=0, keepdims=True) * live for mark in docs.closing]
+        finals_ref[:, cols] = stack_rows(ends + [jnp.zeros((8 - len(ends), bw), jnp.float32)])
+
+    def tile(i, _):
+        cols = pl.ds(pl.multiple_of(i * 256, 256), 256)
+        value = jnp.dot(product_ref[...], out_w[:, cols], preferred_element_type=jnp.float32)
+        for cc in range(n_ch):
+            part[cc % 2, cc // 2, :, cols] = value[cc * rows : (cc + 1) * rows]
+        return 0
+
+    lax.fori_loop(0, out_w.shape[1] // 256, tile, 0)
+    branch = net.ch_sum(part, mid, ylow, yfar, "branch")
+    middle = values + branch
+    middle_ref[...] = middle
+    scale = lax.rsqrt(jnp.mean(middle * middle, axis=-1, keepdims=True) + EPS)
+    low_ref[...] = (middle * scale * ffn_gain_ref[...][None, :]).astype(jnp.bfloat16)
+
+    @pl.when((c == n_ch - 1) & (s < n_seq - 1))
+    def _():
+        for copy in rim_sends:
+            copy.wait_send()
+
+    net.drain()
+
+
+def recur_forward(stream, mix_gain, gelu_w, recur_w, taps, bias, rate_w, rate_b, inlet_w, inlet_b, decay, init, out_w, ffn_gain, lengths, counts):
+    n_seq, n_ch = lax.axis_size("seq"), lax.axis_size("ch")
+    rows, d = stream.shape
+    slots, bw = bias.shape
+    count, wide = rows * n_ch, slots * bw
+    bf, f32 = jnp.bfloat16, jnp.float32
+    dma = pltpu.SemaphoreType.DMA
+    vmem = pl.BlockSpec(memory_space=pltpu.VMEM)
+    smem = pl.BlockSpec(memory_space=pltpu.SMEM)
+    shape = jax.ShapeDtypeStruct
+    return pl.pallas_call(
+        functools.partial(recur_kernel, (n_seq, n_ch, rows, slots, bw)),
+        out_shape=[
+            shape((rows, d), bf), shape((rows, d), f32), shape((RIM + count, d), bf), shape((count, wide), f32),
+            shape((RIM + count, wide), bf), shape((count, wide), bf), shape((count, wide), f32), shape((count, wide), f32),
+            shape((count, wide), f32), shape((8, bw), f32), shape((count, wide), bf), shape((8, wide), f32),
+        ],
+        in_specs=[vmem] * 14 + [smem] * 2,
+        out_specs=[vmem] * 12,
+        scratch_shapes=[
+            pltpu.VMEM((count, wide), f32), pltpu.VMEM((count, wide), f32), pltpu.VMEM((n_seq, 8, bw), f32),
+            pltpu.VMEM((2, 2, rows, d), f32), pltpu.VMEM((2, rows, d), f32),
+            pltpu.VMEM((rows, d), bf), pltpu.VMEM((rows, d), bf),
+            dma((32,)), dma((32,)),
+        ],
+        compiler_params=pltpu.CompilerParams(
+            collective_id=2, has_side_effects=True, vmem_limit_bytes=VMEM_BYTES
+        ),
+    )(stream, mix_gain, gelu_w, recur_w, taps, bias, rate_w, rate_b, inlet_w, inlet_b, decay, init, out_w, ffn_gain, lengths, counts)
 
 
 def ffn_kernel(
@@ -588,6 +914,304 @@
     )(low, cot, weights)
 
 
+def pack_gain(row):
+    tiles = [row[:, i * 128 : (i + 1) * 128] for i in range(row.shape[1] // 128)]
+    return jnp.concatenate([stack_rows(tiles[i : i + 8]) for i in range(0, len(tiles), 8)], axis=1)
+
+
+def norm_back(values, gain, grad):
+    r = lax.rsqrt(jnp.mean(values * values, axis=-1, keepdims=True) + EPS)
+    u = grad * gain
+    to_values = r * u - values * (r * r * r) * jnp.mean(u * values, axis=-1, keepdims=True)
+    to_gain = jnp.sum(grad * values * r, axis=0, keepdims=True)
+    return to_values, to_gain
+
+
+def recur_back_kernel(
+    sizes, nfg_ref, middle_ref, cot_ref, stream_ref, mix_gain_ref, ffn_gain_ref, gelu_w, recur_w, out_w,
+    taps_ref, rate_w, inlet_w, decay_ref, init_ref, mix_ref, gelu_ref, recur_ref, conv_ref, ratep_ref, inletp_ref,
+    state_ref, enter_ref, product_ref, finals_ref, lengths_ref, counts_ref,
+    sgrad_ref, gelu_wg, recur_wg, out_wg, rate_wg, inlet_wg, taps_g, bias_g, rate_bg, inlet_bg, decay_g,
+    finals_out, mixg_out, ffng_out,
+    branch, back_a, back_b, summary, cgrad, part, mid, ylow, yfar, gathered, left, early, late, gates, gates_in, shared,
+    send_sems, recv_sems,
+):
+    n_seq, n_ch, rows, slots, bw, width = sizes
+    count = rows * n_ch
+    wide = slots * bw
+    net = Net(n_seq, n_ch, rows, send_sems, recv_sems)
+    s, c, z, x, y, core = net.s, net.c, net.z, net.x, net.y, net.core
+    net.meet(net.seq_peers() + [net.sibling, net.across])
+    own_s = pl.multiple_of(s * count, count)
+
+    def gather_z(a):
+        view = gathered.at[a, pl.ds(own_s, count)]
+        for k in range(1, net.n_z):
+            net.send(view, view, ("gz", a, k), net.dev(net.z_to[k], x, y, core))
+
+    def gather_x_view(a, k, xx):
+        return gathered.at[a, pl.ds(pl.multiple_of((net.z_from[k] * 2 + xx) * count, count), count)]
+
+    def gather_x(a, k):
+        view = gather_x_view(a, k, x)
+        if k:
+            net.recv(view, ("gz", a, k))
+        net.send(view, view, ("gx", a, k), net.dev(z, 1 - x, y, core))
+
+    def gather_done(a):
+        for k in range(net.n_z):
+            net.recv(gather_x_view(a, k, 1 - x), ("gx", a, k))
+
+    def left_start(a, src):
+        for k in range(1, n_seq):
+            net.send(
+                src(pl.ds(pl.multiple_of(net.s_to[k] * width, width), width)), left.at[a, s, c], ("left", a, k),
+                (net.s_to[k], c),
+            )
+
+    def left_pass(a):
+        for k in range(1, n_seq):
+            net.recv(left.at[a, net.s_from[k], c], ("left", a, k))
+        net.ch_gather_start(lambda cc: left.at[a, :, cc], ("leftch", a))
+
+    def left_done(a):
+        net.ch_gather_finish(lambda cc: left.at[a, :, cc], ("leftch", a))
+
+    nfg = nfg_ref[...]
+    middle = middle_ref[...]
+    to_middle, ffn_part = norm_back(middle, ffn_gain_ref[...][None, :], nfg)
+    middle_grad = cot_ref[...].astype(jnp.float32) + to_middle
+    branch[c] = middle_grad.astype(jnp.bfloat16)
+    net.ch_gather_start(lambda cc: branch.at[cc], "branch")
+    own_cols = pl.ds(pl.multiple_of(s * width, width), width)
+    mix_rows = pl.ds(pl.multiple_of(RIM + c * rows, 16), rows)
+    left[0, s, c] = mix_ref[mix_rows, own_cols]
+    left[1, s, c] = branch[c, :, own_cols]
+    left_start(1, lambda cols: branch.at[c, :, cols])
+    left_start(0, lambda cols: mix_ref.at[mix_rows, cols])
+    gathered[0, pl.ds(own_s, count), :] = product_ref[...]
+    gather_z(0)
+    early[s] = jnp.concatenate([finals_ref[...], pack_gain(ffn_part)], axis=1)
+    net.ch_gather_finish(lambda cc: branch.at[cc], "branch")
+
+    docs = Docs(lengths_ref, s * count, count)
+    keep = docs.keep
+    ahead_docs = Docs(lengths_ref, s * count, count + RIM)
+    one = jnp.ones((1, bw), jnp.float32)
+    row = lax.broadcasted_iota(jnp.int32, (count, bw), 0)
+    enter = enter_ref[...]
+    first_carry, heads_a, heads_b = [], [], []
+    for b in range(slots):
+        cols = pl.ds(b * bw, bw)
+        live = jnp.where(counts_ref[0] > b, 1.0, 0.0)
+        product_grad = contract_last(branch[...].reshape(count, branch.shape[2]), out_w[b * bw : (b + 1) * bw, :])
+        value, slope = smooth_pair(gelu_ref[:, cols])
+        state = state_ref[:, cols]
+        gathered[1, pl.ds(own_s, count), cols] = (product_grad * state * live * slope).astype(jnp.bfloat16)
+        state_grad = product_grad * value * live
+        rate, inlet, sp, log_decay, factor, scale = coefficient_parts(ratep_ref[:, cols], inletp_ref[:, cols], decay_ref[b : b + 1, :])
+        carry = keep * factor
+        following = jnp.where(row < count - 1, pltpu.roll(carry, count - 1, 0), 1.0)
+        total, local = suffix(following, state_grad, count)
+        back_a[:, cols] = total
+        back_b[:, cols] = local
+        heads_a.append(carry[0:1] * total[0:1])
+        heads_b.append(carry[0:1] * local[0:1])
+    summary[s] = stack_rows(heads_a + heads_b + [jnp.zeros((8 - 2 * slots, bw), jnp.float32)])
+    for k in range(1, n_seq):
+        net.send(summary.at[s], summary.at[s], ("sum", k), (net.s_to[k], c))
+    for k in range(1, n_seq):
+        net.recv(summary.at[net.s_from[k]], ("sum", k))
+    enter_back = jnp.zeros((slots, bw), jnp.float32)
+    for q in range(n_seq - 1, 0, -1):
+        after = summary[q, 0:slots] * enter_back + summary[q, slots : 2 * slots]
+        enter_back = jnp.where(s < q, after, enter_back)
+    vec = []
+    for b in range(slots):
+        cols = pl.ds(b * bw, bw)
+        adjoint = back_b[:, cols] + back_a[:, cols] * enter_back[b : b + 1]
+        state = state_ref[:, cols]
+        previous = jnp.where(row > 0, pltpu.roll(state, 1, 0), enter[b : b + 1])
+        decay = decay_ref[b : b + 1, :]
+        rate, inlet, sp, log_decay, factor, scale = coefficient_parts(ratep_ref[:, cols], inletp_ref[:, cols], decay)
+        conv_low = conv_ref[:, cols]
+        conv = conv_low.astype(jnp.float32)
+        init_rows = opening_rows(docs, init_ref[:, cols])
+        log_grad = adjoint * (
+            factor * (keep * previous + (1.0 - keep) * init_rows) - inlet * conv * jnp.exp(2.0 * log_decay) / scale
+        )
+        rate_low = (log_grad * (-8.0 * sp) * rate * (1.0 - rate)).astype(jnp.bfloat16)
+        direct = adjoint * scale
+        inlet_low = (direct * conv * inlet * (1.0 - inlet)).astype(jnp.bfloat16)
+        decay_row = jnp.sum(log_grad * (-8.0 * rate), axis=0, keepdims=True) * sigmoid(decay)
+        back = direct * inlet + contract_last(rate_low, rate_w[b]) + contract_last(inlet_low, inlet_w[b])
+        cgrad[0:count, cols] = back.astype(jnp.bfloat16)
+        gates[0, b] = contract_first(conv_low, rate_low).astype(jnp.bfloat16)
+        gates[1, b] = contract_first(conv_low, inlet_low).astype(jnp.bfloat16)
+        vec.append([
+            jnp.sum(rate_low.astype(jnp.float32), axis=0, keepdims=True),
+            jnp.sum(inlet_low.astype(jnp.float32), axis=0, keepdims=True),
+            decay_row,
+        ])
+    rim = cgrad.at[pl.ds(count, RIM)]
+    rim_send = net.copy(cgrad.at[pl.ds(0, RIM)], rim, "rim", (net.s_to[n_seq - 1], c))
+
+    @pl.when(s > 0)
+    def _():
+        rim_send.start()
+
+    @pl.when(s == n_seq - 1)
+    def _():
+        cgrad[pl.ds(count, RIM), :] = jnp.zeros((RIM, wide), jnp.bfloat16)
+
+    @pl.when(s < n_seq - 1)
+    def _():
+        net.recv(rim, "rim")
+
+    gather_z(1)
+    for k in range(net.n_z):
+        gather_x(0, k)
+    vectors = []
+    for b in range(slots):
+        cols = pl.ds(b * bw, bw)
+        grad = cgrad[:, cols].astype(jnp.float32)
+        own = grad[:count]
+        recur = recur_ref[:, cols].astype(jnp.float32)
+        total = jnp.zeros((count, bw), jnp.float32)
+        tap_rows = []
+        for k in range(taps_ref.shape[0]):
+            tap_rows.append(jnp.sum(own * recur[RIM - k : RIM - k + count] * docs.valid(k), axis=0, keepdims=True))
+            total = total + taps_ref[k, b : b + 1, :] * grad[k : k + count] * ahead_docs.valid(k)[k : k + count]
+        gathered[2, pl.ds(own_s, count), cols] = total.astype(jnp.bfloat16)
+        vectors.append(stack_rows(tap_rows + [jnp.sum(own, axis=0, keepdims=True)] + vec[b]))
+    gather_z(2)
+
+    def tile(i, _):
+        cols = pl.ds(pl.multiple_of(i * 256, 256), 256)
+        own_rows = pl.ds(own_s, count)
+        value = contract_last(gathered[1, own_rows, :], gelu_w[cols, :]) + contract_last(gathered[2, own_rows, :], recur_w[cols, :])
+        for cc in range(n_ch):
+            part[cc % 2, cc // 2, :, cols] = value[cc * rows : (cc + 1) * rows]
+        return 0
+
+    lax.fori_loop(0, gelu_w.shape[0] // 256, tile, 0)
+    gate_rows = rate_wg.shape[1]
+    for k in range(1, n_seq):
+        net.send(
+            gates.at[:, :, pl.ds(pl.multiple_of(net.s_to[k] * gate_rows, gate_rows), gate_rows), :], gates_in.at[s],
+            ("gates", k), (net.s_to[k], c),
+        )
+    gates_in[s] = gates[:, :, pl.ds(pl.multiple_of(s * gate_rows, gate_rows), gate_rows), :]
+    for k in range(1, n_seq):
+        net.send(early.at[s], early.at[s], ("early", k), (net.s_to[k], c))
+    norm_grad = net.ch_sum(part, mid, ylow, yfar, "norm")
+    to_stream, mix_part = norm_back(stream_ref[...].astype(jnp.float32), mix_gain_ref[...][None, :], norm_grad)
+    sgrad_ref[...] = middle_grad + to_stream
+    late[s] = jnp.concatenate(vectors + [pack_gain(mix_part)], axis=1)
+    for k in range(1, n_seq):
+        net.send(late.at[s], late.at[s], ("late", k), (net.s_to[k], c))
+    for a in (0, 1):
+        left_pass(a)
+    for a in (0, 1):
+        left_done(a)
+    for k in range(net.n_z):
+        gather_x(1, k)
+    gather_done(0)
+
+    def left_of(a):
+        return left[a].reshape(n_seq * n_ch * rows, width)
+
+    out_wg[...] = contract_first(gathered[0], left_of(1))
+    for k in range(net.n_z):
+        gather_x(2, k)
+    gather_done(1)
+    gelu_wg[...] = contract_first(left_of(0), gathered[1])
+    for k in range(1, n_seq):
+        net.recv(gates_in.at[net.s_from[k]], ("gates", k))
+        net.recv(early.at[net.s_from[k]], ("early", k))
+        net.recv(late.at[net.s_from[k]], ("late", k))
+    total = gates_in[0].astype(jnp.float32)
+    early_sum, late_sum = early[0], late[0]
+    for q in range(1, n_seq):
+        total = total + gates_in[q].astype(jnp.float32)
+        early_sum = early_sum + early[q]
+        late_sum = late_sum + late[q]
+    rate_wg[...] = total[0]
+    inlet_wg[...] = total[1]
+    shared[c] = jnp.concatenate([early_sum, late_sum[:, wide:]], axis=1)
+    net.ch_gather_start(lambda cc: shared.at[cc], "shared")
+    piece = bw // n_seq
+    for b in range(slots):
+        mine = jnp.zeros((8, piece), jnp.float32)
+        for q in range(n_seq):
+            at = b * bw + q * piece
+            mine = jnp.where(s == q, late_sum[:, at : at + piece], mine)
+        n_taps = taps_ref.shape[0]
+        for k in range(n_taps):
+            taps_g[k, b : b + 1, :] = mine[k : k + 1]
+        for k, ref in enumerate((bias_g, rate_bg, inlet_bg, decay_g)):
+            ref[b : b + 1, :] = mine[n_taps + k : n_taps + k + 1]
+    net.ch_gather_finish(lambda cc: shared.at[cc], "shared")
+    gains = shared[0, :, wide:]
+    for cc in range(1, n_ch):
+        gains = gains + shared[cc, :, wide:]
+    for cc in range(n_ch):
+        finals_out[:, cc * wide : (cc + 1) * wide] = shared[cc, 0 : finals_out.shape[0], 0:wide]
+    half = gains.shape[1] // 2
+    for ref, at in ((ffng_out, 0), (mixg_out, half)):
+        for i in range(half // 128):
+            ref[i * 8 : (i + 1) * 8, :] = gains[:, at + i * 128 : at + (i + 1) * 128]
+    gather_done(2)
+    recur_wg[...] = contract_first(left_of(0), gathered[2])
+
+    @pl.when(s > 0)
+    def _():
+        rim_send.wait_send()
+
+    net.drain()
+
+
+def recur_backward(nfg, middle, cot, stream, mix_gain, ffn_gain, gelu_w, recur_w, out_w, taps, rate_w, inlet_w, decay, init,
+                   mix, gelu_pre, recur, conv_low, rate_pre, inlet_pre, state, enter, product, finals, lengths, counts):
+    n_seq, n_ch = lax.axis_size("seq"), lax.axis_size("ch")
+    rows, d = stream.shape
+    slots, bw = decay.shape
+    count, wide, width = rows * n_ch, slots * bw, d // n_seq
+    bf, f32 = jnp.bfloat16, jnp.float32
+    dma = pltpu.SemaphoreType.DMA
+    vmem = pl.BlockSpec(memory_space=pltpu.VMEM)
+    smem = pl.BlockSpec(memory_space=pltpu.SMEM)
+    shape = jax.ShapeDtypeStruct
+    piece = bw // n_seq
+    vector = shape((slots, piece), f32)
+    packed = wide + d // 8
+    return pl.pallas_call(
+        functools.partial(recur_back_kernel, (n_seq, n_ch, rows, slots, bw, width)),
+        out_shape=[
+            shape((rows, d), f32), shape((width, wide), f32), shape((width, wide), f32), shape((wide, width), f32),
+            shape((slots, piece, bw), f32), shape((slots, piece, bw), f32), shape((taps.shape[0], slots, piece), f32),
+            vector, vector, vector, vector,
+            shape((lengths.shape[0], wide * n_ch), f32), shape((d // 128, 128), f32), shape((d // 128, 128), f32),
+        ],
+        in_specs=[vmem] * 24 + [smem] * 2,
+        out_specs=[vmem] * 14,
+        scratch_shapes=[
+            pltpu.VMEM((n_ch, rows, d), bf), pltpu.VMEM((count, wide), f32), pltpu.VMEM((count, wide), f32),
+            pltpu.VMEM((n_seq, 8, bw), f32), pltpu.VMEM((count + RIM, wide), bf),
+            pltpu.VMEM((2, 2, rows, d), f32), pltpu.VMEM((2, rows, d), f32), pltpu.VMEM((rows, d), bf), pltpu.VMEM((rows, d), bf),
+            pltpu.VMEM((3, n_seq * count, wide), bf), pltpu.VMEM((2, n_seq, n_ch, rows, width), bf),
+            pltpu.VMEM((n_seq, 8, packed), f32), pltpu.VMEM((n_seq, 8, packed), f32),
+            pltpu.VMEM((2, slots, bw, bw), bf), pltpu.VMEM((n_seq, 2, slots, piece, bw), bf),
+            pltpu.VMEM((n_ch, 8, packed + d // 8), f32),
+            dma((96,)), dma((96,)),
+        ],
+        compiler_params=pltpu.CompilerParams(
+            collective_id=3, has_side_effects=True, vmem_limit_bytes=VMEM_BYTES
+        ),
+    )(nfg, middle, cot, stream, mix_gain, ffn_gain, gelu_w, recur_w, out_w, taps, rate_w, inlet_w, decay, init,
+      mix, gelu_pre, recur, conv_low, rate_pre, inlet_pre, state, enter, product, finals, lengths, counts)
+
+
 def small_body(
     stream,
     cotangent,
@@ -610,197 +1234,23 @@
     doc_lengths,
     block_counts,
 ):
-    slot_count = rate_weight.shape[0]
-    block_width = rate_weight.shape[1]
-    local_width = slot_count * block_width
-    taps = conv_taps.shape[0]
-    token_count = stream.shape[0] * lax.axis_size("ch")
-    hidden_width = gate_weight.shape[1]
-    base = lax.axis_index("seq") * token_count
-    offset_all, opening, closing = doc_view(doc_lengths, base, token_count + taps - 1)
-    offset = offset_all[:token_count]
-    opening = opening[:token_count]
-    closing = closing[:token_count]
-    keep = (offset > 0).astype(jnp.float32)[:, None]
-    slot_live = (jnp.arange(slot_count, dtype=jnp.int32) < block_counts[0]).astype(jnp.float32)
-    live = jnp.repeat(slot_live, block_width)[None, :]
-    taps_flat = conv_taps.reshape(taps, local_width)
-    decay_flat = decay_param.reshape(1, local_width)
-    stream_float = stream.astype(jnp.float32)
-    mix_low = normalize(stream_float, mix_gain).astype(jnp.bfloat16)
-    mix_full = spread(mix_low)
-    gelu_pre = jnp.dot(mix_full, gelu_weight, preferred_element_type=jnp.float32)
-    recur_low = jnp.dot(mix_full, recur_weight, preferred_element_type=jnp.float32).astype(
-        jnp.bfloat16
-    )
-    rim = passed_along(recur_low[token_count - taps + 1 :], "seq", 1)
-    extended = jnp.concatenate([rim, recur_low], axis=0).astype(jnp.float32)
-    conv_pre = conv_bias.reshape(1, local_width)
-    for tap_index in range(taps):
-        valid = (offset >= tap_index).astype(jnp.float32)[:, None]
-        lead = taps - 1 - tap_index
-        conv_pre = (
-            conv_pre + taps_flat[tap_index][None, :] * extended[lead : lead + token_count] * valid
-        )
-    conv_low = conv_pre.astype(jnp.bfloat16)
-    conv_value = conv_low.astype(jnp.float32)
-    grouped = conv_low.reshape(token_count, slot_count, block_width)
-    rate_pre = (
-        jnp.einsum("rsi,sio->rso", grouped, rate_weight, preferred_element_type=jnp.float32)
-        + rate_bias[None]
-    ).reshape(token_count, local_width)
-    inlet_pre = (
-        jnp.einsum("rsi,sio->rso", grouped, inlet_weight, preferred_element_type=jnp.float32)
-        + inlet_bias[None]
-    ).reshape(token_count, local_width)
-    init_rows = jnp.dot(opening, init_states, precision=HIGH)
-    carry_factor, source = coefficients(
-        rate_pre, inlet_pre, conv_value, decay_flat, init_rows, keep
-    )
-    cumulative, local_state = lax.associative_scan(affine, (carry_factor, source), axis=0)
-    summary = (cumulative[-1], local_state[-1])
-    entering = entering_2(
-        summary, "seq", affine, (jnp.ones_like(summary[0]), jnp.zeros_like(summary[1])), False
-    )
-    state_in = entering[1]
-    state = local_state + cumulative * state_in[None, :]
-    gelu_value = smooth(gelu_pre)
-    product_low = (gelu_value * state * live).astype(jnp.bfloat16)
-    branch = collect(jnp.dot(product_low, out_weight, preferred_element_type=jnp.float32))
-    middle = stream_float + branch
-    ffn_low = normalize(middle, ffn_gain).astype(jnp.bfloat16)
+    (ffn_low, middle, mix_wide, gelu_pre, recur_wide, conv_low, rate_pre, inlet_pre, state, enter, product_low, finals) = recur_forward(
+        stream, mix_gain, gelu_weight, recur_weight, conv_taps, conv_bias, rate_weight, rate_bias, inlet_weight,
+        inlet_bias, decay_param, init_states, out_weight, ffn_gain, doc_lengths, block_counts,
+    )
     weights = jnp.stack([gate_weight.T, up_weight.T, down_weight])
     ffn_sum, norm_ffn_grad, dw = ffn(ffn_low, cotangent, weights)
     mixed_out = (middle + ffn_sum).astype(jnp.bfloat16)
-    unused, ffn_norm_pull = jax.vjp(normalize, middle, ffn_gain)
-    middle_norm_grad, ffn_gain_part = ffn_norm_pull(norm_ffn_grad)
-    middle_grad = cotangent.astype(jnp.float32) + middle_norm_grad
-    branch_full = spread(middle_grad.astype(jnp.bfloat16))
-    out_weight_grad = contract_first(product_low, branch_full)
-    product_grad = contract_last(branch_full, out_weight)
-    state_grad = product_grad * gelu_value * live
-    unused, gelu_pull = jax.vjp(smooth, gelu_pre)
-    gelu_low = gelu_pull(product_grad * state * live)[0].astype(jnp.bfloat16)
-    following = jnp.concatenate([carry_factor[1:], jnp.ones_like(carry_factor[:1])], axis=0)
-    cum_back, adjoint_local = lax.associative_scan(
-        affine, (jnp.flip(following, 0), jnp.flip(state_grad, 0)), axis=0
-    )
-    cum_back = jnp.flip(cum_back, 0)
-    adjoint_local = jnp.flip(adjoint_local, 0)
-    summary_back = (carry_factor[0] * cum_back[0], carry_factor[0] * adjoint_local[0])
-    arriving = entering_2(
-        summary_back,
-        "seq",
-        affine,
-        (jnp.ones_like(summary_back[0]), jnp.zeros_like(summary_back[1])),
-        True,
-    )
-    adjoint_in = arriving[1]
-    adjoint = adjoint_local + cum_back * adjoint_in[None, :]
-    previous_state = jnp.concatenate([state_in[None, :], state[:-1]], axis=0)
-
-    def local_coefficients(rate_value, inlet_value, conv_part, decay_value):
-        return coefficients(rate_value, inlet_value, conv_part, decay_value, init_rows, keep)
-
-    unused, coefficient_pull = jax.vjp(
-        local_coefficients, rate_pre, inlet_pre, conv_value, decay_flat
-    )
-    rate_grad, inlet_grad, conv_direct, decay_part = coefficient_pull(
-        (adjoint * previous_state, adjoint)
-    )
-    rate_low = rate_grad.astype(jnp.bfloat16).reshape(token_count, slot_count, block_width)
-    inlet_low = inlet_grad.astype(jnp.bfloat16).reshape(token_count, slot_count, block_width)
-    rate_weight_grad = jnp.einsum(
-        "rsi,rso->sio", grouped, rate_low, preferred_element_type=jnp.float32
-    )
-    inlet_weight_grad = jnp.einsum(
-        "rsi,rso->sio", grouped, inlet_low, preferred_element_type=jnp.float32
-    )
-    rate_bias_grad = jnp.sum(rate_low.astype(jnp.float32), axis=0)
-    inlet_bias_grad = jnp.sum(inlet_low.astype(jnp.float32), axis=0)
-    conv_back = jnp.einsum(
-        "rso,sio->rsi", rate_low, rate_weight, preferred_element_type=jnp.float32
-    )
-    conv_back = conv_back + jnp.einsum(
-        "rso,sio->rsi", inlet_low, inlet_weight, preferred_element_type=jnp.float32
-    )
-    conv_low_grad = (conv_direct + conv_back.reshape(token_count, local_width)).astype(jnp.bfloat16)
-    rim_back = passed_along(conv_low_grad[: taps - 1], "seq", -1)
-    ahead = jnp.concatenate([conv_low_grad, rim_back], axis=0).astype(jnp.float32)
-    own_grad = ahead[:token_count]
-    recur_grad = jnp.zeros((token_count, local_width), jnp.float32)
-    tap_grads = []
-    for tap_index in range(taps):
-        lead = taps - 1 - tap_index
-        valid_here = (offset >= tap_index).astype(jnp.float32)[:, None]
-        tap_grads.append(
-            jnp.sum(own_grad * extended[lead : lead + token_count] * valid_here, axis=0)
-        )
-        valid_ahead = (offset_all[tap_index : tap_index + token_count] >= tap_index).astype(
-            jnp.float32
-        )[:, None]
-        recur_grad = (
-            recur_grad
-            + taps_flat[tap_index][None, :]
-            * ahead[tap_index : tap_index + token_count]
-            * valid_ahead
-        )
-    conv_taps_grad = jnp.stack(tap_grads, axis=0).reshape(taps, slot_count, block_width)
-    conv_bias_grad = jnp.sum(own_grad, axis=0).reshape(slot_count, block_width)
-    recur_low_grad = recur_grad.astype(jnp.bfloat16)
-    gelu_weight_grad = contract_first(mix_full, gelu_low)
-    recur_weight_grad = contract_first(mix_full, recur_low_grad)
-    norm_mix_part = contract_last(gelu_low, gelu_weight) + contract_last(
-        recur_low_grad, recur_weight
-    )
-    norm_mix_grad = collect(norm_mix_part)
-    unused, mix_norm_pull = jax.vjp(normalize, stream_float, mix_gain)
-    stream_norm_grad, mix_gain_part = mix_norm_pull(norm_mix_grad)
-    stream_grad = middle_grad + stream_norm_grad
-    finals_local = lax.dot_general(closing, state * live, (((0,), (0,)), ((), ())), precision=HIGH)
-    finals_wide = jnp.zeros((finals_local.shape[0], local_width * lax.axis_size("ch")), jnp.float32)
-    finals_wide = lax.dynamic_update_slice(
-        finals_wide, finals_local, (jnp.int32(0), lax.axis_index("ch") * local_width)
-    )
-    final_states, mix_gain_grad, ffn_gain_grad = lax.psum(
-        (finals_wide, mix_gain_part, ffn_gain_part), ("seq", "ch")
-    )
-    summed = (
-        lax.psum_scatter(gelu_weight_grad, "seq", scatter_dimension=0, tiled=True),
-        lax.psum_scatter(recur_weight_grad, "seq", scatter_dimension=0, tiled=True),
-        lax.psum_scatter(conv_taps_grad, "seq", scatter_dimension=2, tiled=True),
-        lax.psum_scatter(conv_bias_grad, "seq", scatter_dimension=1, tiled=True),
-        lax.psum_scatter(rate_weight_grad, "seq", scatter_dimension=1, tiled=True),
-        lax.psum_scatter(rate_bias_grad, "seq", scatter_dimension=1, tiled=True),
-        lax.psum_scatter(inlet_weight_grad, "seq", scatter_dimension=1, tiled=True),
-        lax.psum_scatter(inlet_bias_grad, "seq", scatter_dimension=1, tiled=True),
-        lax.psum_scatter(
-            decay_part.reshape(slot_count, block_width), "seq", scatter_dimension=1, tiled=True
-        ),
-        lax.psum_scatter(out_weight_grad, "seq", scatter_dimension=1, tiled=True),
-        dw[0].T.astype(jnp.float32),
-        dw[1].T.astype(jnp.float32),
-        dw[2].astype(jnp.float32),
+    (stream_grad, gelu_wg, recur_wg, out_wg, rate_wg, inlet_wg, taps_g, bias_g, rate_bg, inlet_bg, decay_g, final_states,
+     mix_gain_grad, ffn_gain_grad) = recur_backward(
+        norm_ffn_grad, middle, cotangent, stream, mix_gain, ffn_gain, gelu_weight, recur_weight, out_weight, conv_taps,
+        rate_weight, inlet_weight, decay_param, init_states, mix_wide, gelu_pre, recur_wide, conv_low, rate_pre, inlet_pre,
+        state, enter, product_low, finals, doc_lengths, block_counts,
     )
     return (
-        final_states,
-        mixed_out,
-        stream_grad,
-        mix_gain_grad,
-        summed[0],
-        summed[1],
-        summed[2],
-        summed[3],
-        summed[4],
-        summed[5],
-        summed[6],
-        summed[7],
-        summed[8],
-        summed[9],
-        ffn_gain_grad,
-        summed[10],
-        summed[11],
-        summed[12],
+        final_states, mixed_out, stream_grad, mix_gain_grad.reshape(-1), gelu_wg, recur_wg, taps_g, bias_g, rate_wg, rate_bg,
+        inlet_wg, inlet_bg, decay_g, out_wg, ffn_gain_grad.reshape(-1), dw[0].T.astype(jnp.float32),
+        dw[1].T.astype(jnp.float32), dw[2].astype(jnp.float32),
     )
 
 

time: 1770 us -> 352 us (0.20)
  waiting for transfers between devices: 924 us -> 0 us
  local copies, waits for them, and re-layouts: 318 us -> 17.5 us
  Pallas kernels: 175 us -> 327 us
  blocking collectives: 147 us -> 0 us
  other arithmetic: 130 us -> 3.89 us
  matrix products: 38.6 us -> 0 us
    reduce_scatter x7 -> x0, waiting for transfers between devices: 507 us -> none  [the longest x1 123 us: small_body(): lax.psum_scatter(gelu_weight_grad, 'seq', scatter_dimension=0, tiled=True)]
    unnamed x18 -> x0, waiting for transfers between devices: 288 us -> none
    pallas_call x0 -> x2, Pallas kernels: none -> 151 us  [the longest x1 117 us: recur_backward(): pl.pallas_call(functools.partial(recur_back_kernel, (n_seq, n_ch, rows, s...]
    all_gather x6 -> x0, blocking collectives: 147 us -> none  [the longest x4 131 us: entering_2(): everything = jax.tree.map(lambda part: lax.all_gather(part, axis), shard)]
    slice x99 -> x0, local copies, waits for them, and re-layouts: 145 us -> none  [the longest x49 82.2 us: small_body(): lax.associative_scan(affine, (jnp.flip(following, 0), jnp.flip(state_grad...]
    psum x1 -> x0, waiting for transfers between devices: 128 us -> none  [small_body(): lax.psum((finals_wide, mix_gain_part, ffn_gain_part), ('seq', 'ch'))]
    pad x48 -> x0, local copies, waits for them, and re-layouts: 98.1 us -> none  [the longest x24 50 us: small_body(): lax.associative_scan(affine, (carry_factor, source), axis=0)]
    add x38 -> x0, other arithmetic: 54.5 us -> none  [the longest x14 19.9 us: small_body(): lax.associative_scan(affine, (jnp.flip(following, 0), jnp.flip(state_grad...]
  transfers between devices with their start and end apart: 15 -> 0, of which waited for: 13 -> 0; matrix products, arithmetic and copies ran while one was open for 4% -> 0% of each run, Pallas kernels for 0% -> 0%
where the time goes in v2:
time: 352 us; the launch traced here: 350 us
  Pallas kernels  327 us (93%)
  local copies, waits for them, and re-layouts  17.5 us (5%)
  other arithmetic  3.89 us (1%)
    pallas_call x1, Pallas kernels, ffn(): pl.pallas_call(functools.partial(ffn_kernel, (n_seq, n_ch, rows, width, s...  177 us
    pallas_call x1, Pallas kernels, recur_backward(): pl.pallas_call(functools.partial(recur_back_kernel, (n_seq, n_ch, rows, s...  117 us
    pallas_call x1, Pallas kernels, recur_forward(): pl.pallas_call(functools.partial(recur_kernel, (n_seq, n_ch, rows, slots,...  33.8 us
    unnamed x53, local copies, waits for them, and re-layouts  17.5 us

profile of v2, /device:TPU:0, one launch (start us, length us, event | category | flops | bytes accessed | tf_op | source)
XLA Modules:
  0.0 350.4 jit_solution(15590450032462905510)
XLA Ops:
  0.7 0.0 copy-start.2
  1.4 1.3 copy.38.taps_ref
  2.7 1.4 copy.39
  4.1 1.4 copy.40
  5.5 0.0 copy-done.2
  5.5 1.7 pad_maximum_fusion.weight_ref
  7.2 33.8 %shard_map.331 = (bf16[32,2048]{1,0:T(8,128)(2,1)}, f32[32,2048]{1,0:T(8,128)}, bf16[144,2048]{1,0:T(8,128)(2,1)}, f32[128,768]{1,0:T(8,128)}, bf16[144,768]{1,0...) custom-call(bf16[32,2048]{1,0:T(8,128)(2,1)} %stream_ref.3, ...), custom_call_target="tpu_custom_call" | custom-call | tf_op jit(solution)/shard_map/pallas_call | solution.py:646
  41.0 176.7 %shard_map.332 = (f32[32,2048]{1,0:T(8,128)}, f32[32,2048]{1,0:T(8,128)}, bf16[3,1536,256]{2,1,0:T(8,128)(2,1)}) custom-call(bf16[32,2048]{1,0:T(8,128)(2,1)} %get-tuple-element.47.low_ref, bf16[32,2048]{1,0:T(8,128)(2,1)} %cot_ref.3, bf16[3,1536,256]{2,1,0:T(8,128)(2,1)} %pad_maximum_fusion.weight_ref), custom_call_target="tpu_custom_call" | custom-call | tf_op jit(solution)/shard_map/pallas_call | solution.py:879
  217.7 0.0 copy-start.1
  217.7 0.0 copy-start.7
  217.7 0.0 copy-start
  217.7 117.0 %shard_map.333 = (f32[32,2048]{1,0:T(8,128)}, f32[256,768]{1,0:T(8,128)}, f32[256,768]{1,0:T(8,128)}, f32[768,256]{1,0:T(8,128)}, f32[3,32,256]{2,1,0:T(8,128)},...) custom-call(f32[32,2048]{1,0:T(8,128)} %get-tuple-element.48.nfg_ref, ...), custom_call_target="tpu_custom_call" | custom-call | tf_op jit(solution)/shard_map/pallas_call | solution.py:1188
  334.7 0.0 copy-done.1
  334.7 0.0 copy-done.7
  334.7 0.7 add_convert_fusion
  335.4 1.3 copy.42
  336.7 0.0 copy-done
  336.7 1.5 bitcast_convert_fusion
  338.3 1.6 copy.44
  339.9 0.0 copy-start.10
  339.9 0.0 copy-start.6
  339.9 0.0 copy-start.12
  339.9 0.0 copy-start.5
  339.9 0.0 copy-start.4
  339.9 1.6 copy.43
  341.5 0.0 copy-done.10
  341.5 0.0 copy-start.16
  341.5 0.0 copy-start.9
  341.5 0.0 copy-start.15
  341.5 0.0 copy-start.8
  341.5 0.0 copy-start.14
  341.5 0.0 copy-start.13
  341.5 0.0 copy-start.3
  341.6 0.6 copy.59
  342.2 0.0 copy-done.6
  342.2 0.7 copy.60
  342.9 0.0 copy-done.12
  342.9 0.6 copy.61
  343.5 0.0 copy-done.5
  343.5 0.0 copy-start.11
  343.5 0.9 copy.62
  344.4 0.0 copy-done.4
  344.4 0.9 copy.63
  345.3 0.0 copy-done.16
  345.3 0.6 copy.64
  345.9 0.0 copy-done.9
  345.9 0.6 copy.65
  346.5 0.0 copy-done.15
  346.5 0.6 copy.66
  347.1 0.0 copy-done.8
  347.1 0.6 copy.67
  347.7 0.0 copy-done.14
  347.7 0.6 copy.68
  348.3 0.0 copy-done.13
  348.3 0.6 copy.69
  348.9 0.0 copy-done.3
  348.9 0.9 copy.70
  349.8 0.0 copy-done.11
  349.8 0.6 copy.71
Async XLA Ops:
  0.7 4.9 %copy-start.2 = (bf16[1536,256]{1,0:T(8,128)(2,1)S(1)}, bf16[1536,256]{1,0:T(8,128)(2,1)}, u32[]{:S(2)}) copy-start(bf16[1536,256]{1,0:T(8,128)(2,1)} %param.37) | copy-start | bytes 2359300
  217.7 117.0 %copy-start.1 = (f32[32,2048]{1,0:T(8,128)S(1)}, f32[32,2048]{1,0:T(8,128)}, u32[]{:S(2)}) copy-start(f32[32,2048]{1,0:T(8,128)} %get-tuple-element.49.middle_ref) | copy-start | bytes 786436
  217.7 117.0 %copy-start.7 = (f32[32,2048]{1,0:T(8,128)S(1)}, f32[32,2048]{1,0:T(8,128)}, u32[]{:S(2)}) copy-start(f32[32,2048]{1,0:T(8,128)} %get-tuple-element.61) | copy-start | bytes 786436
  217.7 119.0 %copy-start = (bf16[3,1536,256]{2,1,0:T(8,128)(2,1)S(1)}, bf16[3,1536,256]{2,1,0:T(8,128)(2,1)}, u32[]{:S(2)}) copy-start(bf16[3,1536,256]{2,1,0:T(8,128)(2,1)} %get-tuple-element.75) | copy-start | bytes 7077892
  339.9 1.6 copy-start.10
  339.9 2.3 copy-start.6
  339.9 3.0 copy-start.12
  339.9 3.6 %copy-start.5 = (f32[256,768]{1,0:T(8,128)S(1)}, f32[256,768]{1,0:T(8,128)}, u32[]{:S(2)}) copy-start(f32[256,768]{1,0:T(8,128)} %get-tuple-element.119) | copy-start | bytes 2359300
  339.9 4.5 %copy-start.4 = (f32[256,768]{1,0:T(8,128)S(1)}, f32[256,768]{1,0:T(8,128)}, u32[]{:S(2)}) copy-start(f32[256,768]{1,0:T(8,128)} %get-tuple-element.120) | copy-start | bytes 2359300
  341.5 3.8 %copy-start.16 = (f32[3,32]{1,0:T(4,128)S(1)}, f32[3,32]{1,0:T(4,128)}, u32[]{:S(2)}) copy-start(f32[3,32]{1,0:T(4,128)} %get-tuple-element.122) | copy-start | bytes 1156
  341.5 4.3 %copy-start.9 = (f32[3,32,256]{2,1,0:T(8,128)S(1)}, f32[3,32,256]{2,1,0:T(8,128)}, u32[]{:S(2)}) copy-start(f32[3,32,256]{2,1,0:T(8,128)} %get-tuple-element.123) | copy-start | bytes 294916
  341.5 5.0 %copy-start.15 = (f32[3,32]{1,0:T(4,128)S(1)}, f32[3,32]{1,0:T(4,128)}, u32[]{:S(2)}) copy-start(f32[3,32]{1,0:T(4,128)} %get-tuple-element.124) | copy-start | bytes 1156
  341.5 5.6 %copy-start.8 = (f32[3,32,256]{2,1,0:T(8,128)S(1)}, f32[3,32,256]{2,1,0:T(8,128)}, u32[]{:S(2)}) copy-start(f32[3,32,256]{2,1,0:T(8,128)} %get-tuple-element.125) | copy-start | bytes 294916
  341.5 6.2 %copy-start.14 = (f32[3,32]{1,0:T(4,128)S(1)}, f32[3,32]{1,0:T(4,128)}, u32[]{:S(2)}) copy-start(f32[3,32]{1,0:T(4,128)} %get-tuple-element.126) | copy-start | bytes 1156
  341.5 6.8 %copy-start.13 = (f32[3,32]{1,0:T(4,128)S(1)}, f32[3,32]{1,0:T(4,128)}, u32[]{:S(2)}) copy-start(f32[3,32]{1,0:T(4,128)} %get-tuple-element.127) | copy-start | bytes 1156
  341.5 7.3 %copy-start.3 = (f32[768,256]{1,0:T(8,128)S(1)}, f32[768,256]{1,0:T(8,128)}, u32[]{:S(2)}) copy-start(f32[768,256]{1,0:T(8,128)} %get-tuple-element.128) | copy-start | bytes 2359300
  343.5 6.3 %copy-start.11 = (f32[16,128]{1,0:T(8,128)S(1)}, f32[16,128]{1,0:T(8,128)}, u32[]{:S(2)}) copy-start(f32[16,128]{1,0:T(8,128)} %get-tuple-element.74) | copy-start | bytes 24580

commit v3 on v0

--- a/solution.py
+++ b/solution.py
@@ -1,10 +1,20 @@
+import functools
+import types
+
 import jax
 import jax.numpy as jnp
 from jax import lax
+from jax.experimental import pallas as pl
+from jax.experimental.pallas import tpu as pltpu
 from jax.sharding import PartitionSpec as P
 
 EPS = 1e-06
 HIGH = lax.Precision.HIGHEST
+MESH = pl.DeviceIdType.MESH
+K1 = 0.7978845608028654
+K2 = 0.044715
+VMEM_BYTES = 62 * 2**20
+N_SEMS = 400
 
 
 def passed_along(shard, axis, by):
@@ -330,6 +340,965 @@
     )
 
 
+class Net:
+    def __init__(self, n_seq, n_ch, rows, send_sems, recv_sems):
+        self.n_seq, self.n_ch, self.rows = n_seq, n_ch, rows
+        self.n_z = n_seq // 2
+        self.send_sems, self.recv_sems = send_sems, recv_sems
+        self.tags, self.used, self.sent = {}, 0, []
+        self.s, self.c = lax.axis_index("seq"), lax.axis_index("ch")
+        s, c, n_z = self.s, self.c, self.n_z
+        self.z, self.x, self.y, self.core = s // 2, s % 2, c // 2, c % 2
+        x, y = self.x, self.y
+        self.s_to = [(s + k) % n_seq for k in range(n_seq)]
+        self.s_from = [(s + n_seq - k) % n_seq for k in range(n_seq)]
+        self.sibling = self.dev(self.z, x, y, 1 - self.core)
+        self.across = self.dev(self.z, x, 1 - y, self.core)
+        self.beside = self.dev(self.z, 1 - x, y, self.core)
+        self.above = self.dev((self.z + 1) % n_z, x, y, self.core)
+        self.below = self.dev((self.z + n_z - 1) % n_z, x, y, self.core)
+
+    def dev(self, z, x, y, core):
+        return (z * 2 + x, y * 2 + core)
+
+    def block(self, z, x, y, core):
+        rows = self.rows
+        return pl.multiple_of(((z * 2 + x) * self.n_ch + y * 2 + core) * rows, rows)
+
+    def z_of(self, slot):
+        return (self.z + self.n_z - slot) % self.n_z
+
+    def slot(self, at):
+        if at == 0:
+            return 0
+        n_z, z = self.n_z, self.z
+        low, high = (n_z - 1 - z) // (n_z - 1), z // (n_z - 1)
+        inner = (at + 1) // 2 if at % 2 else n_z - at // 2
+        return low * (n_z - at) + high * at + (1 - low - high) * inner
+
+    def meet(self, peers):
+        barrier = pltpu.get_barrier_semaphore()
+        for peer in peers:
+            pl.semaphore_signal(barrier, inc=1, device_id=peer, device_id_type=MESH)
+        pl.semaphore_wait(barrier, len(peers))
+
+    def sems(self, tag, at=0, size=1):
+        if tag not in self.tags:
+            self.tags[tag] = self.used
+            self.used += size
+        index = self.tags[tag] + at
+        return self.send_sems.at[index], self.recv_sems.at[index]
+
+    def copy(self, src, dst, sems, to):
+        return pltpu.make_async_remote_copy(
+            src_ref=src, dst_ref=dst, send_sem=sems[0], recv_sem=sems[1],
+            device_id=to, device_id_type=MESH,
+        )
+
+    def send(self, src, dst, to, sems, when=None):
+        copy = self.copy(src, dst, sems, to)
+        if when is None:
+            copy.start()
+        else:
+            @pl.when(when)
+            def _():
+                copy.start()
+        self.sent.append((copy, when))
+
+    def recv(self, view, sems):
+        self.copy(view, view, sems, (self.s, self.c)).wait_recv()
+
+    def local(self, src, dst, sems):
+        copy = pltpu.make_async_copy(src, dst, sems[0])
+        copy.start()
+        return copy
+
+    def drain(self):
+        for copy, when in self.sent:
+            if when is None:
+                copy.wait_send()
+            else:
+                @pl.when(when)
+                def _(copy=copy):
+                    copy.wait_send()
+        self.sent = []
+
+    def ch_gather_start(self, view_of, tag):
+        mine = view_of(self.c)
+        self.send(mine, mine, self.across, self.sems((tag, "y")))
+        self.send(mine, mine, self.sibling, self.sems((tag, "core")))
+
+    def ch_gather_finish(self, view_of, tag):
+        y, core = self.y, self.core
+        theirs = view_of((1 - y) * 2 + core)
+        self.recv(theirs, self.sems((tag, "y")))
+        self.send(theirs, theirs, self.sibling, self.sems((tag, "fwd")))
+        self.recv(view_of(y * 2 + 1 - core), self.sems((tag, "core")))
+        self.recv(view_of((1 - y) * 2 + 1 - core), self.sems((tag, "fwd")))
+
+    def ch_sum(self, part, mid, low, far, tag):
+        y, core = self.y, self.core
+        first = self.copy(part.at[1 - core], mid, self.sems((tag, "core")), self.sibling)
+        first.start()
+        first.wait()
+        low[...] = (part[core, 1 - y] + mid[1 - y]).astype(jnp.bfloat16)
+        second = self.copy(low, far, self.sems((tag, "y")), self.across)
+        second.start()
+        total = part[core, y] + mid[y]
+        second.wait()
+        return total + far[...].astype(jnp.float32)
+
+    def chain_start(self, mine, target, tag):
+        n_z, z = self.n_z, self.z
+        self.send(mine, target, self.above, (self.sems((tag, "own"), 0, 2)[0], self.sems((tag, "z"), 1, n_z)[1]), z < n_z - 1)
+        self.send(mine, target, self.below, (self.sems((tag, "own"), 1, 2)[0], self.sems((tag, "z"), n_z - 1, n_z)[1]), z > 0)
+
+    def chain_arrive(self, view, slot, tag):
+        n_z, z = self.n_z, self.z
+        self.recv(view, self.sems((tag, "z"), slot, n_z))
+        up = (self.sems((tag, "up"), slot, n_z)[0], self.sems((tag, "z"), (slot + 1) % n_z, n_z)[1])
+        down = (self.sems((tag, "up"), slot, n_z)[0], self.sems((tag, "z"), (slot + n_z - 1) % n_z, n_z)[1])
+        self.send(view, view, self.above, up, (z >= slot) & (z < n_z - 1))
+        self.send(view, view, self.below, down, (z < slot) & (z > 0))
+
+
+class Spread:
+    def __init__(self, net, ref, tag):
+        self.net, self.ref, self.tag = net, ref, tag
+
+    def view(self, slot, x, y, core, half=None):
+        net = self.net
+        at, rows = net.block(net.z_of(slot), x, y, core), net.rows
+        if half is not None:
+            at, rows = pl.multiple_of(at + half * (rows // 2), rows // 2), rows // 2
+        return self.ref.at[pl.ds(at, rows)]
+
+    def sems(self, what, slot):
+        return self.net.sems((self.tag, what), slot, self.net.n_z)
+
+    def start(self):
+        net = self.net
+        mine = self.view(0, net.x, net.y, net.core)
+        net.chain_start(mine, mine, self.tag)
+        self.plane(0)
+
+    def plane(self, slot):
+        net = self.net
+        view = self.view(slot, net.x, net.y, net.core)
+        net.send(view, view, net.beside, self.sems("x", slot))
+        net.send(view, view, net.across, self.sems("y", slot))
+        net.send(view, view, net.sibling, self.sems("s0", slot))
+
+    def arrive(self, slot):
+        net = self.net
+        net.chain_arrive(self.view(slot, net.x, net.y, net.core), slot, self.tag)
+        self.plane(slot)
+
+    def relay(self, slot):
+        net = self.net
+        x, y, core = net.x, net.y, net.core
+        view = self.view(slot, 1 - x, y, core)
+        net.recv(view, self.sems("x", slot))
+        half = self.view(slot, 1 - x, y, core, 0)
+        net.send(half, half, net.across, self.sems("d0", slot))
+        net.send(view, view, net.sibling, self.sems("s1", slot))
+        view = self.view(slot, x, 1 - y, core)
+        net.recv(view, self.sems("y", slot))
+        half = self.view(slot, x, 1 - y, core, 1)
+        net.send(half, half, net.beside, self.sems("d1", slot))
+        net.send(view, view, net.sibling, self.sems("s2", slot))
+
+    def relay_far(self, slot):
+        net = self.net
+        for half in (0, 1):
+            view = self.view(slot, 1 - net.x, 1 - net.y, net.core, half)
+            net.recv(view, self.sems(f"d{half}", slot))
+            net.send(view, view, net.sibling, self.sems(f"s{3 + half}", slot))
+
+    def done(self, slot):
+        net = self.net
+        x, y, core = net.x, net.y, 1 - net.core
+        net.recv(self.view(slot, x, y, core), self.sems("s0", slot))
+        net.recv(self.view(slot, 1 - x, y, core), self.sems("s1", slot))
+        net.recv(self.view(slot, x, 1 - y, core), self.sems("s2", slot))
+        for half in (0, 1):
+            net.recv(self.view(slot, 1 - x, 1 - y, core, half), self.sems(f"s{3 + half}", slot))
+
+
+class Collect:
+    def __init__(self, net, part, sib, far, side, along, tag):
+        self.net, self.part, self.sib, self.far, self.side, self.along, self.tag = net, part, sib, far, side, along, tag
+
+    def sems(self, what, at):
+        return self.net.sems((self.tag, what), at, self.net.n_z)
+
+    def first(self, at):
+        net = self.net
+        net.send(self.part.at[at, 1 - net.core], self.sib.at[at], net.sibling, self.sems("s", at))
+
+    def second(self, at):
+        net = self.net
+        net.recv(self.sib.at[at], self.sems("s", at))
+        core, part, sib = net.core, self.part, self.sib
+
+        def add(i, _):
+            part[at, core, i] = (part[at, core, i].astype(jnp.float32) + sib[at, i].astype(jnp.float32)).astype(jnp.bfloat16)
+            return 0
+
+        lax.fori_loop(0, 4, add, 0)
+        half = net.rows // 2
+        diagonal = part.at[at, core, (1 - net.x) * 2 + 1 - net.y]
+        net.send(diagonal.at[pl.ds(0, half)], self.far.at[at, 0], net.beside, self.sems("f0", at))
+        net.send(diagonal.at[pl.ds(half, half)], self.far.at[at, 1], net.across, self.sems("f1", at))
+
+    def third(self, at):
+        net, part, far = self.net, self.part, self.far
+        half = net.rows // 2
+        for which, index, first, to in (
+            (0, net.x * 2 + 1 - net.y, 0, net.across),
+            (1, (1 - net.x) * 2 + net.y, half, net.beside),
+        ):
+            net.recv(far.at[at, which], self.sems(f"f{which}", at))
+            rows = pl.ds(first, half)
+            value = part[at, net.core, index, rows, :].astype(jnp.float32) + far[at, which].astype(jnp.float32)
+            part[at, net.core, index, rows, :] = value.astype(jnp.bfloat16)
+            net.send(part.at[at, net.core, index], self.side.at[at, which], to, self.sems(f"p{which}", at))
+
+    def fourth(self, at):
+        net = self.net
+        mine = net.x * 2 + net.y
+        for which in (0, 1):
+            net.recv(self.side.at[at, which], self.sems(f"p{which}", at))
+        total = self.part[at, net.core, mine].astype(jnp.float32)
+        total = total + self.side[at, 0].astype(jnp.float32) + self.side[at, 1].astype(jnp.float32)
+        if at == 0:
+            return total
+        slot = net.slot(at)
+        self.part[at, net.core, mine] = total.astype(jnp.bfloat16)
+        net.send(
+            self.part.at[at, net.core, mine], self.along.at[slot], net.dev(net.z_of(slot), net.x, net.y, net.core),
+            self.sems("z", slot),
+        )
+        return None
+
+    def total(self, own):
+        net = self.net
+        for slot in range(1, net.n_z):
+            net.recv(self.along.at[slot], self.sems("z", slot))
+            own = own + self.along[slot].astype(jnp.float32)
+        return own
+
+
+def stack_rows(rows):
+    return jnp.concatenate(rows, axis=0)
+
+
+def smooth_pair(v):
+    t = jnp.tanh(K1 * (v + K2 * v * v * v))
+    value = 0.5 * v * (1.0 + t)
+    slope = 0.5 * (1.0 + t) + 0.5 * v * (1.0 - t * t) * K1 * (1.0 + 3.0 * K2 * v * v)
+    return value, slope
+
+
+def sigmoid(v):
+    return 1.0 / (1.0 + jnp.exp(-v))
+
+
+def softplus_exact(d):
+    u = jnp.exp(-jnp.abs(d))
+    r = u / (2.0 + u)
+    q = r * r
+    series = 1.0 / 15.0
+    for k in (13, 11, 9, 7, 5, 3, 1):
+        series = series * q + 1.0 / k
+    return jnp.maximum(d, 0.0) + 2.0 * r * series
+
+
+def minus_expm1(v):
+    series = 1.0 / 362880.0
+    for k in (40320.0, 5040.0, 720.0, 120.0, 24.0, 6.0, 2.0, 1.0):
+        series = series * v + 1.0 / k
+    return jnp.where(v > -0.5, -v * series, 1.0 - jnp.exp(v))
+
+
+class Docs:
+    def __init__(self, lengths, first, count, before=0):
+        position = first - before + lax.broadcasted_iota(jnp.int32, (count, 1), 0)
+        self.opening, self.closing = [], []
+        start_of = jnp.zeros((count, 1), jnp.int32)
+        start = jnp.int32(0)
+        for e in range(lengths.shape[0]):
+            end = start + lengths[e]
+            owner = (position >= start) & (position < end)
+            start_of = jnp.where(owner, start, start_of)
+            self.opening.append((position == start).astype(jnp.float32))
+            self.closing.append((position == end - 1).astype(jnp.float32))
+            start = end
+        self.offset = position - start_of
+        self.keep = (self.offset > 0).astype(jnp.float32)
+
+    def valid(self, k):
+        return (self.offset >= k).astype(jnp.float32)
+
+
+def prefix(a, b, count):
+    row = lax.broadcasted_iota(jnp.int32, a.shape, 0)
+    k = 1
+    while k < count:
+        inside = row >= k
+        a_far = jnp.where(inside, pltpu.roll(a, k, 0), 1.0)
+        b_far = jnp.where(inside, pltpu.roll(b, k, 0), 0.0)
+        b = a * b_far + b
+        a = a * a_far
+        k *= 2
+    return a, b
+
+
+def suffix(a, b, count):
+    row = lax.broadcasted_iota(jnp.int32, a.shape, 0)
+    k = 1
+    while k < count:
+        inside = row < count - k
+        a_far = jnp.where(inside, pltpu.roll(a, count - k, 0), 1.0)
+        b_far = jnp.where(inside, pltpu.roll(b, count - k, 0), 0.0)
+        b = a * b_far + b
+        a = a * a_far
+        k *= 2
+    return a, b
+
+
+def coefficient_parts(rate_pre, inlet_pre, decay):
+    rate = sigmoid(rate_pre)
+    inlet = sigmoid(inlet_pre)
+    sp = softplus_exact(decay)
+    log_decay = -8.0 * rate * sp
+    factor = jnp.exp(log_decay)
+    scale = jnp.sqrt(minus_expm1(2.0 * log_decay))
+    return rate, inlet, sp, log_decay, factor, scale
+
+
+def opening_rows(docs, init):
+    total = docs.opening[0] * init[0:1]
+    for e in range(1, len(docs.opening)):
+        total = total + docs.opening[e] * init[e : e + 1]
+    return total
+
+
+def pack_gain(row):
+    tiles = [row[:, i * 128 : (i + 1) * 128] for i in range(row.shape[1] // 128)]
+    return jnp.concatenate([stack_rows(tiles[i : i + 8]) for i in range(0, len(tiles), 8)], axis=1)
+
+
+def norm_back(values, gain, grad):
+    r = lax.rsqrt(jnp.mean(values * values, axis=-1, keepdims=True) + EPS)
+    u = grad * gain
+    to_values = r * u - values * (r * r * r) * jnp.mean(u * values, axis=-1, keepdims=True)
+    to_gain = jnp.sum(grad * values * r, axis=0, keepdims=True)
+    return to_values, to_gain
+
+
+RIM = 16
+
+
+def block_kernel(sizes, names, *refs):
+    n_seq, n_ch, rows, d, slots, bw, width, sl = sizes
+    r = types.SimpleNamespace(**dict(zip(names, refs)))
+    bf, f32 = jnp.bfloat16, jnp.float32
+    net = Net(n_seq, n_ch, rows, r.send_sems, r.recv_sems)
+    s, c, x, y, z, core, n_z = net.s, net.c, net.x, net.y, net.z, net.core, net.n_z
+    count, wide, tokens = rows * n_ch, slots * bw, rows * n_ch * n_seq
+    n_taps = r.taps.shape[0]
+    seq_peers = [(net.s_to[k], c) for k in range(1, n_seq)]
+    rim_peers = [(net.s_to[k], (c + i) % n_ch) for k in (1, n_seq - 1) for i in range(1, n_ch)]
+    net.meet(seq_peers + rim_peers + [net.sibling, net.across])
+
+    own_cols = pl.ds(pl.multiple_of(s * width, width), width)
+    own_count = pl.ds(pl.multiple_of(s * count, count), count)
+    own_slice = pl.ds(pl.multiple_of(s * sl, sl), sl)
+    local = []
+
+    values = r.stream[...].astype(f32)
+    scale = lax.rsqrt(jnp.mean(values * values, axis=-1, keepdims=True) + EPS)
+    mix_rows = pl.ds(pl.multiple_of(RIM + c * rows, 16), rows)
+    r.mix[mix_rows, :] = (values * scale * r.mix_gain[...][None, :]).astype(bf)
+
+    def mix_of(cc):
+        return r.mix.at[pl.ds(pl.multiple_of(RIM + cc * rows, 16), rows)]
+
+    last, first = r.mix.at[pl.ds(count, RIM)], r.mix.at[pl.ds(0, RIM)]
+    net.ch_gather_start(mix_of, "mix")
+    for i in range(n_ch):
+        net.send(last, first, (net.s_to[1], i), net.sems("rim", i, n_ch), (c == n_ch - 1) & (s < n_seq - 1))
+
+    @pl.when(s == 0)
+    def _():
+        r.mix[pl.ds(0, RIM), :] = jnp.zeros((RIM, d), bf)
+
+    cots = Spread(net, r.cfull, "cot")
+    lows = Spread(net, r.full, "low")
+    mine = net.block(z, x, y, core)
+    r.cfull[pl.ds(mine, rows), :] = r.cot[...]
+    cots.start()
+
+    def left_start(a, src):
+        r.left[a, s, c] = src[:, own_cols]
+        for k in range(1, n_seq):
+            cols = pl.ds(pl.multiple_of(net.s_to[k] * width, width), width)
+            net.send(src.at[:, cols], r.left.at[a, s, c], (net.s_to[k], c), net.sems(("left", a), k, n_seq))
+
+    def left_pass(a):
+        for k in range(1, n_seq):
+            net.recv(r.left.at[a, net.s_from[k], c], net.sems(("left", a), k, n_seq))
+        net.ch_gather_start(lambda cc: r.left.at[a, :, cc], ("leftch", a))
+
+    def left_done(a):
+        net.ch_gather_finish(lambda cc: r.left.at[a, :, cc], ("leftch", a))
+
+    left_start(0, r.mix.at[mix_rows])
+
+    def turn(a, src):
+        for i in range(src.shape[1] // 256):
+            r.turned[a, i * 256 : (i + 1) * 256, :] = src[:, i * 256 : (i + 1) * 256].T
+
+    def weight_start(a):
+        src = r.turned.at[a] if a < 2 else r.down
+        for k in range(1, n_seq):
+            net.send(
+                src.at[pl.ds(pl.multiple_of(net.s_to[k] * sl, sl), sl)], r.wt.at[a, :, own_cols],
+                (net.s_to[k], c), net.sems(("w", a), k, n_seq),
+            )
+        local.append(net.local(src.at[own_slice], r.wt.at[a, :, own_cols], net.sems(("w", a), 0, n_seq)))
+
+    def weight_done(a):
+        for k in range(1, n_seq):
+            cols = pl.ds(pl.multiple_of(net.s_from[k] * width, width), width)
+            net.recv(r.wt.at[a, :, cols], net.sems(("w", a), k, n_seq))
+        local.pop(0).wait()
+
+    turn(0, r.gate_w)
+    weight_start(0)
+    turn(1, r.up_w)
+
+    net.ch_gather_finish(mix_of, "mix")
+    for i in range(n_ch):
+        @pl.when((s > 0) & (c == i))
+        def _(i=i):
+            net.recv(first, net.sems("rim", i, n_ch))
+
+    docs = Docs(r.lengths, s * count, count)
+    keep = docs.keep
+    ends_a, ends_b = [], []
+    for b in range(slots):
+        cols = pl.ds(b * bw, bw)
+        rowsof = r.mix[...]
+        r.gelu[:, cols] = jnp.dot(rowsof[RIM:], r.gelu_w[:, cols], preferred_element_type=f32)
+        recur = jnp.dot(rowsof, r.recur_w[:, cols], preferred_element_type=f32).astype(bf)
+        r.recur[:, cols] = recur
+        recur = recur.astype(f32)
+        conv_pre = r.bias[b : b + 1, :]
+        for k in range(n_taps):
+            conv_pre = conv_pre + r.taps[k, b : b + 1, :] * recur[RIM - k : RIM - k + count] * docs.valid(k)
+        conv_low = conv_pre.astype(bf)
+        r.conv[:, cols] = conv_low
+        rate_pre = jnp.dot(conv_low, r.rate_w[b], preferred_element_type=f32) + r.rate_b[b : b + 1, :]
+        inlet_pre = jnp.dot(conv_low, r.inlet_w[b], preferred_element_type=f32) + r.inlet_b[b : b + 1, :]
+        r.rate_pre[:, cols] = rate_pre
+        r.inlet_pre[:, cols] = inlet_pre
+        rate, inlet, sp, log_decay, factor, scale = coefficient_parts(rate_pre, inlet_pre, r.decay[b : b + 1, :])
+        source = scale * inlet * conv_low.astype(f32) + (1.0 - keep) * factor * opening_rows(docs, r.init[:, cols])
+        total, part = prefix(keep * factor, source, count)
+        r.scan_a[:, cols] = total
+        r.scan_b[:, cols] = part
+        ends_a.append(total[count - 1 : count])
+        ends_b.append(part[count - 1 : count])
+
+    def exchange(summary, pieces, tag):
+        summary[s] = stack_rows(pieces + [jnp.zeros((8 - 2 * slots, bw), f32)])
+        for k in range(1, n_seq):
+            net.send(summary.at[s], summary.at[s], (net.s_to[k], c), net.sems(tag, k, n_seq))
+
+    def exchanged(summary, tag):
+        for k in range(1, n_seq):
+            net.recv(summary.at[net.s_from[k]], net.sems(tag, k, n_seq))
+
+    exchange(r.summary, ends_a + ends_b, "sum")
+    cots.arrive(net.slot(1))
+    cots.arrive(net.slot(2))
+    weight_start(1)
+    cots.relay(0)
+    exchanged(r.summary, "sum")
+    enter = jnp.zeros((slots, bw), f32)
+    for q in range(n_seq - 1):
+        after = r.summary[q, 0:slots] * enter + r.summary[q, slots : 2 * slots]
+        enter = jnp.where(s > q, after, enter)
+    finals = []
+    for b in range(slots):
+        cols = pl.ds(b * bw, bw)
+        live = jnp.where(r.counts[0] > b, 1.0, 0.0)
+        state = r.scan_b[:, cols] + r.scan_a[:, cols] * enter[b : b + 1]
+        r.state[:, cols] = state
+        value, _ = smooth_pair(r.gelu[:, cols])
+        r.own[0, :, cols] = (value * state * live).astype(bf)
+        ends = [jnp.sum(mark * state, axis=0, keepdims=True) * live for mark in docs.closing]
+        finals.append(stack_rows(ends + [jnp.zeros((8 - len(ends), bw), f32)]))
+
+    def branch_tile(i, _):
+        cols = pl.ds(pl.multiple_of(i * 256, 256), 256)
+        value = jnp.dot(r.own[0], r.out_w[:, cols], preferred_element_type=f32)
+        for cc in range(n_ch):
+            r.part[cc % 2, cc // 2, :, cols] = value[cc * rows : (cc + 1) * rows]
+        return 0
+
+    lax.fori_loop(0, d // 256, branch_tile, 0)
+    middle = values + net.ch_sum(r.part, r.mid, r.ylow, r.yfar, "branch")
+    scale = lax.rsqrt(jnp.mean(middle * middle, axis=-1, keepdims=True) + EPS)
+    r.full[pl.ds(mine, rows), :] = (middle * scale * r.ffn_gain[...][None, :]).astype(bf)
+    r.middle[...] = middle
+
+    lows.start()
+    cots.arrive(net.slot(3))
+    weight_start(2)
+    cots.relay(net.slot(1))
+    cots.relay(net.slot(2))
+    cots.relay_far(0)
+    lows.relay(0)
+    lows.arrive(net.slot(1))
+    lows.arrive(net.slot(2))
+    lows.relay_far(0)
+    lows.relay(net.slot(1))
+    lows.relay(net.slot(2))
+    lows.arrive(net.slot(3))
+    cots.relay(net.slot(3))
+    for at in (1, 2, 3):
+        cots.relay_far(net.slot(at))
+    group = n_ch * 2 * rows
+
+    def chunk(at):
+        return pl.ds(pl.multiple_of(net.z_of(net.slot(at)) * group, group), group)
+
+    weight_done(0)
+    weight_done(1)
+
+    def forward(at):
+        lows.done(net.slot(at))
+        here = chunk(at)
+        gate = contract_last(r.full[here, :], r.wt[0])
+        up = contract_last(r.full[here, :], r.wt[1])
+        value, slope = smooth_pair(gate)
+        r.value[here, :] = value
+        r.slope[here, :] = up * slope
+        r.hid[here, :] = (value * up).astype(bf)
+
+    forward(0)
+    lows.relay_far(net.slot(1))
+    lows.relay(net.slot(3))
+    forward(1)
+    lows.relay_far(net.slot(2))
+    forward(2)
+    lows.relay_far(net.slot(3))
+    forward(3)
+    for at in range(n_z):
+        cots.done(net.slot(at))
+
+    def weight_grad(a, left, right):
+        def tile(i, _):
+            cols = pl.ds(pl.multiple_of(i * 256, 256), 256)
+            r.dwl[a, :, cols] = contract_first(left[...], right[:, cols]).astype(bf)
+            return 0
+
+        lax.fori_loop(0, d // 256, tile, 0)
+        for k in range(1, n_seq):
+            cols = pl.ds(pl.multiple_of(net.s_to[k] * width, width), width)
+            net.send(r.dwl.at[a, :, cols], r.dw.at[a, own_slice], (net.s_to[k], c), net.sems(("dw", a), k, n_seq))
+        local.append(net.local(r.dwl.at[a, :, own_cols], r.dw.at[a, own_slice], net.sems(("dw", a), 0, n_seq)))
+
+    def weight_grad_done(a):
+        for k in range(1, n_seq):
+            rows_at = pl.ds(pl.multiple_of(net.s_from[k] * sl, sl), sl)
+            net.recv(r.dw.at[a, rows_at], net.sems(("dw", a), k, n_seq))
+
+    weight_grad(2, r.hid, r.cfull)
+    down_local = local.pop()
+    weight_done(2)
+    local.append(down_local)
+
+    def spread_out(ref, at, value, cols):
+        value = value.astype(bf)
+        for xx in range(2):
+            for yy in range(2):
+                for cc in range(2):
+                    row = (xx * 4 + yy * 2 + cc) * rows
+                    ref[at, cc, xx * 2 + yy, :, cols] = value[row : row + rows]
+
+    def backward(at):
+        here = chunk(at)
+        grad = contract_last(r.cfull[here, :], r.wt[2])
+        r.gat[here, :] = (grad * r.slope[here, :]).astype(bf)
+        r.upg[here, :] = (grad * r.value[here, :]).astype(bf)
+
+        def tile(i, _):
+            cols = pl.ds(pl.multiple_of(i * 256, 256), 256)
+            value = jnp.dot(r.gat[here, :], r.wt[0, :, cols], preferred_element_type=f32)
+            value = value + jnp.dot(r.upg[here, :], r.wt[1, :, cols], preferred_element_type=f32)
+            spread_out(r.npart, at, value, cols)
+            return 0
+
+        lax.fori_loop(0, d // 256, tile, 0)
+
+    def output(at):
+        here = chunk(at)
+
+        def tile(i, _):
+            cols = pl.ds(pl.multiple_of(i * 256, 256), 256)
+            value = jnp.dot(r.hid[here, :], r.wt[2, :, cols], preferred_element_type=f32)
+            spread_out(r.opart, at, value, cols)
+            return 0
+
+        lax.fori_loop(0, d // 256, tile, 0)
+
+    norms = Collect(net, r.npart, r.nsib, r.nfar, r.nside, r.nalong, "norm")
+    outs = Collect(net, r.opart, r.osib, r.ofar, r.oside, r.oalong, "out")
+    backward(3)
+    norms.first(3)
+    backward(2)
+    norms.first(2)
+    norms.second(3)
+    backward(1)
+    norms.first(1)
+    norms.second(2)
+    norms.third(3)
+    backward(0)
+    norms.first(0)
+    norms.second(1)
+    norms.third(2)
+    norms.fourth(3)
+    norms.second(0)
+    output(3)
+    output(2)
+    norms.third(1)
+    norms.fourth(2)
+    output(1)
+    output(0)
+    norms.third(0)
+    norms.fourth(1)
+    weight_grad(0, r.gat, r.full)
+    nfg = norms.total(norms.fourth(0))
+
+    to_middle, ffn_part = norm_back(middle, r.ffn_gain[...][None, :], nfg)
+    middle_grad = r.cot[...].astype(f32) + to_middle
+    r.branch[c] = middle_grad.astype(bf)
+    net.ch_gather_start(lambda cc: r.branch.at[cc], "bgrad")
+    left_start(1, r.branch.at[c])
+    outs.first(3)
+    outs.first(2)
+    r.early[n_z] = jnp.concatenate(finals + [pack_gain(ffn_part)], axis=1)
+    net.ch_gather_finish(lambda cc: r.branch.at[cc], "bgrad")
+
+    ahead_docs = Docs(r.lengths, s * count, count + RIM)
+    row = lax.broadcasted_iota(jnp.int32, (count, bw), 0)
+    heads_a, heads_b = [], []
+    for b in range(slots):
+        cols = pl.ds(b * bw, bw)
+        live = jnp.where(r.counts[0] > b, 1.0, 0.0)
+        product_grad = contract_last(r.branch[...].reshape(count, d), r.out_w[b * bw : (b + 1) * bw, :])
+        value, slope = smooth_pair(r.gelu[:, cols])
+        r.own[1, :, cols] = (product_grad * r.state[:, cols] * live * slope).astype(bf)
+        rate, inlet, sp, log_decay, factor, scale = coefficient_parts(r.rate_pre[:, cols], r.inlet_pre[:, cols], r.decay[b : b + 1, :])
+        carry = keep * factor
+        following = jnp.where(row < count - 1, pltpu.roll(carry, count - 1, 0), 1.0)
+        total, part = suffix(following, product_grad * value * live, count)
+        r.scan_a[:, cols] = total
+        r.scan_b[:, cols] = part
+        heads_a.append(carry[0:1] * total[0:1])
+        heads_b.append(carry[0:1] * part[0:1])
+    exchange(r.summary_back, heads_a + heads_b, "sumback")
+
+    chains = [r.gathered.at[a] for a in range(3)]
+
+    def gather_view(a, slot, xx):
+        at = (net.z_of(slot) * 2 + xx) * count
+        return r.gathered.at[a, pl.ds(pl.multiple_of(at, count), count)]
+
+    def gather_start(a):
+        view = gather_view(a, 0, x)
+        net.chain_start(r.own.at[a], view, ("g", a))
+        net.send(r.own.at[a], view, net.beside, net.sems(("gx", a), 0, n_z))
+        local.append(net.local(r.own.at[a], view, net.sems(("glocal", a))))
+
+    def gather_arrive(a, at):
+        slot = net.slot(at)
+        view = gather_view(a, slot, x)
+        net.chain_arrive(view, slot, ("g", a))
+        net.send(view, view, net.beside, net.sems(("gx", a), slot, n_z))
+
+    def gather_done(a):
+        for slot in range(n_z):
+            net.recv(gather_view(a, slot, 1 - x), net.sems(("gx", a), slot, n_z))
+
+    gather_start(0)
+    outs.first(1)
+    outs.first(0)
+    for at in (3, 2, 1, 0):
+        outs.second(at)
+    exchanged(r.summary_back, "sumback")
+    enter_back = jnp.zeros((slots, bw), f32)
+    for q in range(n_seq - 1, 0, -1):
+        after = r.summary_back[q, 0:slots] * enter_back + r.summary_back[q, slots : 2 * slots]
+        enter_back = jnp.where(s < q, after, enter_back)
+    vec = []
+    for b in range(slots):
+        cols = pl.ds(b * bw, bw)
+        adjoint = r.scan_b[:, cols] + r.scan_a[:, cols] * enter_back[b : b + 1]
+        previous = jnp.where(row > 0, pltpu.roll(r.state[:, cols], 1, 0), enter[b : b + 1])
+        decay = r.decay[b : b + 1, :]
+        rate, inlet, sp, log_decay, factor, scale = coefficient_parts(r.rate_pre[:, cols], r.inlet_pre[:, cols], decay)
+        conv_low = r.conv[:, cols]
+        conv = conv_low.astype(f32)
+        init_rows = opening_rows(docs, r.init[:, cols])
+        log_grad = adjoint * (
+            factor * (keep * previous + (1.0 - keep) * init_rows) - inlet * conv * jnp.exp(2.0 * log_decay) / scale
+        )
+        rate_low = (log_grad * (-8.0 * sp) * rate * (1.0 - rate)).astype(bf)
+        direct = adjoint * scale
+        inlet_low = (direct * conv * inlet * (1.0 - inlet)).astype(bf)
+        decay_row = jnp.sum(log_grad * (-8.0 * rate), axis=0, keepdims=True) * sigmoid(decay)
+        back = direct * inlet + contract_last(rate_low, r.rate_w[b]) + contract_last(inlet_low, r.inlet_w[b])
+        r.cgrad[0:count, cols] = back.astype(bf)
+        for a, low in enumerate((rate_low, inlet_low)):
+            part = contract_first(conv_low, low).astype(bf)
+            r.gates[a, b] = part.reshape(r.gates.shape[2:])
+        vec.append([
+            jnp.sum(rate_low.astype(f32), axis=0, keepdims=True),
+            jnp.sum(inlet_low.astype(f32), axis=0, keepdims=True),
+            decay_row,
+        ])
+    rim = r.cgrad.at[pl.ds(count, RIM)]
+    net.send(r.cgrad.at[pl.ds(0, RIM)], rim, (net.s_to[n_seq - 1], c), net.sems("rimback"), s > 0)
+
+    @pl.when(s == n_seq - 1)
+    def _():
+        r.cgrad[pl.ds(count, RIM), :] = jnp.zeros((RIM, wide), bf)
+
+    net.send(r.gates.at[:, :, :, 1 - x], r.gates_x, net.beside, net.sems("gatesx"))
+    weight_grad(1, r.upg, r.full)
+
+    @pl.when(s < n_seq - 1)
+    def _():
+        net.recv(rim, net.sems("rimback"))
+
+    vectors = []
+    for b in range(slots):
+        cols = pl.ds(b * bw, bw)
+        grad = r.cgrad[:, cols].astype(f32)
+        own = grad[:count]
+        recur = r.recur[:, cols].astype(f32)
+        total = jnp.zeros((count, bw), f32)
+        tap_rows = []
+        for k in range(n_taps):
+            tap_rows.append(jnp.sum(own * recur[RIM - k : RIM - k + count] * docs.valid(k), axis=0, keepdims=True))
+            total = total + r.taps[k, b : b + 1, :] * grad[k : k + count] * ahead_docs.valid(k)[k : k + count]
+        r.own[2, :, cols] = total.astype(bf)
+        vectors.append(stack_rows(tap_rows + [jnp.sum(own, axis=0, keepdims=True)] + vec[b]))
+    gather_start(2)
+    gather_start(1)
+
+    def norm_tile(i, _):
+        cols = pl.ds(pl.multiple_of(i * 256, 256), 256)
+        value = contract_last(r.own[1], r.gelu_w[cols, :]) + contract_last(r.own[2], r.recur_w[cols, :])
+        for cc in range(n_ch):
+            r.part[cc % 2, cc // 2, :, cols] = value[cc * rows : (cc + 1) * rows]
+        return 0
+
+    lax.fori_loop(0, d // 256, norm_tile, 0)
+    norm_grad = net.ch_sum(r.part, r.mid, r.ylow, r.yfar, "norm")
+    to_stream, mix_part = norm_back(values, r.mix_gain[...][None, :], norm_grad)
+    r.sgrad[...] = middle_grad + to_stream
+    r.late[n_z] = jnp.concatenate(vectors + [pack_gain(mix_part)], axis=1)
+    net.send(r.early.at[n_z], r.pair.at[0], net.beside, net.sems("pair", 0, 2))
+    net.send(r.late.at[n_z], r.pair.at[1], net.beside, net.sems("pair", 1, 2))
+    net.recv(r.gates_x, net.sems("gatesx"))
+
+    def gate_add(i, _):
+        for a in range(2):
+            for b in range(slots):
+                value = r.gates[a, b, i, x].astype(f32) + r.gates_x[a, b, i].astype(f32)
+                r.gates[a, b, i, x] = value.astype(bf)
+        return 0
+
+    lax.fori_loop(0, n_z, gate_add, 0)
+    for k in range(1, n_z):
+        to = net.z_of(k)
+        net.send(r.gates.at[:, :, to, x], r.gates_z.at[k], net.dev(to, x, y, core), net.sems("gatesz", k, n_z))
+    for at in (3, 2, 1, 0):
+        outs.third(at)
+    for a in (0, 1):
+        left_pass(a)
+    for a, ref in enumerate((r.early, r.late)):
+        net.recv(r.pair.at[a], net.sems("pair", a, 2))
+        ref[z] = ref[n_z] + r.pair[a]
+        for k in range(1, n_z):
+            to = net.z_of(k)
+            net.send(ref.at[z], ref.at[z], net.dev(to, x, y, core), net.sems(("vec", a), k, n_z))
+    for at in (1, 2, 3):
+        for a in (0, 2, 1):
+            gather_arrive(a, at)
+    for at in (3, 2, 1):
+        outs.fourth(at)
+    out_sum = outs.fourth(0)
+    for a in (0, 1):
+        left_done(a)
+    for a, ref in enumerate((r.early, r.late)):
+        for k in range(1, n_z):
+            net.recv(ref.at[(z + k) % n_z], net.sems(("vec", a), k, n_z))
+    early, late = r.early[0], r.late[0]
+    for q in range(1, n_z):
+        early, late = early + r.early[q], late + r.late[q]
+    r.shared[c] = jnp.concatenate([early, late[:, wide:]], axis=1)
+    net.ch_gather_start(lambda cc: r.shared.at[cc], "shared")
+    piece = bw // n_seq
+    for b in range(slots):
+        part = jnp.zeros((8, piece), f32)
+        for q in range(n_seq):
+            at = b * bw + q * piece
+            part = jnp.where(s == q, late[:, at : at + piece], part)
+        r.small[b] = part
+    for k in range(1, n_z):
+        net.recv(r.gates_z.at[k], net.sems("gatesz", k, n_z))
+    for a in range(2):
+        for b in range(slots):
+            total = r.gates[a, b, z, x].astype(f32)
+            for k in range(1, n_z):
+                total = total + r.gates_z[k, a, b].astype(f32)
+            r.gate_out[a, b] = total
+    net.ch_gather_finish(lambda cc: r.shared.at[cc], "shared")
+    gains = r.shared[0, :, wide:]
+    for cc in range(1, n_ch):
+        gains = gains + r.shared[cc, :, wide:]
+    for cc in range(n_ch):
+        r.finals[:, cc * wide : (cc + 1) * wide] = r.shared[cc, 0 : r.finals.shape[0], 0:wide]
+    half = gains.shape[1] // 2
+    for a in range(2):
+        for i in range(half // 128):
+            r.gains[a, i * 8 : (i + 1) * 8, :] = gains[:, a * half + i * 128 : a * half + (i + 1) * 128]
+    r.mixed[...] = (middle + outs.total(out_sum)).astype(bf)
+    for a in (2, 0, 1):
+        weight_grad_done(a)
+    for a in (0, 2, 1):
+        gather_done(a)
+    for copy in local:
+        copy.wait()
+    net.drain()
+
+
+def finish_kernel(names, *refs):
+    r = types.SimpleNamespace(**dict(zip(names, refs)))
+
+    def left(a):
+        value = r.left[a]
+        return value.reshape(value.shape[0] * value.shape[1] * value.shape[2], value.shape[3])
+
+    r.out_wg[...] = contract_first(r.gathered[0], left(1))
+    r.gelu_wg[...] = contract_first(left(0), r.gathered[1])
+    r.recur_wg[...] = contract_first(left(0), r.gathered[2])
+    for a, ref in enumerate((r.gate_wg, r.up_wg)):
+        for i in range(ref.shape[1] // 256):
+            ref[:, i * 256 : (i + 1) * 256] = r.dw[a, i * 256 : (i + 1) * 256, :].T.astype(jnp.float32)
+    r.down_wg[...] = r.dw[2].astype(jnp.float32)
+    r.finals_o[...] = r.finals[...]
+    r.mixed_o[...] = r.mixed[...]
+    r.sgrad_o[...] = r.sgrad[...]
+    r.ffn_o[...] = r.gains[0]
+    r.mix_o[...] = r.gains[1]
+    r.rate_o[...] = r.gate_out[0]
+    r.inlet_o[...] = r.gate_out[1]
+    n_taps = r.taps_o.shape[0]
+    for b in range(r.small.shape[0]):
+        for k in range(n_taps):
+            r.taps_o[k, b : b + 1, :] = r.small[b, k : k + 1, :]
+        for k, ref in enumerate((r.bias_o, r.rateb_o, r.inletb_o, r.decay_o)):
+            ref[b : b + 1, :] = r.small[b, n_taps + k : n_taps + k + 1, :]
+
+
+def gathered_body(
+    stream, cotangent, mix_gain, gelu_weight, recur_weight, conv_taps, conv_bias, rate_weight, rate_bias, inlet_weight,
+    inlet_bias, decay_param, init_states, out_weight, ffn_gain, gate_weight, up_weight, down_weight, doc_lengths, block_counts,
+):
+    n_seq, n_ch = lax.axis_size("seq"), lax.axis_size("ch")
+    rows, d = stream.shape
+    slots, bw = conv_bias.shape
+    width, hidden = gate_weight.shape
+    sl = hidden // n_seq
+    n_z = n_seq // 2
+    count, wide, tokens = rows * n_ch, slots * bw, rows * n_ch * n_seq
+    piece = bw // n_seq
+    n_taps, n_docs = conv_taps.shape[0], doc_lengths.shape[0]
+    bf, f32 = jnp.bfloat16, jnp.float32
+    vmem = pl.BlockSpec(memory_space=pltpu.VMEM)
+    smem = pl.BlockSpec(memory_space=pltpu.SMEM)
+    anywhere = pl.BlockSpec(memory_space=pl.ANY)
+    inputs = dict(
+        stream=stream, cot=cotangent, mix_gain=mix_gain, gelu_w=gelu_weight, recur_w=recur_weight, taps=conv_taps,
+        bias=conv_bias, rate_w=rate_weight, rate_b=rate_bias, inlet_w=inlet_weight, inlet_b=inlet_bias, decay=decay_param,
+        init=init_states, out_w=out_weight, ffn_gain=ffn_gain, gate_w=gate_weight, up_w=up_weight, down=down_weight,
+        lengths=doc_lengths, counts=block_counts,
+    )
+    places = dict(lengths=smem, counts=smem, down=anywhere)
+    outputs = dict(
+        gathered=((3, tokens, wide), bf), left=((2, n_seq, n_ch, rows, width), bf), dw=((3, hidden, width), bf),
+        finals=((n_docs, wide * n_ch), f32), mixed=((rows, d), bf), sgrad=((rows, d), f32), gains=((2, d // 128, 128), f32),
+        gate_out=((2, slots, piece, bw), f32), small=((slots, 8, piece), f32),
+    )
+    out_places = dict(gathered=anywhere, dw=anywhere)
+    packed = wide + d // 8
+    scratch = dict(
+        mix=((RIM + count, d), bf), full=((tokens, d), bf), cfull=((tokens, d), bf), turned=((2, hidden, width), bf),
+        wt=((3, sl, d), bf), dwl=((3, sl, d), bf), value=((tokens, sl), f32), slope=((tokens, sl), f32),
+        hid=((tokens, sl), bf), gat=((tokens, sl), bf), upg=((tokens, sl), bf),
+        gelu=((count, wide), f32), recur=((RIM + count, wide), bf), conv=((count, wide), bf), rate_pre=((count, wide), f32),
+        inlet_pre=((count, wide), f32), scan_a=((count, wide), f32), scan_b=((count, wide), f32), state=((count, wide), f32),
+        own=((3, count, wide), bf), cgrad=((count + RIM, wide), bf), branch=((n_ch, rows, d), bf),
+        summary=((n_seq, 8, bw), f32), summary_back=((n_seq, 8, bw), f32),
+        part=((2, 2, rows, d), f32), mid=((2, rows, d), f32), ylow=((rows, d), bf), yfar=((rows, d), bf), middle=((rows, d), f32),
+        npart=((n_z, 2, 4, rows, d), bf), nsib=((n_z, 4, rows, d), bf), nfar=((n_z, 2, rows // 2, d), bf),
+        nside=((n_z, 2, rows, d), bf), nalong=((n_z, rows, d), bf),
+        opart=((n_z, 2, 4, rows, d), bf), osib=((n_z, 4, rows, d), bf), ofar=((n_z, 2, rows // 2, d), bf),
+        oside=((n_z, 2, rows, d), bf), oalong=((n_z, rows, d), bf),
+        gates=((2, slots, n_z, 2, piece, bw), bf), gates_x=((2, slots, n_z, piece, bw), bf), gates_z=((n_z, 2, slots, piece, bw), bf),
+        early=((n_z + 1, 8, packed), f32), late=((n_z + 1, 8, packed), f32), pair=((2, 8, packed), f32),
+        shared=((n_ch, 8, packed + d // 8), f32),
+    )
+    dma = pltpu.SemaphoreType.DMA((N_SEMS,))
+    results = pl.pallas_call(
+        functools.partial(
+            block_kernel, (n_seq, n_ch, rows, d, slots, bw, width, sl),
+            list(inputs) + list(outputs) + list(scratch) + ["send_sems", "recv_sems"],
+        ),
+        out_shape=[jax.ShapeDtypeStruct(*what) for what in outputs.values()],
+        in_specs=[places.get(name, vmem) for name in inputs],
+        out_specs=[out_places.get(name, vmem) for name in outputs],
+        scratch_shapes=[pltpu.VMEM(*what) for what in scratch.values()] + [dma, dma],
+        compiler_params=pltpu.CompilerParams(collective_id=1, has_side_effects=True, vmem_limit_bytes=VMEM_BYTES),
+    )(*inputs.values())
+    vector = ((slots, piece), f32)
+    ends = dict(
+        finals_o=((n_docs, wide * n_ch), f32), mixed_o=((rows, d), bf), sgrad_o=((rows, d), f32), mix_o=((d // 128, 128), f32),
+        gelu_wg=((width, wide), f32), recur_wg=((width, wide), f32), taps_o=((n_taps, slots, piece), f32), bias_o=vector,
+        rate_o=((slots, piece, bw), f32), rateb_o=vector, inlet_o=((slots, piece, bw), f32), inletb_o=vector, decay_o=vector,
+        out_wg=((wide, width), f32), ffn_o=((d // 128, 128), f32), gate_wg=((width, hidden), f32), up_wg=((width, hidden), f32),
+        down_wg=((hidden, width), f32),
+    )
+    last = pl.pallas_call(
+        functools.partial(finish_kernel, list(outputs) + list(ends)),
+        out_shape=[jax.ShapeDtypeStruct(*what) for what in ends.values()],
+        in_specs=[vmem] * len(outputs),
+        out_specs=[vmem] * len(ends),
+        compiler_params=pltpu.CompilerParams(vmem_limit_bytes=VMEM_BYTES),
+    )(*results)
+    named = dict(zip(ends, last))
+    named["mix_o"], named["ffn_o"] = named["mix_o"].reshape(d), named["ffn_o"].reshape(d)
+    return tuple(named.values())
+
+
 def solution(mesh):
     in_specs = (
         P(("seq", "ch"), None),
@@ -373,4 +1342,4 @@
         P("seq", "ch"),
         P("ch", "seq"),
     )
-    return jax.shard_map(body, mesh=mesh, in_specs=in_specs, out_specs=out_specs, check_vma=False)
+    return jax.shard_map(gathered_body if mesh.shape['seq'] == 8 else body, mesh=mesh, in_specs=in_specs, out_specs=out_specs, check_vma=False)

time: 2550 us -> 255 us (0.10)
  waiting for transfers between devices: 1810 us -> 0 us
  local copies, waits for them, and re-layouts: 329 us -> 2.61 us
  Pallas kernels: 0 us -> 251 us
  blocking collectives: 152 us -> 0 us
  other arithmetic: 128 us -> 0 us
  matrix products: 86.8 us -> 0 us
    reduce_scatter x12 -> x0, waiting for transfers between devices: 1180 us -> none  [the longest x1 211 us: body(): lax.psum_scatter(down_weight_grad, 'seq', scatter_dimension=1, tiled=True)]
    unnamed x25 -> x0, waiting for transfers between devices: 263 us -> none
    pallas_call x0 -> x2, Pallas kernels: none -> 251 us  [the longest x1 243 us: gathered_body(): pl.pallas_call(functools.partial(block_kernel, (n_seq, n_ch, rows, d, slo...]
    all_gather x2 -> x0, waiting for transfers between devices: 237 us -> none  [the longest x1 145 us: body(): lax.all_gather(stacked, 'seq', axis=0, tiled=True)]
    slice x100 -> x0, local copies, waits for them, and re-layouts: 164 us -> none  [the longest x49 82.2 us: body(): lax.associative_scan(affine, (jnp.flip(following, 0), jnp.flip(state_grad...]
    all_gather x8 -> x0, blocking collectives: 152 us -> none  [the longest x4 122 us: entering_2(): everything = jax.tree.map(lambda part: lax.all_gather(part, axis), shard)]
    psum x1 -> x0, waiting for transfers between devices: 128 us -> none  [body(): lax.psum((finals_wide, mix_gain_part, ffn_gain_part), ('seq', 'ch'))]
    pad x48 -> x0, local copies, waits for them, and re-layouts: 98.2 us -> none  [the longest x24 50 us: body(): lax.associative_scan(affine, (carry_factor, source), axis=0)]
  transfers between devices with their start and end apart: 22 -> 0, of which waited for: 21 -> 0; matrix products, arithmetic and copies ran while one was open for 4% -> 0% of each run, Pallas kernels for 0% -> 0%
where the time goes in v3:
time: 255 us
  Pallas kernels  251 us (98%)
  local copies, waits for them, and re-layouts  2.61 us (1%)
    pallas_call x1, Pallas kernels, gathered_body(): pl.pallas_call(functools.partial(block_kernel, (n_seq, n_ch, rows, d, slo...  243 us
    pallas_call x1, Pallas kernels, gathered_body(): pl.pallas_call(functools.partial(finish_kernel, list(outputs) + list(ends...  7.9 us

profile of v3, /device:TPU:0, one launch (start us, length us, event | category | flops | bytes accessed | tf_op | source)
XLA Modules:
  0.0 254.9 jit_solution(4692604445501830568)
XLA Ops:
  1.3 1.3 copy.38.refs_5_
  2.6 243.1 %shard_map.331 = (bf16[3,1024,768]{2,1,0:T(8,128)(2,1)}, bf16[2,8,4,32,256]{4,3,2,1,0:T(8,128)(2,1)}, bf16[3,1536,256]{2,1,0:T(8,128)(2,1)}, f32[5,3072]{1,0:T(8...) custom-call(bf16[32,2048]{1,0:T(8,128)(2,1)} %refs_0_.1, ...), custom_call_target="tpu_custom_call" | custom-call | tf_op jit(solution)/shard_map/pallas_call | solution.py:1271
  245.7 7.9 %shard_map.332 = (f32[5,3072]{1,0:T(8,128)}, bf16[32,2048]{1,0:T(8,128)(2,1)}, f32[32,2048]{1,0:T(8,128)}, f32[16,128]{1,0:T(8,128)}, f32[256,768]{1,0:T(8,128)}...) custom-call(bf16[3,1024,768]{2,1,0:T(8,128)(2,1)} %get-tuple-element, ...), custom_call_target="tpu_custom_call" | custom-call | tf_op jit(solution)/shard_map/pallas_call | solution.py:1290
  253.6 1.3 copy.39

commit v4 on v3

v4 whole, which is shorter than its diff:
```python
import functools
import math
import types

import jax
import jax.numpy as jnp
from jax import lax
from jax.experimental import pallas as pl
from jax.experimental.pallas import tpu as pltpu
from jax.sharding import PartitionSpec as P

EPS = 1e-06
HIGH = lax.Precision.HIGHEST
MESH = pl.DeviceIdType.MESH
SEQ = "seq"
CH = "ch"
K1 = 0.7978845608028654
K2 = 0.044715
VMEM_BYTES = 63 * 2**20
TILE = 1024
SEND_SEMS = 96
RECV_SEMS = 128
LOCAL_SEMS = 46


def passed_along(shard, axis, by):
    length = lax.axis_size(axis)
    pairs = [(i, i + by) for i in range(length) if 0 <= i + by < length]
    return lax.ppermute(shard, axis, pairs)


def entering_2(shard, axis, combine, identity, reverse):
    length, here = (lax.axis_size(axis), lax.axis_index(axis))
    everything = jax.tree.map(lambda part: lax.all_gather(part, axis), shard)
    start = jax.tree.map(
        lambda part, zero: jnp.broadcast_to(jnp.asarray(zero, part.dtype), part.shape),
        shard,
        identity,
    )

    def turn(k, before):
        at = length - 1 - k if reverse else k
        reached = at > here if reverse else at < here
        new = combine(before, jax.tree.map(lambda part: part[at], everything))
        return jax.tree.map(lambda a, b: jnp.where(reached, a, b), new, before)

    return lax.fori_loop(0, length, turn, start)


def normalize(values, gain):
    return values * lax.rsqrt(jnp.mean(values * values, axis=-1, keepdims=True) + EPS) * gain


def smooth(values):
    return jax.nn.gelu(values, approximate=True)


def affine(earlier, later):
    return (earlier[0] * later[0], later[0] * earlier[1] + later[1])


def doc_view(lengths, first, count):
    ends = jnp.cumsum(lengths)
    starts = ends - lengths
    position = first + jnp.arange(count, dtype=jnp.int32)
    owner = (position[:, None] >= starts[None, :]) & (position[:, None] < ends[None, :])
    start_of = jnp.sum(jnp.where(owner, starts[None, :], 0), axis=1)
    offset = position - start_of
    opening = (owner & (offset[:, None] == 0)).astype(jnp.float32)
    closing = (owner & (position[:, None] == ends[None, :] - 1)).astype(jnp.float32)
    return (offset, opening, closing)


def coefficients(rate_pre, inlet_pre, conv_value, decay, init_rows, keep):
    rate = jax.nn.sigmoid(rate_pre)
    inlet = jax.nn.sigmoid(inlet_pre)
    log_decay = -8.0 * rate * jax.nn.softplus(decay)
    factor = jnp.exp(log_decay)
    scale = jnp.sqrt(-jnp.expm1(2.0 * log_decay))
    carry_factor = keep * factor
    source = scale * inlet * conv_value + (1.0 - keep) * factor * init_rows
    return (carry_factor, source)


def spread(values):
    return lax.all_gather(values, CH, axis=0, tiled=True)


def collect(terms):
    return lax.psum_scatter(terms, CH, scatter_dimension=0, tiled=True)


def contract_last(left, right):
    return lax.dot_general(
        left, right, (((1,), (1,)), ((), ())), preferred_element_type=jnp.float32
    )


def contract_first(left, right):
    return lax.dot_general(
        left, right, (((0,), (0,)), ((), ())), preferred_element_type=jnp.float32
    )


def body(
    stream,
    cotangent,
    mix_gain,
    gelu_weight,
    recur_weight,
    conv_taps,
    conv_bias,
    rate_weight,
    rate_bias,
    inlet_weight,
    inlet_bias,
    decay_param,
    init_states,
    out_weight,
    ffn_gain,
    gate_weight,
    up_weight,
    down_weight,
    doc_lengths,
    block_counts,
):
    slot_count = rate_weight.shape[0]
    block_width = rate_weight.shape[1]
    local_width = slot_count * block_width
    taps = conv_taps.shape[0]
    token_count = stream.shape[0] * lax.axis_size(CH)
    hidden_width = gate_weight.shape[1]
    base = lax.axis_index(SEQ) * token_count
    offset_all, opening, closing = doc_view(doc_lengths, base, token_count + taps - 1)
    offset = offset_all[:token_count]
    opening = opening[:token_count]
    closing = closing[:token_count]
    keep = (offset > 0).astype(jnp.float32)[:, None]
    slot_live = (jnp.arange(slot_count, dtype=jnp.int32) < block_counts[0]).astype(jnp.float32)
    live = jnp.repeat(slot_live, block_width)[None, :]
    taps_flat = conv_taps.reshape(taps, local_width)
    decay_flat = decay_param.reshape(1, local_width)
    stream_float = stream.astype(jnp.float32)
    mix_low = normalize(stream_float, mix_gain).astype(jnp.bfloat16)
    mix_full = spread(mix_low)
    gelu_pre = jnp.dot(mix_full, gelu_weight, preferred_element_type=jnp.float32)
    recur_low = jnp.dot(mix_full, recur_weight, preferred_element_type=jnp.float32).astype(
        jnp.bfloat16
    )
    rim = passed_along(recur_low[token_count - taps + 1 :], SEQ, 1)
    extended = jnp.concatenate([rim, recur_low], axis=0).astype(jnp.float32)
    conv_pre = conv_bias.reshape(1, local_width)
    for tap_index in range(taps):
        valid = (offset >= tap_index).astype(jnp.float32)[:, None]
        lead = taps - 1 - tap_index
        conv_pre = (
            conv_pre + taps_flat[tap_index][None, :] * extended[lead : lead + token_count] * valid
        )
    conv_low = conv_pre.astype(jnp.bfloat16)
    conv_value = conv_low.astype(jnp.float32)
    grouped = conv_low.reshape(token_count, slot_count, block_width)
    rate_pre = (
        jnp.einsum("rsi,sio->rso", grouped, rate_weight, preferred_element_type=jnp.float32)
        + rate_bias[None]
    ).reshape(token_count, local_width)
    inlet_pre = (
        jnp.einsum("rsi,sio->rso", grouped, inlet_weight, preferred_element_type=jnp.float32)
        + inlet_bias[None]
    ).reshape(token_count, local_width)
    init_rows = jnp.dot(opening, init_states, precision=HIGH)
    carry_factor, source = coefficients(
        rate_pre, inlet_pre, conv_value, decay_flat, init_rows, keep
    )
    cumulative, local_state = lax.associative_scan(affine, (carry_factor, source), axis=0)
    summary = (cumulative[-1], local_state[-1])
    entering = entering_2(
        summary, SEQ, affine, (jnp.ones_like(summary[0]), jnp.zeros_like(summary[1])), False
    )
    state_in = entering[1]
    state = local_state + cumulative * state_in[None, :]
    gelu_value = smooth(gelu_pre)
    product_low = (gelu_value * state * live).astype(jnp.bfloat16)
    branch = collect(jnp.dot(product_low, out_weight, preferred_element_type=jnp.float32))
    middle = stream_float + branch
    ffn_low = normalize(middle, ffn_gain).astype(jnp.bfloat16)
    ffn_full = spread(ffn_low)
    stacked = jnp.concatenate([gate_weight, up_weight], axis=1)
    columns = ffn_full
    gate_up = jnp.dot(
        columns,
        lax.all_gather(stacked, SEQ, axis=0, tiled=True),
        preferred_element_type=jnp.float32,
    )
    gate = gate_up[:, :hidden_width]
    upward = gate_up[:, hidden_width:]
    hidden = (smooth(gate) * upward).astype(jnp.bfloat16)
    ffn_terms = jnp.dot(
        hidden,
        lax.all_gather(down_weight, SEQ, axis=1, tiled=True),
        preferred_element_type=jnp.float32,
    )
    mixed_out = (middle + collect(ffn_terms)).astype(jnp.bfloat16)
    out_grad_full = spread(cotangent)
    columns = out_grad_full
    hidden_grad = contract_last(columns, lax.all_gather(down_weight, SEQ, axis=1, tiled=True))
    down_weight_grad = contract_first(hidden, out_grad_full)
    unused, pair_pull = jax.vjp(lambda left, right: smooth(left) * right, gate, upward)
    gate_grad, up_grad = pair_pull(hidden_grad)
    pair_low = jnp.concatenate([gate_grad, up_grad], axis=1).astype(jnp.bfloat16)
    pair_weight_grad = contract_first(ffn_full, pair_low)
    norm_ffn_part = contract_last(pair_low, lax.all_gather(stacked, SEQ, axis=0, tiled=True))
    norm_ffn_grad = collect(norm_ffn_part)
    unused, ffn_norm_pull = jax.vjp(normalize, middle, ffn_gain)
    middle_norm_grad, ffn_gain_part = ffn_norm_pull(norm_ffn_grad)
    middle_grad = cotangent.astype(jnp.float32) + middle_norm_grad
    branch_full = spread(middle_grad.astype(jnp.bfloat16))
    out_weight_grad = contract_first(product_low, branch_full)
    product_grad = contract_last(branch_full, out_weight)
    state_grad = product_grad * gelu_value * live
    unused, gelu_pull = jax.vjp(smooth, gelu_pre)
    gelu_low = gelu_pull(product_grad * state * live)[0].astype(jnp.bfloat16)
    following = jnp.concatenate([carry_factor[1:], jnp.ones_like(carry_factor[:1])], axis=0)
    cum_back, adjoint_local = lax.associative_scan(
        affine, (jnp.flip(following, 0), jnp.flip(state_grad, 0)), axis=0
    )
    cum_back = jnp.flip(cum_back, 0)
    adjoint_local = jnp.flip(adjoint_local, 0)
    summary_back = (carry_factor[0] * cum_back[0], carry_factor[0] * adjoint_local[0])
    arriving = entering_2(
        summary_back,
        SEQ,
        affine,
        (jnp.ones_like(summary_back[0]), jnp.zeros_like(summary_back[1])),
        True,
    )
    adjoint_in = arriving[1]
    adjoint = adjoint_local + cum_back * adjoint_in[None, :]
    previous_state = jnp.concatenate([state_in[None, :], state[:-1]], axis=0)

    def local_coefficients(rate_value, inlet_value, conv_part, decay_value):
        return coefficients(rate_value, inlet_value, conv_part, decay_value, init_rows, keep)

    unused, coefficient_pull = jax.vjp(
        local_coefficients, rate_pre, inlet_pre, conv_value, decay_flat
    )
    rate_grad, inlet_grad, conv_direct, decay_part = coefficient_pull(
        (adjoint * previous_state, adjoint)
    )
    rate_low = rate_grad.astype(jnp.bfloat16).reshape(token_count, slot_count, block_width)
    inlet_low = inlet_grad.astype(jnp.bfloat16).reshape(token_count, slot_count, block_width)
    rate_weight_grad = jnp.einsum(
        "rsi,rso->sio", grouped, rate_low, preferred_element_type=jnp.float32
    )
    inlet_weight_grad = jnp.einsum(
        "rsi,rso->sio", grouped, inlet_low, preferred_element_type=jnp.float32
    )
    rate_bias_grad = jnp.sum(rate_low.astype(jnp.float32), axis=0)
    inlet_bias_grad = jnp.sum(inlet_low.astype(jnp.float32), axis=0)
    conv_back = jnp.einsum(
        "rso,sio->rsi", rate_low, rate_weight, preferred_element_type=jnp.float32
    )
    conv_back = conv_back + jnp.einsum(
        "rso,sio->rsi", inlet_low, inlet_weight, preferred_element_type=jnp.float32
    )
    conv_low_grad = (conv_direct + conv_back.reshape(token_count, local_width)).astype(jnp.bfloat16)
    rim_back = passed_along(conv_low_grad[: taps - 1], SEQ, -1)
    ahead = jnp.concatenate([conv_low_grad, rim_back], axis=0).astype(jnp.float32)
    own_grad = ahead[:token_count]
    recur_grad = jnp.zeros((token_count, local_width), jnp.float32)
    tap_grads = []
    for tap_index in range(taps):
        lead = taps - 1 - tap_index
        valid_here = (offset >= tap_index).astype(jnp.float32)[:, None]
        tap_grads.append(
            jnp.sum(own_grad * extended[lead : lead + token_count] * valid_here, axis=0)
        )
        valid_ahead = (offset_all[tap_index : tap_index + token_count] >= tap_index).astype(
            jnp.float32
        )[:, None]
        recur_grad = (
            recur_grad
            + taps_flat[tap_index][None, :]
            * ahead[tap_index : tap_index + token_count]
            * valid_ahead
        )
    conv_taps_grad = jnp.stack(tap_grads, axis=0).reshape(taps, slot_count, block_width)
    conv_bias_grad = jnp.sum(own_grad, axis=0).reshape(slot_count, block_width)
    recur_low_grad = recur_grad.astype(jnp.bfloat16)
    gelu_weight_grad = contract_first(mix_full, gelu_low)
    recur_weight_grad = contract_first(mix_full, recur_low_grad)
    norm_mix_part = contract_last(gelu_low, gelu_weight) + contract_last(
        recur_low_grad, recur_weight
    )
    norm_mix_grad = collect(norm_mix_part)
    unused, mix_norm_pull = jax.vjp(normalize, stream_float, mix_gain)
    stream_norm_grad, mix_gain_part = mix_norm_pull(norm_mix_grad)
    stream_grad = middle_grad + stream_norm_grad
    finals_local = lax.dot_general(closing, state * live, (((0,), (0,)), ((), ())), precision=HIGH)
    finals_wide = jnp.zeros((finals_local.shape[0], local_width * lax.axis_size(CH)), jnp.float32)
    finals_wide = lax.dynamic_update_slice(
        finals_wide, finals_local, (jnp.int32(0), lax.axis_index(CH) * local_width)
    )
    final_states, mix_gain_grad, ffn_gain_grad = lax.psum(
        (finals_wide, mix_gain_part, ffn_gain_part), (SEQ, CH)
    )
    summed = (
        lax.psum_scatter(gelu_weight_grad, SEQ, scatter_dimension=0, tiled=True),
        lax.psum_scatter(recur_weight_grad, SEQ, scatter_dimension=0, tiled=True),
        lax.psum_scatter(conv_taps_grad, SEQ, scatter_dimension=2, tiled=True),
        lax.psum_scatter(conv_bias_grad, SEQ, scatter_dimension=1, tiled=True),
        lax.psum_scatter(rate_weight_grad, SEQ, scatter_dimension=1, tiled=True),
        lax.psum_scatter(rate_bias_grad, SEQ, scatter_dimension=1, tiled=True),
        lax.psum_scatter(inlet_weight_grad, SEQ, scatter_dimension=1, tiled=True),
        lax.psum_scatter(inlet_bias_grad, SEQ, scatter_dimension=1, tiled=True),
        lax.psum_scatter(
            decay_part.reshape(slot_count, block_width), SEQ, scatter_dimension=1, tiled=True
        ),
        lax.psum_scatter(out_weight_grad, SEQ, scatter_dimension=1, tiled=True),
        lax.psum_scatter(
            pair_weight_grad[:, :hidden_width], SEQ, scatter_dimension=0, tiled=True
        ),
        lax.psum_scatter(
            pair_weight_grad[:, hidden_width:], SEQ, scatter_dimension=0, tiled=True
        ),
        lax.psum_scatter(down_weight_grad, SEQ, scatter_dimension=1, tiled=True),
    )
    return (
        final_states,
        mixed_out,
        stream_grad,
        mix_gain_grad,
        summed[0],
        summed[1],
        summed[2],
        summed[3],
        summed[4],
        summed[5],
        summed[6],
        summed[7],
        summed[8],
        summed[9],
        ffn_gain_grad,
        summed[10],
        summed[11],
        summed[12],
    )


class Net:
    def __init__(self, n_seq, n_ch, rows, send_sems, recv_sems, local_sems):
        self.n_seq, self.n_ch, self.rows = n_seq, n_ch, rows
        self.n_z = n_seq // 2
        self.send_sems, self.recv_sems, self.local_sems = send_sems, recv_sems, local_sems
        self.tags, self.used, self.sent, self.locals = {}, 0, [], 0
        self.s, self.c = lax.axis_index(SEQ), lax.axis_index(CH)
        s, c, n_z = self.s, self.c, self.n_z
        self.z, self.x, self.y, self.core = s // 2, s % 2, c // 2, c % 2
        x, y = self.x, self.y
        self.s_to = [(s + k) % n_seq for k in range(n_seq)]
        self.s_from = [(s + n_seq - k) % n_seq for k in range(n_seq)]
        self.sibling = self.dev(self.z, x, y, 1 - self.core)
        self.across = self.dev(self.z, x, 1 - y, self.core)
        self.beside = self.dev(self.z, 1 - x, y, self.core)
        self.above = self.dev((self.z + 1) % n_z, x, y, self.core)
        self.below = self.dev((self.z + n_z - 1) % n_z, x, y, self.core)

    def nearest(self):
        order = [self.z * 2 + 1 - self.x]
        for at in range(1, self.n_z):
            there = self.z_of(self.slot(at))
            order += [there * 2 + self.x, there * 2 + 1 - self.x]
        return order

    def dev(self, z, x, y, core):
        return (z * 2 + x, y * 2 + core)

    def block(self, z, x, y, core):
        rows = self.rows
        return pl.multiple_of(((z * 2 + x) * self.n_ch + y * 2 + core) * rows, rows)

    def z_of(self, slot):
        return (self.z + self.n_z - slot) % self.n_z

    def slot(self, at):
        if at == 0:
            return 0
        n_z, z = self.n_z, self.z
        low, high = (n_z - 1 - z) // (n_z - 1), z // (n_z - 1)
        inner = (at + 1) // 2 if at % 2 else n_z - at // 2
        return low * (n_z - at) + high * at + (1 - low - high) * inner

    def greet(self, peers):
        barrier = pltpu.get_barrier_semaphore()
        for peer in peers:
            pl.semaphore_signal(barrier, inc=1, device_id=peer, device_id_type=MESH)

    def meet(self, peers):
        pl.semaphore_wait(pltpu.get_barrier_semaphore(), len(peers))

    def sem(self, tag, at=0, size=1):
        if tag not in self.tags:
            self.tags[tag] = self.used
            self.used += size
        return self.recv_sems.at[self.tags[tag] + at]

    def send(self, src, dst, to, sem, when=None):
        size = self.send_sems.shape[0]
        if len(self.sent) >= size:
            self.sent_wait(len(self.sent) - size)
        copy = pltpu.make_async_remote_copy(
            src_ref=src, dst_ref=dst, send_sem=self.send_sems.at[len(self.sent) % size], recv_sem=sem,
            device_id=to, device_id_type=MESH,
        )
        if when is None:
            copy.start()
        else:
            @pl.when(when)
            def _():
                copy.start()
        self.sent.append((copy, when))

    def sent_wait(self, at):
        if self.sent[at] is None:
            return
        copy, when = self.sent[at]
        self.sent[at] = None
        if when is None:
            copy.wait_send()
        else:
            @pl.when(when)
            def _():
                copy.wait_send()

    def recv(self, view, sem):
        pltpu.make_async_remote_copy(
            src_ref=view, dst_ref=view, send_sem=self.send_sems.at[0], recv_sem=sem,
            device_id=(self.s, self.c), device_id_type=MESH,
        ).wait_recv()

    def local(self, src, dst):
        copy = pltpu.make_async_copy(src, dst, self.local_sems.at[self.locals])
        self.locals += 1
        copy.start()
        return copy

    def drain(self):
        for at in range(len(self.sent)):
            self.sent_wait(at)

    def ch_gather_start(self, view_of, tag):
        mine = view_of(self.c)
        self.send(mine, mine, self.across, self.sem((tag, "y")))
        self.send(mine, mine, self.sibling, self.sem((tag, "core")))

    def ch_gather_finish(self, view_of, tag):
        y, core = self.y, self.core
        theirs = view_of((1 - y) * 2 + core)
        self.recv(theirs, self.sem((tag, "y")))
        self.send(theirs, theirs, self.sibling, self.sem((tag, "fwd")))
        self.recv(view_of(y * 2 + 1 - core), self.sem((tag, "core")))
        self.recv(view_of((1 - y) * 2 + 1 - core), self.sem((tag, "fwd")))

    def ch_sum(self, part, mid, low, far, tag):
        y, core = self.y, self.core
        first = len(self.sent)
        self.send(part.at[1 - core], mid, self.sibling, self.sem((tag, "core")))
        self.recv(mid, self.sem((tag, "core")))
        low[...] = (part[core, 1 - y] + mid[1 - y]).astype(jnp.bfloat16)
        self.send(low, far, self.across, self.sem((tag, "y")))
        total = part[core, y] + mid[y]
        self.recv(far, self.sem((tag, "y")))
        self.sent_wait(first)
        self.sent_wait(first + 1)
        return total + far[...].astype(jnp.float32)

    def chain_start(self, mine, target, tag):
        n_z, z = self.n_z, self.z
        self.send(mine, target, self.above, self.sem((tag, "z"), 1, n_z), z < n_z - 1)
        self.send(mine, target, self.below, self.sem((tag, "z"), n_z - 1, n_z), z > 0)

    def chain_arrive(self, view, slot, tag):
        n_z, z = self.n_z, self.z
        self.recv(view, self.sem((tag, "z"), slot, n_z))
        self.send(view, view, self.above, self.sem((tag, "z"), (slot + 1) % n_z, n_z), (z >= slot) & (z < n_z - 1))
        self.send(view, view, self.below, self.sem((tag, "z"), (slot + n_z - 1) % n_z, n_z), (z < slot) & (z > 0))


class Spread:
    def __init__(self, net, ref, tag):
        self.net, self.ref, self.tag = net, ref, tag

    def view(self, slot, x, y, core):
        net = self.net
        return self.ref.at[pl.ds(net.block(net.z_of(slot), x, y, core), net.rows)]

    def sem(self, what, slot):
        return self.net.sem((self.tag, what), slot, self.net.n_z)

    def start(self):
        net = self.net
        mine = self.view(0, net.x, net.y, net.core)
        net.chain_start(mine, mine, self.tag)
        self.plane(0)

    def plane(self, slot):
        net = self.net
        view = self.view(slot, net.x, net.y, net.core)
        net.send(view, view, net.beside, self.sem("x", slot))
        net.send(view, view, net.across, self.sem("y", slot))
        net.send(view, view, net.sibling, self.sem("s", slot))

    def arrive(self, slot):
        net = self.net
        net.chain_arrive(self.view(slot, net.x, net.y, net.core), slot, self.tag)
        self.plane(slot)

    def relay(self, slot):
        net = self.net
        view = self.view(slot, 1 - net.x, net.y, net.core)
        net.recv(view, self.sem("x", slot))
        net.send(view, view, net.across, self.sem("d", slot))
        net.send(view, view, net.sibling, self.sem("s", slot))

    def relay_far(self, slot):
        net = self.net
        for what, x in (("y", net.x), ("d", 1 - net.x)):
            view = self.view(slot, x, 1 - net.y, net.core)
            net.recv(view, self.sem(what, slot))
            net.send(view, view, net.sibling, self.sem("s", slot))

    def done(self, slot):
        net = self.net
        at = net.block(net.z_of(slot), 0, 0, 0)
        net.recv(self.ref.at[pl.ds(at, 4 * net.rows)], self.sem("s", slot))


class Collect:
    def __init__(self, net, part, sib, far, side, along, tag):
        self.net, self.part, self.sib, self.far, self.side, self.along, self.tag = net, part, sib, far, side, along, tag

    def sem(self, what, at):
        return self.net.sem((self.tag, what), at, self.net.n_z)

    def first(self, at):
        net = self.net
        net.send(self.part.at[at, 1 - net.core], self.sib.at[at], net.sibling, self.sem("s", at))

    def second(self, at):
        net = self.net
        net.recv(self.sib.at[at], self.sem("s", at))
        core, part, sib = net.core, self.part, self.sib
        for first in (1 - net.y, net.y):
            for x in range(2):
                value = part[at, core, first, x].astype(jnp.float32) + sib[at, first, x].astype(jnp.float32)
                part[at, core, first, x] = value.astype(jnp.bfloat16)
            if first is not net.y:
                net.send(part.at[at, core, first], self.far.at[at], net.across, self.sem("f", at))

    def third(self, at):
        net, part, far = self.net, self.part, self.far
        net.recv(far.at[at], self.sem("f", at))
        there = 1 - net.x
        value = part[at, net.core, net.y, there].astype(jnp.float32) + far[at, there].astype(jnp.float32)
        part[at, net.core, net.y, there] = value.astype(jnp.bfloat16)
        net.send(part.at[at, net.core, net.y, there], self.side.at[at], net.beside, self.sem("p", at))

    def plane_total(self, at):
        net = self.net
        net.recv(self.side.at[at], self.sem("p", at))
        total = self.part[at, net.core, net.y, net.x].astype(jnp.float32)
        return total + self.far[at, net.x].astype(jnp.float32) + self.side[at].astype(jnp.float32)

    def fourth(self, at):
        net, part = self.net, self.part
        total = self.plane_total(at)
        if at == 0:
            return total
        slot = net.slot(at)
        part[at, net.core, net.y, net.x] = total.astype(jnp.bfloat16)
        net.send(
            part.at[at, net.core, net.y, net.x], self.along.at[slot],
            net.dev(net.z_of(slot), net.x, net.y, net.core), net.sem((self.tag, "z")),
        )
        return None

    def total(self, own):
        net = self.net
        net.recv(self.along.at[pl.ds(1, net.n_z - 1)], net.sem((self.tag, "z")))
        for slot in range(1, net.n_z):
            own = own + self.along[slot].astype(jnp.float32)
        return own


class CollectEven(Collect):
    def second(self, at):
        net = self.net
        net.recv(self.sib.at[at], self.sem("s", at))
        core, part, sib = net.core, self.part, self.sib
        half = net.rows // 2
        for y in (1 - net.y, net.y):
            for x in (1 - net.x, net.x):
                value = part[at, core, y, x].astype(jnp.float32) + sib[at, y, x].astype(jnp.float32)
                part[at, core, y, x] = value.astype(jnp.bfloat16)
                if y is not net.y and x is not net.x:
                    diagonal = part.at[at, core, y, x]
                    net.send(diagonal.at[pl.ds(0, half)], self.far.at[at, 0], net.beside, self.sem("f0", at))
                    net.send(diagonal.at[pl.ds(half, half)], self.far.at[at, 1], net.across, self.sem("f1", at))

    def third(self, at):
        net, part, far = self.net, self.part, self.far
        half = net.rows // 2
        for which, y, x, first, to in (
            (0, 1 - net.y, net.x, 0, net.across), (1, net.y, 1 - net.x, half, net.beside),
        ):
            net.recv(far.at[at, which], self.sem(f"f{which}", at))
            rows = pl.ds(first, half)
            value = part[at, net.core, y, x, rows, :].astype(jnp.float32) + far[at, which].astype(jnp.float32)
            part[at, net.core, y, x, rows, :] = value.astype(jnp.bfloat16)
            net.send(part.at[at, net.core, y, x], self.side.at[at, which], to, self.sem("p", at))

    def plane_total(self, at):
        net = self.net
        net.recv(self.side.at[at], self.sem("p", at))
        total = self.part[at, net.core, net.y, net.x].astype(jnp.float32)
        return total + self.side[at, 0].astype(jnp.float32) + self.side[at, 1].astype(jnp.float32)


def stack_rows(rows):
    return jnp.concatenate(rows, axis=0)


def smooth_pair(v):
    t = jnp.tanh(K1 * (v + K2 * v * v * v))
    value = 0.5 * v * (1.0 + t)
    slope = 0.5 * (1.0 + t) + 0.5 * v * (1.0 - t * t) * K1 * (1.0 + 3.0 * K2 * v * v)
    return value, slope


def sigmoid(v):
    return 1.0 / (1.0 + jnp.exp(-v))


def softplus_exact(d):
    u = jnp.exp(-jnp.abs(d))
    r = u / (2.0 + u)
    q = r * r
    series = 1.0 / 15.0
    for k in (13, 11, 9, 7, 5, 3, 1):
        series = series * q + 1.0 / k
    return jnp.maximum(d, 0.0) + 2.0 * r * series


def minus_expm1(v):
    series = 1.0 / 362880.0
    for k in (40320.0, 5040.0, 720.0, 120.0, 24.0, 6.0, 2.0, 1.0):
        series = series * v + 1.0 / k
    return jnp.where(v > -0.5, -v * series, 1.0 - jnp.exp(v))


class Docs:
    def __init__(self, lengths, first, count, before=0):
        position = first - before + lax.broadcasted_iota(jnp.int32, (count, 1), 0)
        self.opening, self.closing = [], []
        start_of = jnp.zeros((count, 1), jnp.int32)
        start = jnp.int32(0)
        for e in range(lengths.shape[0]):
            end = start + lengths[e]
            owner = (position >= start) & (position < end)
            start_of = jnp.where(owner, start, start_of)
            self.opening.append((position == start).astype(jnp.float32))
            self.closing.append((position == end - 1).astype(jnp.float32))
            start = end
        self.offset = position - start_of
        self.keep = (self.offset > 0).astype(jnp.float32)

    def valid(self, k):
        return (self.offset >= k).astype(jnp.float32)


def prefix(a, b, count):
    row = lax.broadcasted_iota(jnp.int32, a.shape, 0)
    k = 1
    while k < count:
        inside = row >= k
        a_far = jnp.where(inside, pltpu.roll(a, k, 0), 1.0)
        b_far = jnp.where(inside, pltpu.roll(b, k, 0), 0.0)
        b = a * b_far + b
        a = a * a_far
        k *= 2
    return a, b


def suffix(a, b, count):
    row = lax.broadcasted_iota(jnp.int32, a.shape, 0)
    k = 1
    while k < count:
        inside = row < count - k
        a_far = jnp.where(inside, pltpu.roll(a, count - k, 0), 1.0)
        b_far = jnp.where(inside, pltpu.roll(b, count - k, 0), 0.0)
        b = a * b_far + b
        a = a * a_far
        k *= 2
    return a, b


def coefficient_parts(rate_pre, inlet_pre, decay):
    rate = sigmoid(rate_pre)
    inlet = sigmoid(inlet_pre)
    sp = softplus_exact(decay)
    log_decay = -8.0 * rate * sp
    factor = jnp.exp(log_decay)
    scale = jnp.sqrt(minus_expm1(2.0 * log_decay))
    return rate, inlet, sp, log_decay, factor, scale


def opening_rows(docs, init):
    total = docs.opening[0] * init[0:1]
    for e in range(1, len(docs.opening)):
        total = total + docs.opening[e] * init[e : e + 1]
    return total


def pack_gain(row):
    tiles = [row[:, i * 128 : (i + 1) * 128] for i in range(row.shape[1] // 128)]
    return jnp.concatenate([stack_rows(tiles[i : i + 8]) for i in range(0, len(tiles), 8)], axis=1)


def norm_back(values, gain, grad):
    r = lax.rsqrt(jnp.mean(values * values, axis=-1, keepdims=True) + EPS)
    u = grad * gain
    to_values = r * u - values * (r * r * r) * jnp.mean(u * values, axis=-1, keepdims=True)
    to_gain = jnp.sum(grad * values * r, axis=0, keepdims=True)
    return to_values, to_gain


def unit(size):
    row = lax.broadcasted_iota(jnp.int32, (size, size), 0)
    column = lax.broadcasted_iota(jnp.int32, (size, size), 1)
    return jnp.where(row == column, 1.0, 0.0).astype(jnp.bfloat16)


RIM = 16


def block_kernel(sizes, names, *refs):
    n_seq, n_ch, rows, d, slots, bw, width, sl = sizes
    r = types.SimpleNamespace(**dict(zip(names, refs)))
    bf, f32 = jnp.bfloat16, jnp.float32
    net = Net(n_seq, n_ch, rows, r.send_sems, r.recv_sems, r.local_sems)
    s, c, x, y, z, core, n_z = net.s, net.c, net.x, net.y, net.z, net.core, net.n_z
    count, wide, tokens = rows * n_ch, slots * bw, rows * n_ch * n_seq
    n_taps = r.taps_v.shape[1]
    mine = net.block(z, x, y, core)
    seq_peers = [(net.s_to[k], c) for k in range(1, n_seq)]
    rim_peers = [(net.s_to[k], (c + i) % n_ch) for k in (1, n_seq - 1) for i in range(1, n_ch)]
    peers = seq_peers + rim_peers + [net.sibling, net.across]
    net.greet(peers)
    loads = {}
    cuts = dict(gelu_w=4, recur_w=4, out_w=4)

    def load_halves(name, dst):
        src, size = getattr(r, name), dst.shape[2]
        loads[name] = [net.local(src.at[:, pl.ds(i * size, size)], dst.at[i]) for i in range(2)]

    def load(name, n):
        src, dst = getattr(r, name), getattr(r, name + "_v")
        if n == 1:
            loads[name] = [net.local(src, dst)]
            return
        size = src.shape[0] // n
        loads[name] = [
            net.local(src.at[pl.ds(i * size, size)], dst.at[pl.ds(i * size, size)])
            for i in range(n)
        ]

    def loaded(name):
        for copy in loads.pop(name):
            copy.wait()

    load("stream", 1)
    load("mix_gain", 1)
    load_halves("gate_w", r.give)
    load("cot", 1)
    load_halves("up_w", r.take)
    for name in ("gelu_w", "recur_w", "taps", "bias", "rate_w", "rate_b",
                 "inlet_w", "inlet_b", "decay", "init", "out_w", "ffn_gain"):
        load(name, cuts.get(name, 1))

    own_cols = pl.ds(pl.multiple_of(s * width, width), width)
    own_count = pl.ds(pl.multiple_of(s * count, count), count)
    own_slice = pl.ds(pl.multiple_of(s * sl, sl), sl)
    local = []

    loaded("stream")
    loaded("mix_gain")
    values = r.stream_v[...].astype(f32)
    scale = lax.rsqrt(jnp.mean(values * values, axis=-1, keepdims=True) + EPS)
    mix_rows = pl.ds(pl.multiple_of(RIM + c * rows, 16), rows)
    r.mix[mix_rows, :] = (values * scale * r.mix_gain_v[...][None, :]).astype(bf)

    loaded("cot")
    r.cfull[pl.ds(mine, rows), :] = r.cot_v[...]

    def turn(a, src):
        half = src.shape[2]
        for i in range(2 * half // 256):
            at = i * 256 % half
            r.turned[a, i * 256 : (i + 1) * 256, :] = contract_first(
                src[i * 256 // half, :, at : at + 256], unit(src.shape[1])
            ).astype(bf)

    loaded("gate_w")
    turn(0, r.give)
    loaded("up_w")
    turn(1, r.take)
    net.meet(peers)

    def mix_of(cc):
        return r.mix.at[pl.ds(pl.multiple_of(RIM + cc * rows, 16), rows)]

    last, first = r.mix.at[pl.ds(count, RIM)], r.mix.at[pl.ds(0, RIM)]
    net.ch_gather_start(mix_of, "mix")
    for i in range(n_ch):
        net.send(last, first, (net.s_to[1], i), net.sem("rim"), (c == n_ch - 1) & (s < n_seq - 1))

    @pl.when(s == 0)
    def _():
        r.mix[pl.ds(0, RIM), :] = jnp.zeros((RIM, d), bf)

    cots = Spread(net, r.cfull, "cot")
    lows = Spread(net, r.full, "low")
    cots.start()

    pair_width = 2 * width

    def pair_cols(to):
        return pl.ds(pl.multiple_of(to * pair_width, pair_width), pair_width)

    def left_start(a, src):
        r.left[a, z, c] = src[:, pair_cols(z)]
        for at in range(1, n_z):
            to = net.z_of(net.slot(at))
            net.send(src.at[:, pair_cols(to)], r.left.at[a, z, c], net.dev(to, x, y, core), net.sem(("left", a)))

    def left_pass(a):
        net.recv(r.left.at[a, pl.ds(0, n_z - 1), c], net.sem(("left", a)))
        net.ch_gather_start(lambda cc: r.left.at[a, :, cc], ("leftch", a))

    def left_done(a):
        net.ch_gather_finish(lambda cc: r.left.at[a, :, cc], ("leftch", a))

    left_start(0, r.mix.at[mix_rows])

    others = net.nearest()

    def weight_start(a, which=None):
        src = r.turned.at[a] if a < 2 else r.down
        which = others if which is None else which
        for to in which:
            net.send(
                src.at[pl.ds(pl.multiple_of(to * sl, sl), sl)], r.wt.at[a, :, own_cols], (to, c), net.sem(("w", a)),
            )
        if which[-1] is others[-1]:
            local.append(net.local(src.at[own_slice], r.wt.at[a, :, own_cols]))

    def weight_done(a):
        net.recv(r.wt.at[a, :, pl.ds(0, (n_seq - 1) * width)], net.sem(("w", a)))
        local.pop(0).wait()

    weight_start(0, others[:2])
    for name in [name for name in loads if name != "out_w"]:
        loaded(name)

    net.ch_gather_finish(mix_of, "mix")
    cots.arrive(net.slot(1))
    for i in range(n_ch):
        @pl.when((s > 0) & (c == i))
        def _(i=i):
            net.recv(first, net.sem("rim"))

    docs = Docs(r.lengths, s * count, count)
    keep = docs.keep
    ends_a, ends_b = [], []
    for b in range(slots):
        cols = pl.ds(b * bw, bw)
        rowsof = r.mix[...]
        r.gelu[:, cols] = jnp.dot(rowsof[RIM:], r.gelu_w_v[:, cols], preferred_element_type=f32)
        recur = jnp.dot(rowsof, r.recur_w_v[:, cols], preferred_element_type=f32).astype(bf)
        r.recur[:, cols] = recur
        recur = recur.astype(f32)
        conv_pre = r.bias_v[b : b + 1, :]
        for k in range(n_taps):
            conv_pre = conv_pre + r.taps_v[b, k : k + 1, :] * recur[RIM - k : RIM - k + count] * docs.valid(k)
        conv_low = conv_pre.astype(bf)
        r.conv[:, cols] = conv_low
        rate_pre = jnp.dot(conv_low, r.rate_w_v[b], preferred_element_type=f32) + r.rate_b_v[b : b + 1, :]
        inlet_pre = jnp.dot(conv_low, r.inlet_w_v[b], preferred_element_type=f32) + r.inlet_b_v[b : b + 1, :]
        r.rate_pre[:, cols] = rate_pre
        r.inlet_pre[:, cols] = inlet_pre
        rate, inlet, sp, log_decay, factor, scale = coefficient_parts(rate_pre, inlet_pre, r.decay_v[b : b + 1, :])
        source = scale * inlet * conv_low.astype(f32) + (1.0 - keep) * factor * opening_rows(docs, r.init_v[:, cols])
        total, part = prefix(keep * factor, source, count)
        r.scan_a[:, cols] = total
        r.scan_b[:, cols] = part
        ends_a.append(total[count - 1 : count])
        ends_b.append(part[count - 1 : count])

    def exchange(summary, pieces, tag):
        summary[s] = stack_rows(pieces + [jnp.zeros((8 - 2 * slots, bw), f32)])
        for k in range(1, n_seq):
            net.send(summary.at[s], summary.at[s], (net.s_to[k], c), net.sem(tag))

    def exchanged(summary, tag):
        net.recv(summary.at[pl.ds(0, n_seq - 1)], net.sem(tag))

    exchange(r.summary, ends_a + ends_b, "sum")
    cots.arrive(net.slot(2))
    cots.relay(0)
    weight_start(0, others[2:])
    loaded("out_w")
    exchanged(r.summary, "sum")
    enter = jnp.zeros((slots, bw), f32)
    for q in range(n_seq - 1):
        after = r.summary[q, 0:slots] * enter + r.summary[q, slots : 2 * slots]
        enter = jnp.where(s > q, after, enter)
    finals = []
    for b in range(slots):
        cols = pl.ds(b * bw, bw)
        live = jnp.where(r.counts[0] > b, 1.0, 0.0)
        state = r.scan_b[:, cols] + r.scan_a[:, cols] * enter[b : b + 1]
        r.state[:, cols] = state
        value, _ = smooth_pair(r.gelu[:, cols])
        r.gath[0, z, :, cols] = (value * state * live).astype(bf)
        ends = [jnp.sum(mark * state, axis=0, keepdims=True) * live for mark in docs.closing]
        finals.append(stack_rows(ends + [jnp.zeros((8 - len(ends), bw), f32)]))

    def branch_tile(i, _):
        cols = pl.ds(pl.multiple_of(i * TILE, TILE), TILE)
        value = jnp.dot(r.gath[0, z], r.out_w_v[:, cols], preferred_element_type=f32)
        for cc in range(n_ch):
            r.part[cc % 2, cc // 2, :, cols] = value[cc * rows : (cc + 1) * rows]
        return 0

    lax.fori_loop(0, d // TILE, branch_tile, 0)
    middle = values + net.ch_sum(r.part, r.mid, r.ylow, r.yfar, "branch")
    scale = lax.rsqrt(jnp.mean(middle * middle, axis=-1, keepdims=True) + EPS)
    r.full[pl.ds(mine, rows), :] = (middle * scale * r.ffn_gain_v[...][None, :]).astype(bf)
    r.middle[...] = middle

    def gather_start(a):
        net.chain_start(r.gath.at[a, z], r.gath.at[a, z], ("g", a))

    def gather_arrive(a, at):
        slot = net.slot(at)
        net.chain_arrive(r.gath.at[a, net.z_of(slot)], slot, ("g", a))

    def gather_product(a):
        right = r.gath[a].reshape(n_z * count, wide)
        for which, there in ((0, 1 - x), (1, x)):
            half = r.left[1 if a == 0 else 0, :, :, :, pl.ds(pl.multiple_of(there * width, width), width)]
            half = half.reshape(n_z * count, width)
            value = contract_first(right, half) if a == 0 else contract_first(half, right)
            if which == 0:
                ref = r.give_out if a == 0 else r.give.at[a - 1]
                ref[...] = value.astype(bf)
                net.send(ref, r.take_out if a == 0 else r.take.at[a - 1], net.beside, net.sem(("take", a)))
            elif a == 0:
                r.keep_out_v[...] = value
                local.append(net.local(r.keep_out_v, r.keep_out))
            else:
                r.keep_v[a - 1] = value
                local.append(net.local(r.keep_v.at[a - 1], r.keep.at[a - 1]))

    def gather_done(a):
        ref = r.take_out if a == 0 else r.take.at[a - 1]
        net.recv(ref, net.sem(("take", a)))
        local.append(net.local(ref, r.took_out if a == 0 else r.took.at[a - 1]))

    lows.start()
    weight_start(1, others[:2])
    cots.relay(net.slot(1))
    lows.relay(0)
    lows.arrive(net.slot(1))
    weight_start(1, others[2:4])
    cots.relay(net.slot(2))
    lows.arrive(net.slot(2))
    cots.arrive(net.slot(3))
    weight_start(1, others[4:])
    lows.relay_far(0)
    lows.relay(net.slot(1))
    lows.relay(net.slot(2))
    lows.arrive(net.slot(3))
    weight_start(2)
    gather_start(0)
    group = n_ch * 2 * rows

    def chunk(at):
        return pl.ds(pl.multiple_of(net.z_of(net.slot(at)) * group, group), group)

    weight_done(0)
    weight_done(1)

    def forward(at):
        lows.done(net.slot(at))
        here = chunk(at)
        gate = contract_last(r.full[here, :], r.wt[0])
        up = contract_last(r.full[here, :], r.wt[1])
        value, slope = smooth_pair(gate)
        r.value[here, :] = value
        r.slope[here, :] = up * slope
        r.hid[here, :] = (value * up).astype(bf)

    lows.relay_far(net.slot(1))
    forward(0)
    lows.relay_far(net.slot(2))
    lows.relay(net.slot(3))
    forward(1)
    cots.relay(net.slot(3))
    forward(2)
    lows.relay_far(net.slot(3))
    for at in range(n_z):
        cots.relay_far(net.slot(at))
    forward(3)
    for at in range(n_z):
        cots.done(net.slot(at))

    def weight_grad(a, left, right):
        def tile(i, _):
            cols = pl.ds(pl.multiple_of(i * TILE, TILE), TILE)
            r.dwl[a, :, cols] = contract_first(left[...], right[:, cols]).astype(bf)
            return 0

        lax.fori_loop(0, d // TILE, tile, 0)

    def weight_grad_send(a, which=None):
        which = others if which is None else which
        for to in which:
            cols = pl.ds(pl.multiple_of(to * width, width), width)
            net.send(r.dwl.at[a, :, cols], r.dw.at[a, own_slice], (to, c), net.sem(("dw", a)))
        if which[-1] is others[-1]:
            local.append(net.local(r.dwl.at[a, :, own_cols], r.dw.at[a, own_slice]))

    def weight_grad_done(a):
        net.recv(r.dw.at[a, pl.ds(0, (n_seq - 1) * sl)], net.sem(("dw", a)))

    weight_grad(2, r.hid, r.cfull)
    weight_done(2)
    weight_grad_send(2)

    def spread_out(ref, at, value, cols):
        value = value.astype(bf)
        for xx in range(2):
            for yy in range(2):
                for cc in range(2):
                    row = (xx * 4 + yy * 2 + cc) * rows
                    ref[at, cc, yy, xx, :, cols] = value[row : row + rows]

    def backward(at):
        here = chunk(at)
        grad = contract_last(r.cfull[here, :], r.wt[2])
        r.gat[here, :] = (grad * r.slope[here, :]).astype(bf)
        r.upg[here, :] = (grad * r.value[here, :]).astype(bf)

        def tile(i, _):
            cols = pl.ds(pl.multiple_of(i * TILE, TILE), TILE)
            value = jnp.dot(r.gat[here, :], r.wt[0, :, cols], preferred_element_type=f32)
            value = value + jnp.dot(r.upg[here, :], r.wt[1, :, cols], preferred_element_type=f32)
            spread_out(r.npart, at, value, cols)
            return 0

        lax.fori_loop(0, d // TILE, tile, 0)

    def output(at):
        here = chunk(at)

        def tile(i, _):
            cols = pl.ds(pl.multiple_of(i * TILE, TILE), TILE)
            value = jnp.dot(r.hid[here, :], r.wt[2, :, cols], preferred_element_type=f32)
            spread_out(r.opart, at, value, cols)
            return 0

        lax.fori_loop(0, d // TILE, tile, 0)

    norms = CollectEven(net, r.npart, r.nsib, r.nfar, r.nside, r.nalong, "norm")
    outs = Collect(net, r.opart, r.osib, r.ofar, r.oside, r.oalong, "out")
    backward(3)
    norms.first(3)
    backward(2)
    norms.first(2)
    norms.second(3)
    backward(1)
    norms.first(1)
    norms.second(2)
    norms.third(3)
    backward(0)
    norms.first(0)
    norms.second(1)
    norms.third(2)
    norms.fourth(3)
    norms.second(0)
    output(3)
    output(2)
    norms.third(1)
    norms.fourth(2)
    output(1)
    output(0)
    norms.third(0)
    norms.fourth(1)
    for at in (3, 2, 1, 0):
        outs.first(at)
    gather_arrive(0, 1)
    weight_grad(0, r.gat, r.full)
    weight_grad(1, r.upg, r.full)
    own_norm = norms.fourth(0)
    left_pass(0)
    gather_arrive(0, 2)
    nfg = norms.total(own_norm)

    to_middle, ffn_part = norm_back(middle, r.ffn_gain_v[...][None, :], nfg)
    middle_grad = r.cot_v[...].astype(f32) + to_middle
    r.branch[c] = middle_grad.astype(bf)
    net.ch_gather_start(lambda cc: r.branch.at[cc], "bgrad")
    left_start(1, r.branch.at[c])
    weight_grad_send(0, others[:3])
    for at in (3, 2, 1, 0):
        outs.second(at)
    r.early[n_z] = jnp.concatenate(finals + [pack_gain(ffn_part)], axis=1)
    net.send(r.early.at[n_z], r.pair.at[0], net.beside, net.sem("pair", 0, 2))
    net.ch_gather_finish(lambda cc: r.branch.at[cc], "bgrad")

    ahead_docs = Docs(r.lengths, s * count, count + RIM)
    row = lax.broadcasted_iota(jnp.int32, (count, bw), 0)
    heads_a, heads_b = [], []
    for b in range(slots):
        cols = pl.ds(b * bw, bw)
        live = jnp.where(r.counts[0] > b, 1.0, 0.0)
        product_grad = contract_last(r.branch[...].reshape(count, d), r.out_w_v[b * bw : (b + 1) * bw, :])
        value, slope = smooth_pair(r.gelu[:, cols])
        r.gath[1, z, :, cols] = (product_grad * r.state[:, cols] * live * slope).astype(bf)
        rate, inlet, sp, log_decay, factor, scale = coefficient_parts(r.rate_pre[:, cols], r.inlet_pre[:, cols], r.decay_v[b : b + 1, :])
        carry = keep * factor
        following = jnp.where(row < count - 1, pltpu.roll(carry, count - 1, 0), 1.0)
        total, part = suffix(following, product_grad * value * live, count)
        r.scan_a[:, cols] = total
        r.scan_b[:, cols] = part
        heads_a.append(carry[0:1] * total[0:1])
        heads_b.append(carry[0:1] * part[0:1])
    exchange(r.summary_back, heads_a + heads_b, "sumback")

    gather_start(1)
    gather_arrive(0, 3)
    weight_grad_send(0, others[3:4])
    exchanged(r.summary_back, "sumback")

    def pair_sum(a, ref):
        net.recv(r.pair.at[a], net.sem("pair", a, 2))
        ref[z] = ref[n_z] + r.pair[a]
        for k in range(1, n_z):
            to = net.z_of(k)
            net.send(ref.at[z], ref.at[z], net.dev(to, x, y, core), net.sem(("vec", a)))

    pair_sum(0, r.early)
    enter_back = jnp.zeros((slots, bw), f32)
    for q in range(n_seq - 1, 0, -1):
        after = r.summary_back[q, 0:slots] * enter_back + r.summary_back[q, slots : 2 * slots]
        enter_back = jnp.where(s < q, after, enter_back)
    vec = []
    for b in range(slots):
        cols = pl.ds(b * bw, bw)
        adjoint = r.scan_b[:, cols] + r.scan_a[:, cols] * enter_back[b : b + 1]
        previous = jnp.where(row > 0, pltpu.roll(r.state[:, cols], 1, 0), enter[b : b + 1])
        decay = r.decay_v[b : b + 1, :]
        rate, inlet, sp, log_decay, factor, scale = coefficient_parts(r.rate_pre[:, cols], r.inlet_pre[:, cols], decay)
        conv_low = r.conv[:, cols]
        conv = conv_low.astype(f32)
        init_rows = opening_rows(docs, r.init_v[:, cols])
        log_grad = adjoint * (
            factor * (keep * previous + (1.0 - keep) * init_rows) - inlet * conv * jnp.exp(2.0 * log_decay) / scale
        )
        rate_low = (log_grad * (-8.0 * sp) * rate * (1.0 - rate)).astype(bf)
        direct = adjoint * scale
        inlet_low = (direct * conv * inlet * (1.0 - inlet)).astype(bf)
        decay_row = jnp.sum(log_grad * (-8.0 * rate), axis=0, keepdims=True) * sigmoid(decay)
        back = direct * inlet + contract_last(rate_low, r.rate_w_v[b]) + contract_last(inlet_low, r.inlet_w_v[b])
        r.cgrad[0:count, cols] = back.astype(bf)
        for a, low in enumerate((rate_low, inlet_low)):
            part = contract_first(conv_low, low).astype(bf)
            r.gates[a, b] = part.reshape(r.gates.shape[2:])
        vec.append([
            jnp.sum(rate_low.astype(f32), axis=0, keepdims=True),
            jnp.sum(inlet_low.astype(f32), axis=0, keepdims=True),
            decay_row,
        ])
    rim = r.cgrad.at[pl.ds(count, RIM)]
    net.send(r.cgrad.at[pl.ds(0, RIM)], rim, (net.s_to[n_seq - 1], c), net.sem("rimback"), s > 0)

    @pl.when(s == n_seq - 1)
    def _():
        r.cgrad[pl.ds(count, RIM), :] = jnp.zeros((RIM, wide), bf)

    net.send(r.gates.at[:, :, :, 1 - x], r.gates_x, net.beside, net.sem("gatesx"))
    gather_arrive(1, 1)
    weight_grad_send(0, others[4:])

    @pl.when(s < n_seq - 1)
    def _():
        net.recv(rim, net.sem("rimback"))

    vectors = []
    for b in range(slots):
        cols = pl.ds(b * bw, bw)
        grad = r.cgrad[:, cols].astype(f32)
        own = grad[:count]
        recur = r.recur[:, cols].astype(f32)
        total = jnp.zeros((count, bw), f32)
        tap_rows = []
        for k in range(n_taps):
            tap_rows.append(jnp.sum(own * recur[RIM - k : RIM - k + count] * docs.valid(k), axis=0, keepdims=True))
            total = total + r.taps_v[b, k : k + 1, :] * grad[k : k + count] * ahead_docs.valid(k)[k : k + count]
        r.gath[2, z, :, cols] = total.astype(bf)
        vectors.append(stack_rows(tap_rows + [jnp.sum(own, axis=0, keepdims=True)] + vec[b]))
    gather_start(2)
    for at in (3, 2, 1, 0):
        outs.third(at)

    def norm_tile(i, _):
        cols = pl.ds(pl.multiple_of(i * TILE, TILE), TILE)
        value = contract_last(r.gath[1, z], r.gelu_w_v[cols, :]) + contract_last(r.gath[2, z], r.recur_w_v[cols, :])
        for cc in range(n_ch):
            r.part[cc % 2, cc // 2, :, cols] = value[cc * rows : (cc + 1) * rows]
        return 0

    lax.fori_loop(0, d // TILE, norm_tile, 0)
    gather_arrive(1, 2)
    left_pass(1)
    left_done(0)
    norm_grad = net.ch_sum(r.part, r.mid, r.ylow, r.yfar, "norm")
    to_stream, mix_part = norm_back(values, r.mix_gain_v[...][None, :], norm_grad)
    r.sgrad_v[...] = middle_grad + to_stream
    r.late[n_z] = jnp.concatenate(vectors + [pack_gain(mix_part)], axis=1)
    net.send(r.late.at[n_z], r.pair.at[1], net.beside, net.sem("pair", 1, 2))
    net.recv(r.gates_x, net.sem("gatesx"))

    def gate_add(i, _):
        for a in range(2):
            for b in range(slots):
                value = r.gates[a, b, i, x].astype(f32) + r.gates_x[a, b, i].astype(f32)
                r.gates[a, b, i, x] = value.astype(bf)
        return 0

    lax.fori_loop(0, n_z, gate_add, 0)
    gather_arrive(2, 1)
    weight_grad_send(1, others[:3])
    for k in range(1, n_z):
        to = net.z_of(k)
        net.send(r.gates.at[:, :, to, x], r.gates_z.at[k], net.dev(to, x, y, core), net.sem("gatesz"))
    pair_sum(1, r.late)
    left_done(1)
    gather_product(0)
    gather_arrive(1, 3)
    gather_arrive(2, 2)
    for at in (3, 2, 1):
        outs.fourth(at)
    out_sum = outs.fourth(0)
    weight_grad_send(1, others[3:])
    gather_product(1)
    gather_arrive(2, 3)
    gather_product(2)
    for a, ref in enumerate((r.early, r.late)):
        net.recv(ref.at[pl.ds(0, n_z - 1)], net.sem(("vec", a)))
    early, late = r.early[0], r.late[0]
    for q in range(1, n_z):
        early, late = early + r.early[q], late + r.late[q]
    r.shared[c] = jnp.concatenate([early, late[:, wide:]], axis=1)
    net.ch_gather_start(lambda cc: r.shared.at[cc], "shared")
    piece = bw // n_seq
    for b in range(slots):
        part = jnp.zeros((8, piece), f32)
        for q in range(n_seq):
            at = b * bw + q * piece
            part = jnp.where(s == q, late[:, at : at + piece], part)
        r.small_v[b] = part
    net.recv(r.gates_z.at[pl.ds(1, n_z - 1)], net.sem("gatesz"))
    for a in range(2):
        for b in range(slots):
            total = r.gates[a, b, z, x].astype(f32)
            for k in range(1, n_z):
                total = total + r.gates_z[k, a, b].astype(f32)
            r.gate_out_v[a, b] = total
    net.ch_gather_finish(lambda cc: r.shared.at[cc], "shared")
    gains = r.shared[0, :, wide:]
    for cc in range(1, n_ch):
        gains = gains + r.shared[cc, :, wide:]
    for cc in range(n_ch):
        r.finals_v[:, cc * wide : (cc + 1) * wide] = r.shared[cc, 0 : r.finals_v.shape[0], 0:wide]
    half = gains.shape[1] // 2
    for a in range(2):
        for i in range(half // 128):
            r.gains_v[a, i * 8 : (i + 1) * 8, :] = gains[:, a * half + i * 128 : a * half + (i + 1) * 128]
    r.mixed_v[...] = (middle + outs.total(out_sum)).astype(bf)
    for a in (2, 0, 1):
        weight_grad_done(a)
    for a in range(3):
        gather_done(a)
    for name in ("finals", "mixed", "sgrad", "gains", "gate_out", "small"):
        local.append(net.local(getattr(r, name + "_v"), getattr(r, name)))
    for copy in local:
        copy.wait()
    net.drain()


def finish_kernel(names, *refs):
    r = types.SimpleNamespace(**dict(zip(names, refs)))
    f32 = jnp.float32
    used = []

    def sem():
        used.append(0)
        return r.sems.at[len(used) - 1]

    def copy(src, dst):
        start = pltpu.make_async_copy(src, dst, sem())
        start.start()
        return start

    incoming = {}
    for name, index in (("dw", 2), ("dw", 0), ("dw", 1), ("keep", 0), ("took", 0), ("keep", 1), ("took", 1)):
        incoming[name, index] = copy(getattr(r, name).at[index], getattr(r, name + "_v").at[index])
    for name in ("keep_out", "took_out", "gains", "gate_out", "small", "finals", "mixed", "sgrad"):
        incoming[name] = copy(getattr(r, name), getattr(r, name + "_v"))
    leaving = []

    def leave(name):
        leaving.append(copy(getattr(r, name + "_v"), getattr(r, name)))

    incoming["dw", 2].wait()
    r.down_wg_v[...] = r.dw_v[2].astype(f32)
    leave("down_wg")
    for a, name in enumerate(("gate_wg", "up_wg")):
        incoming["dw", a].wait()
        ref = getattr(r, name + "_v")
        for i in range(ref.shape[1] // 256):
            ref[:, i * 256 : (i + 1) * 256] = contract_first(r.dw_v[a, i * 256 : (i + 1) * 256, :], unit(256))
        leave(name)
    for a, name in enumerate(("gelu_wg", "recur_wg")):
        incoming["keep", a].wait()
        incoming["took", a].wait()
        getattr(r, name + "_v")[...] = r.keep_v[a] + r.took_v[a].astype(f32)
        leave(name)
    for name in ("keep_out", "took_out", "gains", "gate_out", "small", "finals", "mixed", "sgrad"):
        incoming[name].wait()
    r.out_wg_v[...] = r.keep_out_v[...] + r.took_out_v[...].astype(f32)
    leave("out_wg")
    leaving += [
        copy(r.finals_v, r.finals_o), copy(r.mixed_v, r.mixed_o), copy(r.sgrad_v, r.sgrad_o),
        copy(r.gains_v.at[0], r.ffn_o), copy(r.gains_v.at[1], r.mix_o), copy(r.gate_out_v.at[0], r.rate_o),
        copy(r.gate_out_v.at[1], r.inlet_o),
    ]
    n_taps = r.taps_o_v.shape[1]
    for b in range(r.small_v.shape[0]):
        for k in range(n_taps):
            r.taps_o_v[b, k : k + 1, :] = r.small_v[b, k : k + 1, :]
        for k, name in enumerate(("bias_o", "rateb_o", "inletb_o", "decay_o")):
            getattr(r, name + "_v")[b : b + 1, :] = r.small_v[b, n_taps + k : n_taps + k + 1, :]
    for name in ("taps_o", "bias_o", "rateb_o", "inletb_o", "decay_o"):
        leave(name)
    for start in leaving:
        start.wait()


def gathered_body(
    stream, cotangent, mix_gain, gelu_weight, recur_weight, conv_taps, conv_bias, rate_weight, rate_bias, inlet_weight,
    inlet_bias, decay_param, init_states, out_weight, ffn_gain, gate_weight, up_weight, down_weight, doc_lengths, block_counts,
):
    n_seq, n_ch = lax.axis_size(SEQ), lax.axis_size(CH)
    rows, d = stream.shape
    slots, bw = conv_bias.shape
    width, hidden = gate_weight.shape
    sl = hidden // n_seq
    n_z = n_seq // 2
    count, wide, tokens = rows * n_ch, slots * bw, rows * n_ch * n_seq
    piece = bw // n_seq
    n_taps, n_docs = conv_taps.shape[0], doc_lengths.shape[0]
    bf, f32 = jnp.bfloat16, jnp.float32
    vmem = pl.BlockSpec(memory_space=pltpu.VMEM)
    smem = pl.BlockSpec(memory_space=pltpu.SMEM)
    anywhere = pl.BlockSpec(memory_space=pl.ANY)
    inputs = dict(
        stream=stream, cot=cotangent, mix_gain=mix_gain, gelu_w=gelu_weight, recur_w=recur_weight, taps=conv_taps.transpose(1, 0, 2),
        bias=conv_bias, rate_w=rate_weight, rate_b=rate_bias, inlet_w=inlet_weight, inlet_b=inlet_bias, decay=decay_param,
        init=init_states, out_w=out_weight, ffn_gain=ffn_gain, gate_w=gate_weight, up_w=up_weight, down=down_weight,
        lengths=doc_lengths, counts=block_counts,
    )
    places = dict(lengths=smem, counts=smem)
    staged = [name for name in inputs if name not in ("lengths", "counts", "gate_w", "up_w", "down")]
    outputs = dict(
        keep=((2, width, wide), f32), keep_out=((wide, width), f32), took=((2, width, wide), bf), took_out=((wide, width), bf),
        dw=((3, hidden, width), bf),
        finals=((n_docs, wide * n_ch), f32), mixed=((rows, d), bf), sgrad=((rows, d), f32), gains=((2, d // 128, 128), f32),
        gate_out=((2, slots, piece, bw), f32), small=((slots, 8, piece), f32),
    )
    packed = wide + d // 8
    scratch = dict(
        mix=((RIM + count, d), bf), full=((tokens, d), bf), cfull=((tokens, d), bf), turned=((2, hidden, width), bf),
        wt=((3, sl, d), bf), dwl=((3, sl, d), bf), value=((tokens, sl), f32), slope=((tokens, sl), f32),
        hid=((tokens, sl), bf), gat=((tokens, sl), bf), upg=((tokens, sl), bf),
        gelu=((count, wide), f32), recur=((RIM + count, wide), bf), conv=((count, wide), bf), rate_pre=((count, wide), f32),
        inlet_pre=((count, wide), f32), scan_a=((count, wide), f32), scan_b=((count, wide), f32), state=((count, wide), f32),
        gath=((3, n_z, count, wide), bf), left=((2, n_z, n_ch, rows, 2 * width), bf), give=((2, width, wide), bf),
        give_out=((wide, width), bf), take=((2, width, wide), bf), take_out=((wide, width), bf), cgrad=((count + RIM, wide), bf), branch=((n_ch, rows, d), bf),
        summary=((n_seq, 8, bw), f32), summary_back=((n_seq, 8, bw), f32),
        part=((2, 2, rows, d), f32), mid=((2, rows, d), f32), ylow=((rows, d), bf), yfar=((rows, d), bf), middle=((rows, d), f32),
        npart=((n_z, 2, 2, 2, rows, d), bf), nsib=((n_z, 2, 2, rows, d), bf), nfar=((n_z, 2, rows // 2, d), bf),
        nside=((n_z, 2, rows, d), bf), nalong=((n_z, rows, d), bf),
        opart=((n_z, 2, 2, 2, rows, d), bf), osib=((n_z, 2, 2, rows, d), bf), ofar=((n_z, 2, rows, d), bf),
        oside=((n_z, rows, d), bf), oalong=((n_z, rows, d), bf),
        gates=((2, slots, n_z, 2, piece, bw), bf), gates_x=((2, slots, n_z, piece, bw), bf), gates_z=((n_z, 2, slots, piece, bw), bf),
        early=((n_z + 1, 8, packed), f32), late=((n_z + 1, 8, packed), f32), pair=((2, 8, packed), f32),
        shared=((n_ch, 8, packed + d // 8), f32),
    )
    scratch.update({name + "_v": (inputs[name].shape, inputs[name].dtype) for name in staged})
    scratch.update({name + "_v": what for name, what in outputs.items() if name not in ("took", "took_out", "dw")})
    dma = pltpu.SemaphoreType.DMA
    results = pl.pallas_call(
        functools.partial(
            block_kernel, (n_seq, n_ch, rows, d, slots, bw, width, sl),
            list(inputs) + list(outputs) + list(scratch) + ["send_sems", "recv_sems", "local_sems"],
        ),
        out_shape=[jax.ShapeDtypeStruct(*what) for what in outputs.values()],
        in_specs=[places.get(name, anywhere) for name in inputs],
        out_specs=[anywhere] * len(outputs),
        scratch_shapes=[pltpu.VMEM(*what) for what in scratch.values()] + [dma((SEND_SEMS,)), dma((RECV_SEMS,)), dma((LOCAL_SEMS,))],
        compiler_params=pltpu.CompilerParams(collective_id=1, has_side_effects=True, vmem_limit_bytes=VMEM_BYTES),
    )(*inputs.values())
    vector = ((slots, piece), f32)
    ends = dict(
        finals_o=((n_docs, wide * n_ch), f32), mixed_o=((rows, d), bf), sgrad_o=((rows, d), f32), mix_o=((d // 128, 128), f32),
        gelu_wg=((width, wide), f32), recur_wg=((width, wide), f32), taps_o=((slots, n_taps, piece), f32), bias_o=vector,
        rate_o=((slots, piece, bw), f32), rateb_o=vector, inlet_o=((slots, piece, bw), f32), inletb_o=vector, decay_o=vector,
        out_wg=((wide, width), f32), ffn_o=((d // 128, 128), f32), gate_wg=((width, hidden), f32), up_wg=((width, hidden), f32),
        down_wg=((hidden, width), f32),
    )
    direct = ("finals_o", "mixed_o", "sgrad_o", "ffn_o", "mix_o", "rate_o", "inlet_o")
    kept = {name + "_v": outputs[name] for name in outputs}
    kept.update({name + "_v": what for name, what in ends.items() if name not in direct})
    last = pl.pallas_call(
        functools.partial(finish_kernel, list(outputs) + list(ends) + list(kept) + ["sems"]),
        out_shape=[jax.ShapeDtypeStruct(*what) for what in ends.values()],
        in_specs=[anywhere] * len(outputs),
        out_specs=[anywhere] * len(ends),
        scratch_shapes=[pltpu.VMEM(*what) for what in kept.values()] + [pltpu.SemaphoreType.DMA((40,))],
        compiler_params=pltpu.CompilerParams(vmem_limit_bytes=VMEM_BYTES),
    )(*results)
    named = dict(zip(ends, last))
    named["taps_o"] = named["taps_o"].transpose(1, 0, 2)
    named["mix_o"], named["ffn_o"] = named["mix_o"].reshape(d), named["ffn_o"].reshape(d)
    return tuple(named.values())


def solution(mesh):
    in_specs = (
        P((SEQ, CH), None),
        P((SEQ, CH), None),
        P(),
        P(None, CH),
        P(None, CH),
        P(None, CH, None),
        P(CH, None),
        P(CH, None, None),
        P(CH, None),
        P(CH, None, None),
        P(CH, None),
        P(CH, None),
        P(None, CH),
        P(CH, None),
        P(),
        P(SEQ, CH),
        P(SEQ, CH),
        P(CH, SEQ),
        P(),
        P(CH),
    )
    out_specs = (
        P(),
        P((SEQ, CH), None),
        P((SEQ, CH), None),
        P(),
        P(SEQ, CH),
        P(SEQ, CH),
        P(None, CH, SEQ),
        P(CH, SEQ),
        P(CH, SEQ, None),
        P(CH, SEQ),
        P(CH, SEQ, None),
        P(CH, SEQ),
        P(CH, SEQ),
        P(CH, SEQ),
        P(),
        P(SEQ, CH),
        P(SEQ, CH),
        P(CH, SEQ),
    )
    return jax.shard_map(gathered_body if mesh.shape[SEQ] == 8 else body, mesh=mesh, in_specs=in_specs, out_specs=out_specs, check_vma=False)
```

time: 255 us -> 217 us (0.85); the launches traced: 255 us -> 214 us
  Pallas kernels: 251 us -> 212 us
  local copies, waits for them, and re-layouts: 2.61 us -> 0 us
    pallas_call x1, Pallas kernels: 243 us -> 206 us  [gathered_body(): pl.pallas_call(functools.partial(block_kernel, (n_seq, n_ch, rows, d, slo...]
    unnamed x2 -> x0, local copies, waits for them, and re-layouts: 2.61 us -> none
where the time goes in v4:
time: 217 us; the launch traced here: 214 us
  Pallas kernels  212 us (98%)
    pallas_call x1, Pallas kernels, gathered_body(): pl.pallas_call(functools.partial(block_kernel, (n_seq, n_ch, rows, d, slo...  206 us
    pallas_call x1, Pallas kernels, gathered_body(): pl.pallas_call(functools.partial(finish_kernel, list(outputs) + list(ends...  6.19 us

profile of v4, /device:TPU:0, one launch (start us, length us, event | category | flops | bytes accessed | tf_op | source)
XLA Modules:
  0.0 213.9 jit_solution(17731977605106989004)
XLA Ops:
  1.3 206.2 %shard_map.331 = (f32[2,256,768]{2,1,0:T(8,128)}, f32[768,256]{1,0:T(8,128)}, bf16[2,256,768]{2,1,0:T(8,128)(2,1)}, bf16[768,256]{1,0:T(8,128)(2,1)}, bf16[3,153...) custom-call(bf16[32,2048]{1,0:T(8,128)(2,1)} %refs_0_.1, ...), custom_call_target="tpu_custom_call" | custom-call | tf_op jit(solution)/shard_map/pallas_call | solution.py:1424
  207.5 6.2 %shard_map.332 = (f32[5,3072]{1,0:T(8,128)}, bf16[32,2048]{1,0:T(8,128)(2,1)}, f32[32,2048]{1,0:T(8,128)}, f32[16,128]{1,0:T(8,128)}, f32[256,768]{1,0:T(8,128)}...) custom-call(f32[2,256,768]{2,1,0:T(8,128)} %get-tuple-element.47.ref, ...), custom_call_target="tpu_custom_call" | custom-call | tf_op jit(solution)/shard_map/pallas_call | solution.py:1446

commit v5 on v4

--- a/solution.py
+++ b/solution.py
@@ -19,7 +19,7 @@
 VMEM_BYTES = 63 * 2**20
 TILE = 1024
 SEND_SEMS = 96
-RECV_SEMS = 128
+RECV_SEMS = 140
 LOCAL_SEMS = 46
 
 
@@ -485,6 +485,39 @@
         self.send(view, view, self.below, self.sem((tag, "z"), (slot + n_z - 1) % n_z, n_z), (z < slot) & (z > 0))
 
 
+    def chain_sum(self, k, term, lands, add, tag):
+        n_z, z = self.n_z, self.z
+        for way, to, goes, comes in ((1, self.above, z + k < n_z, z > 0), (n_z - 1, self.below, z >= k, z < n_z - 1)):
+            land, name = lands[way > 1], (tag, way > 1)
+            mine = term((z + way * k) % n_z)
+            if k < n_z - 1:
+                @pl.when(goes & comes)
+                def _():
+                    self.recv(land.at[k], self.sem(name, k, n_z - 1))
+                    add(mine, land.at[k])
+
+            self.send(mine, land.at[k - 1], to, self.sem(name, k - 1, n_z - 1), goes)
+
+    def chain_sum_last(self, lands, add, total, tag):
+        n_z, z = self.n_z, self.z
+        for side, comes in ((0, z > 0), (1, z < n_z - 1)):
+            @pl.when(comes)
+            def _(side=side):
+                self.recv(lands[side].at[0], self.sem((tag, side > 0), 0, n_z - 1))
+                add(total, lands[side].at[0])
+
+    def arrival(self, slot):
+        n_z, z = self.n_z, self.z
+        low, high = (n_z - 1 - z) // (n_z - 1), z // (n_z - 1)
+        far = slot // (n_z // 2 + 1)
+        inner = (1 - far) * (2 * slot - 1) + far * 2 * (n_z - slot)
+        return (low * (n_z - slot) + high * slot + (1 - low - high) * inner + n_z) % n_z
+
+
+def add_into(mine, more):
+    mine[...] = (mine[...].astype(jnp.float32) + more[...].astype(jnp.float32)).astype(mine.dtype)
+
+
 class Spread:
     def __init__(self, net, ref, tag):
         self.net, self.ref, self.tag = net, ref, tag
@@ -535,8 +568,8 @@
 
 
 class Collect:
-    def __init__(self, net, part, sib, far, side, along, tag):
-        self.net, self.part, self.sib, self.far, self.side, self.along, self.tag = net, part, sib, far, side, along, tag
+    def __init__(self, net, part, sib, far, side, tag):
+        self.net, self.part, self.sib, self.far, self.side, self.tag = net, part, sib, far, side, tag
 
     def sem(self, what, at):
         return self.net.sem((self.tag, what), at, self.net.n_z)
@@ -575,20 +608,13 @@
         total = self.plane_total(at)
         if at == 0:
             return total
-        slot = net.slot(at)
         part[at, net.core, net.y, net.x] = total.astype(jnp.bfloat16)
-        net.send(
-            part.at[at, net.core, net.y, net.x], self.along.at[slot],
-            net.dev(net.z_of(slot), net.x, net.y, net.core), net.sem((self.tag, "z")),
-        )
         return None
 
-    def total(self, own):
+    def term(self, there):
         net = self.net
-        net.recv(self.along.at[pl.ds(1, net.n_z - 1)], net.sem((self.tag, "z")))
-        for slot in range(1, net.n_z):
-            own = own + self.along[slot].astype(jnp.float32)
-        return own
+        at = net.arrival((net.z + net.n_z - there) % net.n_z)
+        return self.part.at[at, net.core, net.y, net.x]
 
 
 class CollectEven(Collect):
@@ -914,9 +940,9 @@
         net.recv(summary.at[pl.ds(0, n_seq - 1)], net.sem(tag))
 
     exchange(r.summary, ends_a + ends_b, "sum")
+    weight_start(0, others[2:])
+    cots.relay(0)
     cots.arrive(net.slot(2))
-    cots.relay(0)
-    weight_start(0, others[2:])
     loaded("out_w")
     exchanged(r.summary, "sum")
     enter = jnp.zeros((slots, bw), f32)
@@ -942,7 +968,7 @@
         return 0
 
     lax.fori_loop(0, d // TILE, branch_tile, 0)
-    middle = values + net.ch_sum(r.part, r.mid, r.ylow, r.yfar, "branch")
+    middle = r.stream_v[...].astype(f32) + net.ch_sum(r.part, r.mid, r.ylow, r.yfar, "branch")
     scale = lax.rsqrt(jnp.mean(middle * middle, axis=-1, keepdims=True) + EPS)
     r.full[pl.ds(mine, rows), :] = (middle * scale * r.ffn_gain_v[...][None, :]).astype(bf)
     r.middle[...] = middle
@@ -1081,8 +1107,14 @@
 
         lax.fori_loop(0, d // TILE, tile, 0)
 
-    norms = CollectEven(net, r.npart, r.nsib, r.nfar, r.nside, r.nalong, "norm")
-    outs = Collect(net, r.opart, r.osib, r.ofar, r.oside, r.oalong, "out")
+    def norm_step(k):
+        net.chain_sum(k, norms.term, (r.oup, r.odown), add_into, 2)
+
+    def out_step(k):
+        net.chain_sum(k, outs.term, (r.oup, r.odown), add_into, 0)
+
+    norms = CollectEven(net, r.npart, r.nsib, r.nfar, r.nside, "norm")
+    outs = Collect(net, r.opart, r.osib, r.ofar, r.oside, "out")
     backward(3)
     norms.first(3)
     backward(2)
@@ -1097,27 +1129,32 @@
     norms.second(1)
     norms.third(2)
     norms.fourth(3)
+    norm_step(3)
     norms.second(0)
     output(3)
     output(2)
     norms.third(1)
     norms.fourth(2)
+    norm_step(2)
     output(1)
     output(0)
     norms.third(0)
     norms.fourth(1)
+    norm_step(1)
     for at in (3, 2, 1, 0):
         outs.first(at)
     gather_arrive(0, 1)
     weight_grad(0, r.gat, r.full)
     weight_grad(1, r.upg, r.full)
-    own_norm = norms.fourth(0)
+    r.sgrad_v[...] = norms.fourth(0)
     left_pass(0)
     gather_arrive(0, 2)
-    nfg = norms.total(own_norm)
-
-    to_middle, ffn_part = norm_back(middle, r.ffn_gain_v[...][None, :], nfg)
+    net.chain_sum_last((r.oup, r.odown), add_into, r.sgrad_v, 2)
+    nfg = r.sgrad_v[...]
+
+    to_middle, ffn_part = norm_back(r.middle[...], r.ffn_gain_v[...][None, :], nfg)
     middle_grad = r.cot_v[...].astype(f32) + to_middle
+    r.sgrad_v[...] = middle_grad
     r.branch[c] = middle_grad.astype(bf)
     net.ch_gather_start(lambda cc: r.branch.at[cc], "bgrad")
     left_start(1, r.branch.at[c])
@@ -1235,11 +1272,14 @@
     left_pass(1)
     left_done(0)
     norm_grad = net.ch_sum(r.part, r.mid, r.ylow, r.yfar, "norm")
-    to_stream, mix_part = norm_back(values, r.mix_gain_v[...][None, :], norm_grad)
-    r.sgrad_v[...] = middle_grad + to_stream
+    to_stream, mix_part = norm_back(r.stream_v[...].astype(f32), r.mix_gain_v[...][None, :], norm_grad)
+    r.sgrad_v[...] += to_stream
     r.late[n_z] = jnp.concatenate(vectors + [pack_gain(mix_part)], axis=1)
     net.send(r.late.at[n_z], r.pair.at[1], net.beside, net.sem("pair", 1, 2))
     net.recv(r.gates_x, net.sem("gatesx"))
+
+    def gate_step(k):
+        net.chain_sum(k, lambda there: r.gates.at[:, :, there, x], (r.gates_up, r.gates_down), add_into, 1)
 
     def gate_add(i, _):
         for a in range(2):
@@ -1251,9 +1291,7 @@
     lax.fori_loop(0, n_z, gate_add, 0)
     gather_arrive(2, 1)
     weight_grad_send(1, others[:3])
-    for k in range(1, n_z):
-        to = net.z_of(k)
-        net.send(r.gates.at[:, :, to, x], r.gates_z.at[k], net.dev(to, x, y, core), net.sem("gatesz"))
+    gate_step(3)
     pair_sum(1, r.late)
     left_done(1)
     gather_product(0)
@@ -1261,10 +1299,16 @@
     gather_arrive(2, 2)
     for at in (3, 2, 1):
         outs.fourth(at)
-    out_sum = outs.fourth(0)
-    weight_grad_send(1, others[3:])
+    r.middle[...] += outs.fourth(0)
+    out_step(3)
+    gate_step(2)
+    weight_grad_send(1, others[3:5])
     gather_product(1)
+    out_step(2)
+    gate_step(1)
+    weight_grad_send(1, others[5:])
     gather_arrive(2, 3)
+    out_step(1)
     gather_product(2)
     for a, ref in enumerate((r.early, r.late)):
         net.recv(ref.at[pl.ds(0, n_z - 1)], net.sem(("vec", a)))
@@ -1280,13 +1324,8 @@
             at = b * bw + q * piece
             part = jnp.where(s == q, late[:, at : at + piece], part)
         r.small_v[b] = part
-    net.recv(r.gates_z.at[pl.ds(1, n_z - 1)], net.sem("gatesz"))
-    for a in range(2):
-        for b in range(slots):
-            total = r.gates[a, b, z, x].astype(f32)
-            for k in range(1, n_z):
-                total = total + r.gates_z[k, a, b].astype(f32)
-            r.gate_out_v[a, b] = total
+    r.gate_out_v[...] = r.gates[:, :, z, x].astype(f32)
+    net.chain_sum_last((r.gates_up, r.gates_down), add_into, r.gate_out_v, 1)
     net.ch_gather_finish(lambda cc: r.shared.at[cc], "shared")
     gains = r.shared[0, :, wide:]
     for cc in range(1, n_ch):
@@ -1297,7 +1336,8 @@
     for a in range(2):
         for i in range(half // 128):
             r.gains_v[a, i * 8 : (i + 1) * 8, :] = gains[:, a * half + i * 128 : a * half + (i + 1) * 128]
-    r.mixed_v[...] = (middle + outs.total(out_sum)).astype(bf)
+    net.chain_sum_last((r.oup, r.odown), add_into, r.middle, 0)
+    r.mixed_v[...] = r.middle[...].astype(bf)
     for a in (2, 0, 1):
         weight_grad_done(a)
     for a in range(3):
@@ -1411,10 +1451,10 @@
         summary=((n_seq, 8, bw), f32), summary_back=((n_seq, 8, bw), f32),
         part=((2, 2, rows, d), f32), mid=((2, rows, d), f32), ylow=((rows, d), bf), yfar=((rows, d), bf), middle=((rows, d), f32),
         npart=((n_z, 2, 2, 2, rows, d), bf), nsib=((n_z, 2, 2, rows, d), bf), nfar=((n_z, 2, rows // 2, d), bf),
-        nside=((n_z, 2, rows, d), bf), nalong=((n_z, rows, d), bf),
+        nside=((n_z, 2, rows, d), bf),
         opart=((n_z, 2, 2, 2, rows, d), bf), osib=((n_z, 2, 2, rows, d), bf), ofar=((n_z, 2, rows, d), bf),
-        oside=((n_z, rows, d), bf), oalong=((n_z, rows, d), bf),
-        gates=((2, slots, n_z, 2, piece, bw), bf), gates_x=((2, slots, n_z, piece, bw), bf), gates_z=((n_z, 2, slots, piece, bw), bf),
+        oside=((n_z, rows, d), bf), oup=((n_z - 1, rows, d), bf), odown=((n_z - 1, rows, d), bf),
+        gates=((2, slots, n_z, 2, piece, bw), bf), gates_x=((2, slots, n_z, piece, bw), bf), gates_up=((n_z - 1, 2, slots, piece, bw), bf), gates_down=((n_z - 1, 2, slots, piece, bw), bf),
         early=((n_z + 1, 8, packed), f32), late=((n_z + 1, 8, packed), f32), pair=((2, 8, packed), f32),
         shared=((n_ch, 8, packed + d // 8), f32),
     )

time: 217 us -> 207 us (0.954); the launches traced: 214 us -> 207 us
  Pallas kernels: 212 us -> 205 us
    pallas_call x1, Pallas kernels: 206 us -> 199 us  [gathered_body(): pl.pallas_call(functools.partial(block_kernel, (n_seq, n_ch, rows, d, slo...]
where the time goes in v5:
time: 207 us
  Pallas kernels  205 us (99%)
    pallas_call x1, Pallas kernels, gathered_body(): pl.pallas_call(functools.partial(block_kernel, (n_seq, n_ch, rows, d, slo...  199 us
    pallas_call x1, Pallas kernels, gathered_body(): pl.pallas_call(functools.partial(finish_kernel, list(outputs) + list(ends...  6.19 us

profile of v5, /device:TPU:0, one launch (start us, length us, event | category | flops | bytes accessed | tf_op | source)
XLA Modules:
  0.0 206.8 jit_solution(9455424239079653720)
XLA Ops:
  1.3 199.2 %shard_map.331 = (f32[2,256,768]{2,1,0:T(8,128)}, f32[768,256]{1,0:T(8,128)}, bf16[2,256,768]{2,1,0:T(8,128)(2,1)}, bf16[768,256]{1,0:T(8,128)(2,1)}, bf16[3,153...) custom-call(bf16[32,2048]{1,0:T(8,128)(2,1)} %refs_0_.1, ...), custom_call_target="tpu_custom_call" | custom-call | tf_op jit(solution)/shard_map/pallas_call | solution.py:1464
  200.5 6.2 %shard_map.332 = (f32[5,3072]{1,0:T(8,128)}, bf16[32,2048]{1,0:T(8,128)(2,1)}, f32[32,2048]{1,0:T(8,128)}, f32[16,128]{1,0:T(8,128)}, f32[256,768]{1,0:T(8,128)}...) custom-call(f32[2,256,768]{2,1,0:T(8,128)} %get-tuple-element.47.ref, ...), custom_call_target="tpu_custom_call" | custom-call | tf_op jit(solution)/shard_map/pallas_call | solution.py:1486

commit v6 on v5

--- a/solution.py
+++ b/solution.py
@@ -835,10 +835,6 @@
                 src[i * 256 // half, :, at : at + 256], unit(src.shape[1])
             ).astype(bf)
 
-    loaded("gate_w")
-    turn(0, r.give)
-    loaded("up_w")
-    turn(1, r.take)
     net.meet(peers)
 
     def mix_of(cc):
@@ -893,6 +889,10 @@
         net.recv(r.wt.at[a, :, pl.ds(0, (n_seq - 1) * width)], net.sem(("w", a)))
         local.pop(0).wait()
 
+    loaded("gate_w")
+    turn(0, r.give)
+    loaded("up_w")
+    turn(1, r.take)
     weight_start(0, others[:2])
     for name in [name for name in loads if name != "out_w"]:
         loaded(name)
@@ -989,7 +989,7 @@
             if which == 0:
                 ref = r.give_out if a == 0 else r.give.at[a - 1]
                 ref[...] = value.astype(bf)
-                net.send(ref, r.take_out if a == 0 else r.take.at[a - 1], net.beside, net.sem(("take", a)))
+                net.send(ref, r.took_out if a == 0 else r.took.at[a - 1], net.beside, net.sem(("take", a)))
             elif a == 0:
                 r.keep_out_v[...] = value
                 local.append(net.local(r.keep_out_v, r.keep_out))
@@ -998,9 +998,7 @@
                 local.append(net.local(r.keep_v.at[a - 1], r.keep.at[a - 1]))
 
     def gather_done(a):
-        ref = r.take_out if a == 0 else r.take.at[a - 1]
-        net.recv(ref, net.sem(("take", a)))
-        local.append(net.local(ref, r.took_out if a == 0 else r.took.at[a - 1]))
+        net.recv(r.took_out if a == 0 else r.took.at[a - 1], net.sem(("take", a)))
 
     lows.start()
     weight_start(1, others[:2])
@@ -1161,8 +1159,11 @@
     weight_grad_send(0, others[:3])
     for at in (3, 2, 1, 0):
         outs.second(at)
-    r.early[n_z] = jnp.concatenate(finals + [pack_gain(ffn_part)], axis=1)
-    net.send(r.early.at[n_z], r.pair.at[0], net.beside, net.sem("pair", 0, 2))
+    n_docs = r.finals_v.shape[0]
+    spare = jnp.concatenate([ffn_part, jnp.zeros((1, (8 - n_docs) * wide - d), f32)], axis=1)
+    spare = [spare[:, i * wide : (i + 1) * wide] for i in range(8 - n_docs)]
+    r.early[n_z] = stack_rows([jnp.concatenate(finals, axis=1)[:n_docs]] + spare)
+    net.send(r.early.at[n_z], r.early_pair, net.beside, net.sem("pair", 0, 2))
     net.ch_gather_finish(lambda cc: r.branch.at[cc], "bgrad")
 
     ahead_docs = Docs(r.lengths, s * count, count + RIM)
@@ -1189,14 +1190,11 @@
     weight_grad_send(0, others[3:4])
     exchanged(r.summary_back, "sumback")
 
-    def pair_sum(a, ref):
-        net.recv(r.pair.at[a], net.sem("pair", a, 2))
-        ref[z] = ref[n_z] + r.pair[a]
-        for k in range(1, n_z):
-            to = net.z_of(k)
-            net.send(ref.at[z], ref.at[z], net.dev(to, x, y, core), net.sem(("vec", a)))
-
-    pair_sum(0, r.early)
+    net.recv(r.early_pair, net.sem("pair", 0, 2))
+    r.early[z] = r.early[n_z] + r.early_pair[...]
+    for k in range(1, n_z):
+        to = net.z_of(k)
+        net.send(r.early.at[z], r.early.at[z], net.dev(to, x, y, core), net.sem(("vec", 0)))
     enter_back = jnp.zeros((slots, bw), f32)
     for q in range(n_seq - 1, 0, -1):
         after = r.summary_back[q, 0:slots] * enter_back + r.summary_back[q, slots : 2 * slots]
@@ -1274,8 +1272,9 @@
     norm_grad = net.ch_sum(r.part, r.mid, r.ylow, r.yfar, "norm")
     to_stream, mix_part = norm_back(r.stream_v[...].astype(f32), r.mix_gain_v[...][None, :], norm_grad)
     r.sgrad_v[...] += to_stream
-    r.late[n_z] = jnp.concatenate(vectors + [pack_gain(mix_part)], axis=1)
-    net.send(r.late.at[n_z], r.pair.at[1], net.beside, net.sem("pair", 1, 2))
+    local.append(net.local(r.sgrad_v, r.sgrad))
+    r.late[...] = jnp.concatenate(vectors + [pack_gain(mix_part)], axis=1)
+    net.send(r.late, r.late_pair, net.beside, net.sem("pair", 1, 2))
     net.recv(r.gates_x, net.sem("gatesx"))
 
     def gate_step(k):
@@ -1292,7 +1291,17 @@
     gather_arrive(2, 1)
     weight_grad_send(1, others[:3])
     gate_step(3)
-    pair_sum(1, r.late)
+    net.recv(r.late_pair, net.sem("pair", 1, 2))
+    late = r.late[...] + r.late_pair[...]
+    piece = bw // n_seq
+    gap = jnp.zeros((8, r.late_out.shape[2] - (late.shape[1] - wide) - 2 * slots * piece), f32)
+    for q in range(n_z):
+        cuts_at = [b * bw + 2 * q * piece for b in range(slots)]
+        r.late_out[q] = jnp.concatenate([late[:, at : at + 2 * piece] for at in cuts_at] + [gap, late[:, wide:]], axis=1)
+    r.late_in[z] = r.late_out[z]
+    for k in range(1, n_z):
+        to = net.z_of(k)
+        net.send(r.late_out.at[to], r.late_in.at[z], net.dev(to, x, y, core), net.sem(("vec", 1)))
     left_done(1)
     gather_product(0)
     gather_arrive(1, 3)
@@ -1307,43 +1316,43 @@
     out_step(2)
     gate_step(1)
     weight_grad_send(1, others[5:])
+    for a, ref in enumerate((r.early, r.late_in)):
+        net.recv(ref.at[pl.ds(0, n_z - 1)], net.sem(("vec", a)))
+    early, late = r.early[0], r.late_in[0]
+    for q in range(1, n_z):
+        early, late = early + r.early[q], late + r.late_in[q]
+    r.shared[c] = jnp.concatenate([early, late[:, late.shape[1] - d // 8 :]], axis=1)
+    net.ch_gather_start(lambda cc: r.shared.at[cc], "shared")
+    for b in range(slots):
+        at = 2 * b * piece
+        r.small_v[b] = jnp.where(x == 0, late[:, at : at + piece], late[:, at + piece : at + 2 * piece])
+    local.append(net.local(r.small_v, r.small))
     gather_arrive(2, 3)
     out_step(1)
     gather_product(2)
-    for a, ref in enumerate((r.early, r.late)):
-        net.recv(ref.at[pl.ds(0, n_z - 1)], net.sem(("vec", a)))
-    early, late = r.early[0], r.late[0]
-    for q in range(1, n_z):
-        early, late = early + r.early[q], late + r.late[q]
-    r.shared[c] = jnp.concatenate([early, late[:, wide:]], axis=1)
-    net.ch_gather_start(lambda cc: r.shared.at[cc], "shared")
-    piece = bw // n_seq
-    for b in range(slots):
-        part = jnp.zeros((8, piece), f32)
-        for q in range(n_seq):
-            at = b * bw + q * piece
-            part = jnp.where(s == q, late[:, at : at + piece], part)
-        r.small_v[b] = part
     r.gate_out_v[...] = r.gates[:, :, z, x].astype(f32)
     net.chain_sum_last((r.gates_up, r.gates_down), add_into, r.gate_out_v, 1)
+    local.append(net.local(r.gate_out_v, r.gate_out))
     net.ch_gather_finish(lambda cc: r.shared.at[cc], "shared")
-    gains = r.shared[0, :, wide:]
+    total = r.shared[0]
     for cc in range(1, n_ch):
-        gains = gains + r.shared[cc, :, wide:]
+        total = total + r.shared[cc]
     for cc in range(n_ch):
-        r.finals_v[:, cc * wide : (cc + 1) * wide] = r.shared[cc, 0 : r.finals_v.shape[0], 0:wide]
-    half = gains.shape[1] // 2
-    for a in range(2):
-        for i in range(half // 128):
-            r.gains_v[a, i * 8 : (i + 1) * 8, :] = gains[:, a * half + i * 128 : a * half + (i + 1) * 128]
+        r.finals_v[:, cc * wide : (cc + 1) * wide] = r.shared[cc, 0:n_docs, 0:wide]
+    local.append(net.local(r.finals_v, r.finals))
+    for i in range(d // 128):
+        at, line = i * 128 % wide, n_docs + i * 128 // wide
+        r.gains_v[0, i : i + 1, :] = total[line : line + 1, at : at + 128]
+    for i in range(d // 1024):
+        r.gains_v[1, i * 8 : (i + 1) * 8, :] = total[:, wide + i * 128 : wide + (i + 1) * 128]
+    local.append(net.local(r.gains_v, r.gains))
     net.chain_sum_last((r.oup, r.odown), add_into, r.middle, 0)
     r.mixed_v[...] = r.middle[...].astype(bf)
+    local.append(net.local(r.mixed_v, r.mixed))
     for a in (2, 0, 1):
         weight_grad_done(a)
     for a in range(3):
         gather_done(a)
-    for name in ("finals", "mixed", "sgrad", "gains", "gate_out", "small"):
-        local.append(net.local(getattr(r, name + "_v"), getattr(r, name)))
     for copy in local:
         copy.wait()
     net.drain()
@@ -1364,7 +1373,7 @@
         return start
 
     incoming = {}
-    for name, index in (("dw", 2), ("dw", 0), ("dw", 1), ("keep", 0), ("took", 0), ("keep", 1), ("took", 1)):
+    for name, index in (("dw", 0), ("dw", 1), ("dw", 2), ("keep", 0), ("took", 0), ("keep", 1), ("took", 1)):
         incoming[name, index] = copy(getattr(r, name).at[index], getattr(r, name + "_v").at[index])
     for name in ("keep_out", "took_out", "gains", "gate_out", "small", "finals", "mixed", "sgrad"):
         incoming[name] = copy(getattr(r, name), getattr(r, name + "_v"))
@@ -1373,15 +1382,15 @@
     def leave(name):
         leaving.append(copy(getattr(r, name + "_v"), getattr(r, name)))
 
-    incoming["dw", 2].wait()
-    r.down_wg_v[...] = r.dw_v[2].astype(f32)
-    leave("down_wg")
     for a, name in enumerate(("gate_wg", "up_wg")):
         incoming["dw", a].wait()
         ref = getattr(r, name + "_v")
         for i in range(ref.shape[1] // 256):
             ref[:, i * 256 : (i + 1) * 256] = contract_first(r.dw_v[a, i * 256 : (i + 1) * 256, :], unit(256))
         leave(name)
+    incoming["dw", 2].wait()
+    r.down_wg_v[...] = r.dw_v[2].astype(f32)
+    leave("down_wg")
     for a, name in enumerate(("gelu_wg", "recur_wg")):
         incoming["keep", a].wait()
         incoming["took", a].wait()
@@ -1447,7 +1456,7 @@
         gelu=((count, wide), f32), recur=((RIM + count, wide), bf), conv=((count, wide), bf), rate_pre=((count, wide), f32),
         inlet_pre=((count, wide), f32), scan_a=((count, wide), f32), scan_b=((count, wide), f32), state=((count, wide), f32),
         gath=((3, n_z, count, wide), bf), left=((2, n_z, n_ch, rows, 2 * width), bf), give=((2, width, wide), bf),
-        give_out=((wide, width), bf), take=((2, width, wide), bf), take_out=((wide, width), bf), cgrad=((count + RIM, wide), bf), branch=((n_ch, rows, d), bf),
+        give_out=((wide, width), bf), take=((2, width, wide), bf), cgrad=((count + RIM, wide), bf), branch=((n_ch, rows, d), bf),
         summary=((n_seq, 8, bw), f32), summary_back=((n_seq, 8, bw), f32),
         part=((2, 2, rows, d), f32), mid=((2, rows, d), f32), ylow=((rows, d), bf), yfar=((rows, d), bf), middle=((rows, d), f32),
         npart=((n_z, 2, 2, 2, rows, d), bf), nsib=((n_z, 2, 2, rows, d), bf), nfar=((n_z, 2, rows // 2, d), bf),
@@ -1455,8 +1464,9 @@
         opart=((n_z, 2, 2, 2, rows, d), bf), osib=((n_z, 2, 2, rows, d), bf), ofar=((n_z, 2, rows, d), bf),
         oside=((n_z, rows, d), bf), oup=((n_z - 1, rows, d), bf), odown=((n_z - 1, rows, d), bf),
         gates=((2, slots, n_z, 2, piece, bw), bf), gates_x=((2, slots, n_z, piece, bw), bf), gates_up=((n_z - 1, 2, slots, piece, bw), bf), gates_down=((n_z - 1, 2, slots, piece, bw), bf),
-        early=((n_z + 1, 8, packed), f32), late=((n_z + 1, 8, packed), f32), pair=((2, 8, packed), f32),
-        shared=((n_ch, 8, packed + d // 8), f32),
+        early=((n_z + 1, 8, wide), f32), early_pair=((8, wide), f32), late=((8, packed), f32), late_pair=((8, packed), f32),
+        late_out=((n_z, 8, 2 * d // 8), f32), late_in=((n_z, 8, 2 * d // 8), f32),
+        shared=((n_ch, 8, packed), f32),
     )
     scratch.update({name + "_v": (inputs[name].shape, inputs[name].dtype) for name in staged})
     scratch.update({name + "_v": what for name, what in outputs.items() if name not in ("took", "took_out", "dw")})

time: 207 us -> 205 us (level)
  no operation moved by 1% of the time
where the time goes in v6:
time: 205 us
  Pallas kernels  204 us (100%)
    pallas_call x1, Pallas kernels, gathered_body(): pl.pallas_call(functools.partial(block_kernel, (n_seq, n_ch, rows, d, slo...  198 us
    pallas_call x1, Pallas kernels, gathered_body(): pl.pallas_call(functools.partial(finish_kernel, list(outputs) + list(ends...  5.35 us

profile of v6, /device:TPU:0, one launch (start us, length us, event | category | flops | bytes accessed | tf_op | source)
XLA Modules:
  0.0 205.1 jit_solution(7139281751232260361)
XLA Ops:
  1.3 198.3 %shard_map.331 = (f32[2,256,768]{2,1,0:T(8,128)}, f32[768,256]{1,0:T(8,128)}, bf16[2,256,768]{2,1,0:T(8,128)(2,1)}, bf16[768,256]{1,0:T(8,128)(2,1)}, bf16[3,153...) custom-call(bf16[32,2048]{1,0:T(8,128)(2,1)} %refs_0_.1, ...), custom_call_target="tpu_custom_call" | custom-call | tf_op jit(solution)/shard_map/pallas_call | solution.py:1474
  199.6 5.3 %shard_map.332 = (f32[5,3072]{1,0:T(8,128)}, bf16[32,2048]{1,0:T(8,128)(2,1)}, f32[32,2048]{1,0:T(8,128)}, f32[16,128]{1,0:T(8,128)}, f32[256,768]{1,0:T(8,128)}...) custom-call(f32[2,256,768]{2,1,0:T(8,128)} %get-tuple-element.47.ref, ...), custom_call_target="tpu_custom_call" | custom-call | tf_op jit(solution)/shard_map/pallas_call | solution.py:1496

commit v7 on v6

--- a/solution.py
+++ b/solution.py
@@ -1372,8 +1372,13 @@
         start.start()
         return start
 
-    incoming = {}
-    for name, index in (("dw", 0), ("dw", 1), ("dw", 2), ("keep", 0), ("took", 0), ("keep", 1), ("took", 1)):
+    incoming, halves = {}, {}
+    for a in range(2):
+        size = r.dw.shape[1] // 2
+        for half in range(2):
+            at = pl.ds(half * size, size)
+            halves[a, half] = copy(r.dw.at[a, at], r.dw_v.at[a, at])
+    for name, index in (("dw", 2), ("keep", 0), ("took", 0), ("keep", 1), ("took", 1)):
         incoming[name, index] = copy(getattr(r, name).at[index], getattr(r, name + "_v").at[index])
     for name in ("keep_out", "took_out", "gains", "gate_out", "small", "finals", "mixed", "sgrad"):
         incoming[name] = copy(getattr(r, name), getattr(r, name + "_v"))
@@ -1383,11 +1388,14 @@
         leaving.append(copy(getattr(r, name + "_v"), getattr(r, name)))
 
     for a, name in enumerate(("gate_wg", "up_wg")):
-        incoming["dw", a].wait()
-        ref = getattr(r, name + "_v")
-        for i in range(ref.shape[1] // 256):
-            ref[:, i * 256 : (i + 1) * 256] = contract_first(r.dw_v[a, i * 256 : (i + 1) * 256, :], unit(256))
-        leave(name)
+        ref, out = getattr(r, name + "_v"), getattr(r, name)
+        size = ref.shape[1] // 2
+        for half in range(2):
+            halves[a, half].wait()
+            for i in range(half * size // 256, (half + 1) * size // 256):
+                ref[:, i * 256 : (i + 1) * 256] = contract_first(r.dw_v[a, i * 256 : (i + 1) * 256, :], unit(256))
+            cols = pl.ds(half * size, size)
+            leaving.append(copy(ref.at[:, cols], out.at[:, cols]))
     incoming["dw", 2].wait()
     r.down_wg_v[...] = r.dw_v[2].astype(f32)
     leave("down_wg")

time: 205 us -> 206 us (level)
  no operation moved by 1% of the time
where the time goes in v7:
time: 206 us
  Pallas kernels  204 us (99%)
    pallas_call x1, Pallas kernels, gathered_body(): pl.pallas_call(functools.partial(block_kernel, (n_seq, n_ch, rows, d, slo...  198 us
    pallas_call x1, Pallas kernels, gathered_body(): pl.pallas_call(functools.partial(finish_kernel, list(outputs) + list(ends...  6 us

profile of v7, /device:TPU:0, one launch (start us, length us, event | category | flops | bytes accessed | tf_op | source)
XLA Modules:
  0.0 205.8 jit_solution(11701261932028765547)
XLA Ops:
  1.3 198.3 %shard_map.331 = (f32[2,256,768]{2,1,0:T(8,128)}, f32[768,256]{1,0:T(8,128)}, bf16[2,256,768]{2,1,0:T(8,128)(2,1)}, bf16[768,256]{1,0:T(8,128)(2,1)}, bf16[3,153...) custom-call(bf16[32,2048]{1,0:T(8,128)(2,1)} %refs_0_.1, ...), custom_call_target="tpu_custom_call" | custom-call | tf_op jit(solution)/shard_map/pallas_call | solution.py:1482
  199.6 6.0 %shard_map.332 = (f32[5,3072]{1,0:T(8,128)}, bf16[32,2048]{1,0:T(8,128)(2,1)}, f32[32,2048]{1,0:T(8,128)}, f32[16,128]{1,0:T(8,128)}, f32[256,768]{1,0:T(8,128)}...) custom-call(f32[2,256,768]{2,1,0:T(8,128)} %get-tuple-element.47.ref, ...), custom_call_target="tpu_custom_call" | custom-call | tf_op jit(solution)/shard_map/pallas_call | solution.py:1504
